TPU v7x, 32 devices: a whole 2x2x4 slice. The times are simulated.
32 devices in a mesh: row: 8 (over y, x, core), col: 4 (over z).
Axes of the slice: x: 2, y: 2, z: 4, core: 2. Of those that a mesh axis runs over, the one named last changes fastest.
Arguments:
- spectra: bfloat16 [2, 4, 128, 8192], P(None, None, 'col', 'row'), may hold values from -6 to 6
Outputs:
- cross: float32 [2, 4, 8192, 8192], P(None, None, 'row', 'col')
All inputs are finite; a program needn't handle non-finite values.
Results may differ from a plain program's by a relative error of at most 0.0039.
Values may be sent and summed in bfloat16 or wider, within the bound.
No kernel may reach another device: no remote copies, remote signals or barrier semaphores. Data moves between devices by JAX's collectives and lax.ppermute only.
A program may use at most 192 MiB of HBM per device.

v0:
```python
import math

import jax
import jax.numpy as jnp
from jax import lax
from jax.sharding import PartitionSpec as P


def from_root(array, axis, root):
    mine = lax.axis_index(axis) == root
    return lax.psum(jnp.where(mine, array, jnp.zeros_like(array)), axis)


def whiten(raw):
    real_part = raw[0].astype(jnp.float32)
    imag_part = raw[1].astype(jnp.float32)
    magnitude = jnp.sqrt(real_part * real_part + imag_part * imag_part)
    blank_row = jnp.zeros_like(magnitude[:1])
    upper_side = jnp.concatenate([magnitude[1:], blank_row], axis=0)
    lower_side = jnp.concatenate([blank_row, magnitude[:-1]], axis=0)
    bin_count = magnitude.shape[0]
    positions = jnp.arange(bin_count)
    neighbours = (
        3.0
        - (positions == 0).astype(jnp.float32)
        - (positions == bin_count - 1).astype(jnp.float32)
    )
    neighbours = neighbours.reshape((bin_count, 1, 1))
    water_level = jnp.maximum((magnitude + upper_side + lower_side) / neighbours, 0.75)
    return jnp.stack([real_part / water_level, imag_part / water_level]).astype(jnp.bfloat16)


def pair_product(left_rows, segment):
    stacked_left = jnp.concatenate([left_rows[0], left_rows[1]], axis=1)
    right_real = jnp.concatenate([segment[0], segment[1]], axis=1)
    right_imag = jnp.concatenate([-segment[1], segment[0]], axis=1)
    right_side = jnp.concatenate([right_real, right_imag], axis=2)
    product = jnp.einsum(
        "fki,fkj->fij", stacked_left, right_side, preferred_element_type=jnp.float32
    )
    n_columns = segment.shape[3]
    return jnp.stack([product[:, :, :n_columns], product[:, :, n_columns:]])


def shards(spectra):
    whitened = whiten(spectra)
    window_rows = lax.all_gather(whitened, "col", axis=2, tiled=True)
    norm_factor = 1.0 / math.sqrt(window_rows.shape[2])
    groups = lax.axis_size("row") // lax.axis_size("col")
    blocks = []
    for part_index in range(groups):
        source = lax.axis_index("col") * groups + part_index
        received = from_root(window_rows, "row", source)
        blocks.append(pair_product(window_rows, received))
    summed = jnp.concatenate(blocks, axis=3)
    return summed * norm_factor


def solution(mesh):
    in_specs = (P(None, None, "col", "row"),)
    out_specs = P(None, None, "row", "col")
    return jax.shard_map(shards, mesh=mesh, in_specs=in_specs, out_specs=out_specs, check_vma=False)
```

profile of v0, /device:TPU:1, one launch (start us, length us, event | category | flops | bytes accessed | tf_op | source)
XLA Modules:
  0.0 276.5 jit_solution(12808363118539165295)
XLA Ops:
  6.5 0.0 all-gather.2.cloned.1.call-start
  6.5 1.2 fusion.17
  7.8 0.1 fusion.28
  7.9 1.4 fusion.21
  9.2 1.0 fusion.20
  10.3 0.8 pad_maximum_fusion.3
  11.1 0.0 all-gather.2.cloned.1.call-update
  11.1 0.0 all-reduce.5.cloned.1.call-start
  11.2 48.1 %all-gather.2.cloned.1.call-done = bf16[2,4,128,1024]{3,2,1,0:T(8,128)(2,1)} async-done(((bf16[2,4,32,1024]{3,2,1,0:T(8,128)(2,1)}), bf16[2,4,128,1024]{3,2,1,0:T(8,128)(2,1)}) %all-gather.2.cloned.1.call-update) | async-done | bytes 2097168 | tf_op jit(solution)/shard_map/all_gather | solution.py:47
  59.3 3.9 %broadcast_select_fusion.1 = (bf16[2,4,128,1024]{3,2,1,0:T(8,128)(2,1)}, bf16[2,4,128,1024]{3,2,1,0:T(8,128)(2,1)}) fusion(bf16[2,4,128,1024]{3,2,1,0:T(8,128)(2,1)} %all-gather.2.cloned.1.call-done, pred[]{:T(512)S(6)} %eq.22, pred[]{:T(512)S(6)} %eq.23), kind=kLoop, calls=%fused_computation.23 | loop fusion | flops 2097152 | bytes 6291458 | tf_op jit(solution)/shard_map/jit(_where)/select_n | solution.py:11
  63.2 0.0 all-reduce.5.cloned.1.call-update
  63.2 1.8 slice_bitcast_fusion.9
  65.0 78.2 %all-reduce.5.cloned.1.call-done = (bf16[2,4,128,1024]{3,2,1,0:T(8,128)(2,1)}, bf16[2,4,128,1024]{3,2,1,0:T(8,128)(2,1)}) async-done(((bf16[2,4,128,1024]{3,2,1,0:T(8,128)(2,1)}, bf16[2,4,128,1024]{3,2,1,0:T(8,128)(2,1)}), (bf16[2,4,128,1024]{3,2,1,0:T(8,128)(2,1)}, bf16[2,4,128,1024]{3,2,1,0:T(8,128)(2,1)})) %all-reduce.5.cloned.1.call-update) | async-done | bytes 4194320 | tf_op jit(solution)/shard_map/psum | solution.py:11
  143.3 2.7 fusion.26
  145.9 4.2 %slice_bitcast_fusion.4 = (bf16[4,128,1024]{2,1,0:T(8,128)(2,1)}, bf16[4,128,1024]{2,1,0:T(8,128)(2,1)}, bf16[4,128,1024]{2,1,0:T(8,128)(2,1)}, bf16[4,128,1024]{2,1,0:T(8,128)(2,1)}) fusion(bf16[2,4,128,1024]{3,2,1,0:T(8,128)(2,1)} %get-tuple-element.5, bf16[2,4,128,1024]{3,2,1,0:T(8,128)(2,1)} %get-tuple-element.6), kind=kLoop, calls=%fused_computation.24 | loop fusion | bytes 8388608 | tf_op jit(solution)/shard_map/squeeze | solution.py:35
  150.1 15.6 %fusion.8 = f32[4,1024,2048]{2,1,0:T(8,128)} fusion(bf16[4,128,1024]{2,1,0:T(8,128)(2,1)} %get-tuple-element.18, bf16[4,128,1024]{2,1,0:T(8,128)(2,1)} %get-tuple-element.26, bf16[4,128,1024]{2,1,0:T(8,128)(2,1)} %get-tuple-element.17, bf16[4,128,1024]{2,1,0:T(8,128)(2,1)S(1)} %get-tuple-element.16, bf16[4,128,1024]{2,1,0:T(8,128)(2,1)S(1)} %get-tuple-element.15), kind=kOutput, calls=%fused_computation.13 | convolution fusion | flops 4315938816 | bytes 38797312 | tf_op jit(solution)/shard_map/fki,fkj->fij/dot_general | solution.py:38
  165.8 21.8 %slice_bitcast_fusion.1 = (f32[1,4,1024,1024]{3,2,1,0:T(8,128)}, f32[1,4,1024,1024]{3,2,1,0:T(8,128)}) fusion(f32[4,1024,2048]{2,1,0:T(8,128)} %fusion.8), kind=kLoop, calls=%fused_computation.2 | loop fusion | bytes 67108864 | tf_op jit(solution)/shard_map/stack | solution.py:42
  187.6 15.5 %fusion = f32[4,1024,2048]{2,1,0:T(8,128)} fusion(bf16[4,128,1024]{2,1,0:T(8,128)(2,1)} %get-tuple-element.23, bf16[4,128,1024]{2,1,0:T(8,128)(2,1)S(1)} %get-tuple-element.25, bf16[4,128,1024]{2,1,0:T(8,128)(2,1)} %get-tuple-element.24, bf16[4,128,1024]{2,1,0:T(8,128)(2,1)S(1)} %get-tuple-element.16, bf16[4,128,1024]{2,1,0:T(8,128)(2,1)S(1)} %get-tuple-element.15), kind=kOutput, calls=%fused_computation.5 | convolution fusion | flops 4315938816 | bytes 38797312 | tf_op jit(solution)/shard_map/fki,fkj->fij/dot_general | solution.py:38
  203.1 21.8 %slice_bitcast_fusion.3 = (f32[1,4,1024,1024]{3,2,1,0:T(8,128)}, f32[1,4,1024,1024]{3,2,1,0:T(8,128)}) fusion(f32[4,1024,2048]{2,1,0:T(8,128)} %fusion), kind=kLoop, calls=%fused_computation.4 | loop fusion | bytes 67108864 | tf_op jit(solution)/shard_map/stack | solution.py:42
  224.9 44.8 %maximum_multiply_fusion = f32[2,4,1024,2048]{3,2,1,0:T(8,128)} fusion(f32[1,4,1024,1024]{3,2,1,0:T(8,128)} %get-tuple-element.12, f32[1,4,1024,1024]{3,2,1,0:T(8,128)} %get-tuple-element.11, f32[1,4,1024,1024]{3,2,1,0:T(8,128)} %get-tuple-element.10, f32[1,4,1024,1024]{3,2,1,0:T(8,128)} %get-tuple-element.9), kind=kLoop, calls=%fused_computation | loop fusion | flops 67108864 | bytes 134217728 | tf_op jit(solution)/shard_map/mul | solution.py:56
  (1 shorter events, 0.0 us)
Async XLA Ops:
  6.5 52.7 %all-gather.2.cloned.1.call-start = ((), (), s32[]{:S(2)}) async-start(), calls=%async_computation | async-start | bytes 2621440 | tf_op jit(solution)/shard_map/all_gather | solution.py:47
  11.1 132.1 %all-reduce.5.cloned.1.call-start = ((), (), s32[]{:S(2)}) async-start(), calls=%async_computation.1 | async-start | bytes 8388608 | tf_op jit(solution)/shard_map/psum | solution.py:11
Sparse Core Ops, SparseCore 0:
  11.3 47.9 all-gather.1
  63.3 79.8 all-reduce.4
where the time goes:
time: 278 us; the launch traced here: 277 us
  waiting for transfers between devices  126 us (45%)
  other arithmetic  55.9 us (20%)
  local copies, waits for them, and re-layouts  49.7 us (18%)
  matrix products  31.2 us (11%)
  between operations  13.4 us (5%)
    psum x1, waiting for transfers between devices, from_root(): return lax.psum(jnp.where(mine, array, jnp.zeros_like(array)), axis)  78.2 us
    all_gather x1, waiting for transfers between devices, shards(): window_rows = lax.all_gather(whitened, 'col', axis=2, tiled=True)  48.1 us
    mul x1, other arithmetic, shards(): return summed * norm_factor  44.8 us
    another operation x2, local copies, waits for them, and re-layouts, pair_product(): return jnp.stack([product[:, :, :n_columns], product[:, :, n_columns:]])  43.6 us
    dot_general x2, matrix products, pair_product(): jnp.einsum('fki,fkj->fij', stacked_left, right_side, preferred_element_ty...  31.2 us
  transfers between devices with their start and end apart: 2, of which 2 were waited for; matrix products, arithmetic and copies ran while one was open for 1% of the time, Pallas kernels for 0%

commit v1 on v0

v1 whole, which is shorter than its diff:
```python
import functools
import math

import jax
import jax.numpy as jnp
from jax import lax
from jax.experimental import pallas as pl
from jax.experimental.pallas import tpu as pltpu
from jax.sharding import PartitionSpec as P


def whiten_kernel(n_split, steps, raw, *refs):
    n_bins, width = raw.shape[1], raw.shape[2]
    row_outs, held = refs[:-1], refs[-1]
    q = lax.axis_index("row") // 2
    real = [raw[0, f].astype(jnp.float32) for f in range(n_bins)]
    imag = [raw[1, f].astype(jnp.float32) for f in range(n_bins)]
    magnitude = [jnp.sqrt(a * a + b * b) for a, b in zip(real, imag)]
    part = held.shape[1]
    rows = min(part, width)
    for f in range(n_bins):
        near = [magnitude[g] for g in (f, f + 1, f - 1) if 0 <= g < n_bins]
        level = jnp.maximum(sum(near[1:], near[0]) / float(len(near)), 0.75)
        for p, values in ((0, real[f]), (1, imag[f])):
            white = (values / level).astype(jnp.bfloat16)
            for at in range(0, width, rows):
                piece, start = divmod(p * width + at, part)
                held[f * n_split + piece, start : start + rows] = white[at : at + rows]
    for chunk, out in zip(steps, row_outs):
        for i, step in enumerate(chunk):
            for s in range(n_split):
                out[i, s] = held[((q // n_split) ^ step) * n_split + s]


def whiten(raw, n, n_split, steps):
    _, n_bins, width, channels = raw.shape
    part = 2 * width // n_split
    shapes = [(len(chunk), n_split, part, channels) for chunk in steps] + [(n, part, channels)]
    outs = pl.pallas_call(
        functools.partial(whiten_kernel, n_split, steps),
        out_shape=[jax.ShapeDtypeStruct(shape, jnp.bfloat16) for shape in shapes],
        in_specs=[pl.BlockSpec(memory_space=pltpu.VMEM)],
        out_specs=[pl.BlockSpec(memory_space=pltpu.VMEM)] * len(shapes),
        compiler_params=pltpu.CompilerParams(vmem_limit_bytes=24 << 20),
        name="whiten",
    )(raw)
    return outs[:-1], outs[-1]


def product_kernel(chunk, n, n_split, n_rows, tile, norm, *refs):
    shards, refs = refs[:n_rows], refs[n_rows:]
    count = len(chunk) * n_split
    near, far = refs[:count], refs[count : 2 * count]
    out, turned, made, out_sem = refs[-4:]
    q, k, z = lax.axis_index("row") // 2, lax.axis_index("row") % 2, lax.axis_index("col")
    part, channels = shards[0].shape[2:]
    slots = made.shape[0]
    per_block = channels // tile
    n_tiles = 2 * per_block
    pairs = [(s, d) for s in range(n_split) for d in range(n)]

    def left_part(i, s, d):
        s = s ^ (q % n_split)
        if n == 4 and d == 3:
            return jnp.where((z == 0) | (z == 3), shards[4][i, s], shards[3][i, s])
        return shards[d][i, s]

    def store(i, at):
        block = jnp.where(at < per_block, k, 1 - k)
        start = pl.multiple_of(block * channels + (at % per_block) * tile, tile)
        total = i * n_tiles + at
        return pltpu.make_async_copy(
            made.at[total % slots],
            out.at[:, (q // n_split) ^ chunk[i], :, pl.ds(start, tile)],
            out_sem.at[total % slots],
        )

    def one_tile(columns, i, at):
        total = i * n_tiles + at

        @pl.when(total >= slots)
        def _():
            store(i, at).wait()

        start = pl.multiple_of((at % per_block) * tile, tile)
        piece = lambda s, d: columns[s][z ^ d, :, pl.ds(start, tile)]
        right = jnp.concatenate([piece(s, d) for s, d in pairs], axis=0)
        made[total % slots, 0] = norm * jnp.dot(turned[i % 2], right, preferred_element_type=jnp.float32)
        half = part // 2 if n_split == 1 else n_split // 2
        crossed = []
        for s, d in pairs:
            if n_split == 1:
                values = piece(s, d)
                crossed += [-values[half:], values[:half]]
            else:
                sign = jnp.where((s ^ (q % n_split)) < half, -1.0, 1.0).astype(jnp.bfloat16)
                crossed.append(piece(s ^ half, d) * sign)
        right = jnp.concatenate(crossed, axis=0)
        made[total % slots, 1] = norm * jnp.dot(turned[i % 2], right, preferred_element_type=jnp.float32)
        store(i, at).start()

    for i in range(len(chunk)):
        left = jnp.concatenate([left_part(i, s, d) for s, d in pairs], axis=0)
        turned[i % 2] = left.T
        mine = slice(i * n_split, (i + 1) * n_split)
        for columns, first in ((near[mine], 0), (far[mine], per_block)):
            lax.fori_loop(first, first + per_block, lambda at, _: one_tile(columns, i, at), None)
    total = len(chunk) * n_tiles
    for at in range(max(0, total - slots), total):
        store(at // n_tiles, at % n_tiles).wait()


def product(chunk, n, n_split, shards, near, far, before, n_columns, n_bins):
    part, channels = shards[0].shape[2:]
    depth = n * n_split * part
    tile = min(256, channels)
    slots = min(4, n_columns // tile)
    operands = [*shards, *near, *far]
    specs = [pl.BlockSpec(memory_space=pltpu.VMEM)] * len(operands)
    aliases = {}
    if before is not None:
        aliases = {len(operands): 0}
        operands.append(before)
        specs.append(pl.BlockSpec(memory_space=pl.ANY))
    norm = 1.0 / math.sqrt(depth // 2)
    return pl.pallas_call(
        functools.partial(product_kernel, chunk, n, n_split, len(shards), tile, norm),
        out_shape=jax.ShapeDtypeStruct((2, n_bins, channels, n_columns), jnp.float32),
        in_specs=specs,
        out_specs=pl.BlockSpec(memory_space=pl.ANY),
        scratch_shapes=[
            pltpu.VMEM((2, channels, depth), jnp.bfloat16),
            pltpu.VMEM((slots, 2, channels, tile), jnp.float32),
            pltpu.SemaphoreType.DMA((slots,)),
        ],
        input_output_aliases=aliases,
        cost_estimate=pl.CostEstimate(
            flops=len(chunk) * 4 * channels * n_columns * depth,
            bytes_accessed=len(chunk) * 8 * channels * n_columns,
            transcendentals=0,
        ),
        compiler_params=pltpu.CompilerParams(vmem_limit_bytes=32 << 20),
        name="product",
    )(*operands)


def gather_rows(mine, n):
    def by_xor(d):
        return lax.ppermute(mine, "col", [(z, z ^ d) for z in range(n)])

    if n != 4:
        return [mine] + [by_xor(d) for d in range(1, n)]
    one, two = by_xor(1), by_xor(2)
    middle = lax.ppermute(mine, "col", [(1, 2), (2, 1)])
    ends = lax.ppermute(two, "col", [(2, 3), (1, 0)])
    return [mine, one, two, middle, ends]


def shards(spectra):
    n = lax.axis_size("col")
    n_bins, channels = spectra.shape[1], spectra.shape[3]
    assert lax.axis_size("row") == 2 * n and n % n_bins == 0
    n_split = n // n_bins
    steps = [chunk for chunk in ((0,), tuple(range(1, n_bins - 1)), (n_bins - 1,)) if chunk]
    rows, pieces = whiten(spectra, n, n_split, steps)

    same_core = [[2 * q + k for q in range(n)] for k in range(2)]
    blocks = lax.all_to_all(pieces, "row", 0, 0, axis_index_groups=same_core, tiled=True)
    held = lax.all_to_all(blocks, "col", 0, 0, tiled=True)
    out = None
    for chunk, mine in zip(steps, rows):
        near = []
        for d in range(chunk[0] * n_split, (chunk[-1] + 1) * n_split):
            moves = [(2 * q + k, 2 * (q ^ d) + k) for q in range(n) for k in range(2)]
            near.append(lax.ppermute(held, "row", moves) if d else held)
        far = [lax.ppermute(x, "row", [(r, r ^ 1) for r in range(2 * n)]) for x in near]
        out = product(chunk, n, n_split, gather_rows(mine, n), near, far, out, 2 * channels, n_bins)
    return out


def solution(mesh):
    in_specs = (P(None, None, "col", "row"),)
    out_specs = P(None, None, "row", "col")
    return jax.shard_map(shards, mesh=mesh, in_specs=in_specs, out_specs=out_specs, check_vma=False)
```

time: 278 us -> 99.3 us (0.36)
  waiting for transfers between devices: 126 us -> 20.9 us
  other arithmetic: 55.9 us -> 0 us
  local copies, waits for them, and re-layouts: 49.7 us -> 1.04 us
  starting transfers between devices: 0.04 us -> 40.2 us
  matrix products: 31.2 us -> 0 us
  Pallas kernels: 0 us -> 25 us
  between operations: 13.4 us -> 0.16 us
  blocking collectives: 0 us -> 11.4 us
    psum x1 -> x0, waiting for transfers between devices: 78.2 us -> none  [from_root(): return lax.psum(jnp.where(mine, array, jnp.zeros_like(array)), axis)]
    all_gather x1 -> x0, waiting for transfers between devices: 48.1 us -> none  [shards(): window_rows = lax.all_gather(whitened, 'col', axis=2, tiled=True)]
    mul x1 -> x0, other arithmetic: 44.8 us -> none  [shards(): return summed * norm_factor]
    another operation x2 -> x0, local copies, waits for them, and re-layouts: 43.6 us -> none  [pair_product(): return jnp.stack([product[:, :, :n_columns], product[:, :, n_columns:]])]
    ppermute x0 -> x19, starting transfers between devices: none -> 35.6 us  [the longest x4 17.9 us: shards(): lax.ppermute(x, 'row', [(r, r ^ 1) for r in range(2 * n)])]
    dot_general x2 -> x0, matrix products: 31.2 us -> none  [pair_product(): jnp.einsum('fki,fkj->fij', stacked_left, right_side, preferred_element_ty...]
    pallas_call x0 -> x4, Pallas kernels: none -> 25 us  [the longest x3 24.6 us: product(): pl.pallas_call(functools.partial(product_kernel, chunk, n, n_split, len(s...]
    all_to_all x0 -> x1, waiting for transfers between devices: none -> 13.6 us  [shards(): held = lax.all_to_all(blocks, 'col', 0, 0, tiled=True)]
  transfers between devices with their start and end apart: 2 -> 20, of which waited for: 2 -> 5; matrix products, arithmetic and copies ran while one was open for 1% -> 0% of each run, Pallas kernels for 0% -> 18%
where the time goes in v1:
time: 99.3 us; the launch traced here: 98.7 us
  starting transfers between devices  40.2 us (40%)
  Pallas kernels  25 us (25%)
  waiting for transfers between devices  20.9 us (21%)
  blocking collectives  11.4 us (11%)
  local copies, waits for them, and re-layouts  1.04 us (1%)
    pallas_call x3, Pallas kernels, product(): pl.pallas_call(functools.partial(product_kernel, chunk, n, n_split, len(s...  24.6 us
    ppermute x4, starting transfers between devices, shards(): lax.ppermute(x, 'row', [(r, r ^ 1) for r in range(2 * n)])  17.9 us
    all_to_all x1, waiting for transfers between devices, shards(): held = lax.all_to_all(blocks, 'col', 0, 0, tiled=True)  13.6 us
    all_to_all x1, blocking collectives, shards(): lax.all_to_all(pieces, 'row', 0, 0, axis_index_groups=same_core, tiled=True)  11.4 us
    ppermute x6, starting transfers between devices, by_xor(): return lax.ppermute(mine, 'col', [(z, z ^ d) for z in range(n)])  8.96 us
    all_to_all x1, starting transfers between devices, shards(): held = lax.all_to_all(blocks, 'col', 0, 0, tiled=True)  4.59 us
    ppermute x6, waiting for transfers between devices, by_xor(): return lax.ppermute(mine, 'col', [(z, z ^ d) for z in range(n)])  4.27 us
    ppermute x3, starting transfers between devices, gather_rows(): ends = lax.ppermute(two, 'col', [(2, 3), (1, 0)])  3.87 us
  transfers between devices with their start and end apart: 20, of which 5 were waited for; matrix products, arithmetic and copies ran while one was open for 0% of the time, Pallas kernels for 18%

profile of v1, /device:TPU:1, one launch (start us, length us, event | category | flops | bytes accessed | tf_op | source)
XLA Modules:
  0.0 98.7 jit_solution(4949840450473085904)
XLA Ops:
  0.0 0.0 copy-start
  0.0 1.0 %copy-done = bf16[2,4,32,1024]{3,2,1,0:T(8,128)(2,1)S(1)} copy-done((bf16[2,4,32,1024]{3,2,1,0:T(8,128)(2,1)S(1)}, bf16[2,4,32,1024]{3,2,1,0:T(8,128)(2,1)}, u32[]{:S(2)}) %copy-start) | copy-done | bytes 524312
  1.0 0.4 whiten.1
  1.4 11.4 %all_to_all.10 = bf16[4,64,1024]{2,1,0:T(8,128)(2,1)} all-to-all(bf16[4,64,1024]{2,1,0:T(8,128)(2,1)S(1)} %get-tuple-element.10), channel_id=1, replica_groups={{0,8,16,24},{4,12,20,28},{1,9,17,25},{5,13,21,29},{2,10,18,26},{6,14,22..., dimensions={0} | all-to-all | bytes 1048576 | tf_op jit(solution)/shard_map/all_to_all | solution.py:168
  12.9 4.6 %all-to-all-start.1 = ((bf16[4,64,1024]{2,1,0:T(8,128)(2,1)}), bf16[4,64,1024]{2,1,0:T(8,128)(2,1)S(1)}, u32[]{:S(2)}, u32[]{:S(2)}) async-start(bf16[4,64,1024]{2,1,0:T(8,128)(2,1)} %all_to_all.10), calls=%async_computation.1 | async-start | bytes 1048576 | tf_op jit(solution)/shard_map/all_to_all | solution.py:169
  17.5 2.4 %collective-permute-start.15 = (bf16[1,1,64,1024]{3,2,1,0:T(8,128)(2,1)S(1)}, bf16[1,1,64,1024]{3,2,1,0:T(8,128)(2,1)S(1)}, u32[]{:S(2)}, u32[]{:S(2)}) collective-permute-start(bf16[1,1,64,1024]{3,2,1,0:T(8,128)(2,1)S(1)} %get-tuple-element.12.refs_0_), channel_id=1, source_target_pairs={{0,2},{1,3},{2,0},{3,1},{4,6},{5,7},{6,4},{7,5},{8,10},{9,11},{10,... | collective-permute-start | bytes 393224 | tf_op jit(solution)/shard_map/ppermute | solution.py:149
  19.8 13.6 %all-to-all-done.1.refs_5_ = bf16[4,64,1024]{2,1,0:T(8,128)(2,1)S(1)} async-done(((bf16[4,64,1024]{2,1,0:T(8,128)(2,1)}), bf16[4,64,1024]{2,1,0:T(8,128)(2,1)S(1)}, u32[]{:S(2)}, u32[]{:S(2)}) %all-to-all-start.1) | async-done | bytes 524320 | tf_op jit(solution)/shard_map/all_to_all | solution.py:169
  33.4 1.6 %collective-permute-start.10 = (bf16[4,64,1024]{2,1,0:T(8,128)(2,1)S(1)}, bf16[4,64,1024]{2,1,0:T(8,128)(2,1)S(1)}, u32[]{:S(2)}, u32[]{:S(2)}) collective-permute-start(bf16[4,64,1024]{2,1,0:T(8,128)(2,1)S(1)} %all-to-all-done.1.refs_5_), channel_id=1, source_target_pairs={{0,8},{4,12},{8,0},{12,4},{16,24},{20,28},{24,16},{28,20},{1,9},{5... | collective-permute-start | bytes 1572872 | tf_op jit(solution)/shard_map/ppermute | solution.py:175
  35.0 0.2 collective-permute-start.11
  35.2 0.0 collective-permute-start.14
  35.3 0.7 collective-permute-start.16
  35.9 0.6 collective-permute-done.15.refs_2_
  36.5 3.4 %collective-permute-start.1 = (bf16[1,1,64,1024]{3,2,1,0:T(8,128)(2,1)S(1)}, bf16[1,1,64,1024]{3,2,1,0:T(8,128)(2,1)S(1)}, u32[]{:S(2)}, u32[]{:S(2)}) collective-permute-start(bf16[1,1,64,1024]{3,2,1,0:T(8,128)(2,1)S(1)} %get-tuple-element.9.refs_0_), channel_id=1, source_target_pairs={{0,2},{1,3},{2,0},{3,1},{4,6},{5,7},{6,4},{7,5},{8,10},{9,11},{10,... | collective-permute-start | bytes 393224 | tf_op jit(solution)/shard_map/ppermute | solution.py:149
  39.9 0.0 collective-permute-done.14.refs_1_
  39.9 1.3 %collective-permute-start.17 = (bf16[1,1,64,1024]{3,2,1,0:T(8,128)(2,1)S(1)}, bf16[1,1,64,1024]{3,2,1,0:T(8,128)(2,1)S(1)}, u32[]{:S(2)}, u32[]{:S(2)}) collective-permute-start(bf16[1,1,64,1024]{3,2,1,0:T(8,128)(2,1)S(1)} %collective-permute-done.15.refs_2_), channel_id=1, source_target_pairs={{2,3},{1,0},{6,7},{5,4},{10,11},{9,8},{14,15},{13,12},{18,19},{17,... | collective-permute-start | bytes 393224 | tf_op jit(solution)/shard_map/ppermute | solution.py:155
  41.2 0.0 collective-permute-done.16.refs_3_
  41.2 1.9 %collective-permute-start.7 = (bf16[2,1,64,1024]{3,2,1,0:T(8,128)(2,1)S(1)}, bf16[2,1,64,1024]{3,2,1,0:T(8,128)(2,1)S(1)}, u32[]{:S(2)}, u32[]{:S(2)}) collective-permute-start(bf16[2,1,64,1024]{3,2,1,0:T(8,128)(2,1)S(1)} %get-tuple-element.11.refs_0_), channel_id=1, source_target_pairs={{0,2},{1,3},{2,0},{3,1},{4,6},{5,7},{6,4},{7,5},{8,10},{9,11},{10,... | collective-permute-start | bytes 786440 | tf_op jit(solution)/shard_map/ppermute | solution.py:149
  43.1 2.0 %collective-permute-done.1.refs_2_ = bf16[1,1,64,1024]{3,2,1,0:T(8,128)(2,1)S(1)} collective-permute-done((bf16[1,1,64,1024]{3,2,1,0:T(8,128)(2,1)S(1)}, bf16[1,1,64,1024]{3,2,1,0:T(8,128)(2,1)S(1)}, u32[]{:S(2)}, u32[]{:S(2)}) %collective-permute-start.1) | collective-permute-done | bytes 131104 | tf_op jit(solution)/shard_map/ppermute | solution.py:149
  45.0 10.4 %collective-permute-start.18 = (bf16[4,64,1024]{2,1,0:T(8,128)(2,1)S(1)}, bf16[4,64,1024]{2,1,0:T(8,128)(2,1)S(1)}, u32[]{:S(2)}, u32[]{:S(2)}) collective-permute-start(bf16[4,64,1024]{2,1,0:T(8,128)(2,1)S(1)} %all-to-all-done.1.refs_5_), channel_id=1, source_target_pairs={{0,4},{4,0},{8,12},{12,8},{16,20},{20,16},{24,28},{28,24},{1,5},{5... | collective-permute-start | bytes 1572872 | tf_op jit(solution)/shard_map/ppermute | solution.py:176
  55.5 0.0 collective-permute-done.17.refs_4_
  55.5 1.1 %collective-permute-start.4 = (bf16[4,64,1024]{2,1,0:T(8,128)(2,1)S(1)}, bf16[4,64,1024]{2,1,0:T(8,128)(2,1)S(1)}, u32[]{:S(2)}, u32[]{:S(2)}) collective-permute-start(bf16[4,64,1024]{2,1,0:T(8,128)(2,1)S(1)} %all-to-all-done.1.refs_5_), channel_id=1, source_target_pairs={{0,24},{4,28},{8,16},{12,20},{16,8},{20,12},{24,0},{28,4},{1,25},{... | collective-permute-start | bytes 1572872 | tf_op jit(solution)/shard_map/ppermute | solution.py:175
  56.6 0.0 collective-permute-done.7.refs_2_
  56.6 0.0 collective-permute-start.6
  56.6 0.0 collective-permute-done.10.refs_5_
  56.6 4.6 %collective-permute-start.12 = (bf16[4,64,1024]{2,1,0:T(8,128)(2,1)S(1)}, bf16[4,64,1024]{2,1,0:T(8,128)(2,1)S(1)}, u32[]{:S(2)}, u32[]{:S(2)}) collective-permute-start(bf16[4,64,1024]{2,1,0:T(8,128)(2,1)S(1)} %collective-permute-done.10.refs_5_), channel_id=1, source_target_pairs={{0,4},{4,0},{8,12},{12,8},{16,20},{20,16},{24,28},{28,24},{1,5},{5... | collective-permute-start | bytes 1572872 | tf_op jit(solution)/shard_map/ppermute | solution.py:176
  61.2 0.0 collective-permute-done.11.refs_6_
  61.2 0.1 collective-permute-start.13
  61.3 1.7 %collective-permute-done.6.refs_1_ = bf16[2,1,64,1024]{3,2,1,0:T(8,128)(2,1)S(1)} collective-permute-done((bf16[2,1,64,1024]{3,2,1,0:T(8,128)(2,1)S(1)}, bf16[2,1,64,1024]{3,2,1,0:T(8,128)(2,1)S(1)}, u32[]{:S(2)}, u32[]{:S(2)}) %collective-permute-start.6) | collective-permute-done | bytes 262176 | tf_op jit(solution)/shard_map/ppermute | solution.py:149
  63.0 0.7 collective-permute-start.8
  63.6 0.0 collective-permute-done.18.refs_6_
  63.7 1.3 %collective-permute-start.9 = (bf16[2,1,64,1024]{3,2,1,0:T(8,128)(2,1)S(1)}, bf16[2,1,64,1024]{3,2,1,0:T(8,128)(2,1)S(1)}, u32[]{:S(2)}, u32[]{:S(2)}) collective-permute-start(bf16[2,1,64,1024]{3,2,1,0:T(8,128)(2,1)S(1)} %collective-permute-done.7.refs_2_), channel_id=1, source_target_pairs={{2,3},{1,0},{6,7},{5,4},{10,11},{9,8},{14,15},{13,12},{18,19},{17,... | collective-permute-start | bytes 786440 | tf_op jit(solution)/shard_map/ppermute | solution.py:155
  65.0 3.0 %collective-permute-done.4.refs_5_ = bf16[4,64,1024]{2,1,0:T(8,128)(2,1)S(1)} collective-permute-done((bf16[4,64,1024]{2,1,0:T(8,128)(2,1)S(1)}, bf16[4,64,1024]{2,1,0:T(8,128)(2,1)S(1)}, u32[]{:S(2)}, u32[]{:S(2)}) %collective-permute-start.4) | collective-permute-done | bytes 524320 | tf_op jit(solution)/shard_map/ppermute | solution.py:175
  68.0 2.7 %collective-permute-start.5 = (bf16[4,64,1024]{2,1,0:T(8,128)(2,1)S(1)}, bf16[4,64,1024]{2,1,0:T(8,128)(2,1)S(1)}, u32[]{:S(2)}, u32[]{:S(2)}) collective-permute-start(bf16[4,64,1024]{2,1,0:T(8,128)(2,1)S(1)} %collective-permute-done.4.refs_5_), channel_id=1, source_target_pairs={{0,4},{4,0},{8,12},{12,8},{16,20},{20,16},{24,28},{28,24},{1,5},{5... | collective-permute-start | bytes 1572872 | tf_op jit(solution)/shard_map/ppermute | solution.py:176
  70.7 6.5 %product.3.refs_9_ = f32[2,4,1024,2048]{3,2,1,0:T(8,128)} custom-call(bf16[1,1,64,1024]{3,2,1,0:T(8,128)(2,1)S(1)} %get-tuple-element.12.refs_0_, bf16[1,1,64,1024]{3,2,1,0:T(8,128)(2,1)S(1)} %collective-permute-done.14.refs_1_, bf16[1,1,64,1024]{3,2,1,0:T(8,128)(2,1)S(1)} %collective-permute-done.15.refs_2_, ...), custom_call_target="tpu_custom_call" | custom-call | flops 2147483648 | bytes 16777216 | tf_op jit(solution)/shard_map/product/pallas_call | solution.py:126
  77.2 0.0 collective-permute-done.8.refs_3_
  77.2 1.4 %collective-permute-start = (bf16[1,1,64,1024]{3,2,1,0:T(8,128)(2,1)S(1)}, bf16[1,1,64,1024]{3,2,1,0:T(8,128)(2,1)S(1)}, u32[]{:S(2)}, u32[]{:S(2)}) collective-permute-start(bf16[1,1,64,1024]{3,2,1,0:T(8,128)(2,1)S(1)} %get-tuple-element.9.refs_0_), channel_id=1, source_target_pairs={{0,1},{1,0},{2,3},{3,2},{4,5},{5,4},{6,7},{7,6},{8,9},{9,8},{10,11... | collective-permute-start | bytes 393224 | tf_op jit(solution)/shard_map/ppermute | solution.py:149
  78.6 0.0 collective-permute-done.9.refs_4_
  78.6 0.7 collective-permute-start.2
  79.3 0.0 collective-permute-done.12.refs_7_
  79.3 1.3 %collective-permute-start.3 = (bf16[1,1,64,1024]{3,2,1,0:T(8,128)(2,1)S(1)}, bf16[1,1,64,1024]{3,2,1,0:T(8,128)(2,1)S(1)}, u32[]{:S(2)}, u32[]{:S(2)}) collective-permute-start(bf16[1,1,64,1024]{3,2,1,0:T(8,128)(2,1)S(1)} %collective-permute-done.1.refs_2_), channel_id=1, source_target_pairs={{2,3},{1,0},{6,7},{5,4},{10,11},{9,8},{14,15},{13,12},{18,19},{17,... | collective-permute-start | bytes 393224 | tf_op jit(solution)/shard_map/ppermute | solution.py:155
  80.6 0.0 collective-permute-done.13.refs_8_
  80.6 11.6 %product.4.refs_7_ = f32[2,4,1024,2048]{3,2,1,0:T(8,128)} custom-call(bf16[2,1,64,1024]{3,2,1,0:T(8,128)(2,1)S(1)} %get-tuple-element.11.refs_0_, bf16[2,1,64,1024]{3,2,1,0:T(8,128)(2,1)S(1)} %collective-permute-done.6.refs_1_, bf16[2,1,64,1024]{3,2,1,0:T(8,128)(2,1)S(1)} %collective-permute-done.7.refs_2_, ...), custom_call_target="tpu_custom_call", output_to_operand_aliasing={{}: (9, {})} | custom-call | flops 4294967296 | bytes 33554432 | tf_op jit(solution)/shard_map/product/pallas_call | solution.py:126
  92.2 0.0 collective-permute-done.refs_1_
  92.2 0.0 collective-permute-done.2.refs_3_
  92.2 0.0 collective-permute-done.3.refs_4_
  92.2 0.0 collective-permute-done.5.refs_6_
  92.2 6.5 %product.5 = f32[2,4,1024,2048]{3,2,1,0:T(8,128)} custom-call(bf16[1,1,64,1024]{3,2,1,0:T(8,128)(2,1)S(1)} %get-tuple-element.9.refs_0_, bf16[1,1,64,1024]{3,2,1,0:T(8,128)(2,1)S(1)} %collective-permute-done.refs_1_, bf16[1,1,64,1024]{3,2,1,0:T(8,128)(2,1)S(1)} %collective-permute-done.1.refs_2_, ...), custom_call_target="tpu_custom_call", output_to_operand_aliasing={{}: (7, {})} | custom-call | flops 2147483648 | bytes 16777216 | tf_op jit(solution)/shard_map/product/pallas_call | solution.py:126
Async XLA Ops:
  0.0 1.0 %copy-start = (bf16[2,4,32,1024]{3,2,1,0:T(8,128)(2,1)S(1)}, bf16[2,4,32,1024]{3,2,1,0:T(8,128)(2,1)}, u32[]{:S(2)}) copy-start(bf16[2,4,32,1024]{3,2,1,0:T(8,128)(2,1)} %raw.1) | copy-start | bytes 1572868
  12.9 20.5 %all-to-all-start.1 = ((bf16[4,64,1024]{2,1,0:T(8,128)(2,1)}), bf16[4,64,1024]{2,1,0:T(8,128)(2,1)S(1)}, u32[]{:S(2)}, u32[]{:S(2)}) async-start(bf16[4,64,1024]{2,1,0:T(8,128)(2,1)} %all_to_all.10), calls=%async_computation.1 | async-start | bytes 1048576 | tf_op jit(solution)/shard_map/all_to_all | solution.py:169
  17.5 19.0 %collective-permute-start.15 = (bf16[1,1,64,1024]{3,2,1,0:T(8,128)(2,1)S(1)}, bf16[1,1,64,1024]{3,2,1,0:T(8,128)(2,1)S(1)}, u32[]{:S(2)}, u32[]{:S(2)}) collective-permute-start(bf16[1,1,64,1024]{3,2,1,0:T(8,128)(2,1)S(1)} %get-tuple-element.12.refs_0_), channel_id=1, source_target_pairs={{0,2},{1,3},{2,0},{3,1},{4,6},{5,7},{6,4},{7,5},{8,10},{9,11},{10,... | collective-permute-start | bytes 393224 | tf_op jit(solution)/shard_map/ppermute | solution.py:149
  33.4 23.1 %collective-permute-start.10 = (bf16[4,64,1024]{2,1,0:T(8,128)(2,1)S(1)}, bf16[4,64,1024]{2,1,0:T(8,128)(2,1)S(1)}, u32[]{:S(2)}, u32[]{:S(2)}) collective-permute-start(bf16[4,64,1024]{2,1,0:T(8,128)(2,1)S(1)} %all-to-all-done.1.refs_5_), channel_id=1, source_target_pairs={{0,8},{4,12},{8,0},{12,4},{16,24},{20,28},{24,16},{28,20},{1,9},{5... | collective-permute-start | bytes 1572872 | tf_op jit(solution)/shard_map/ppermute | solution.py:175
  35.0 26.2 %collective-permute-start.11 = (bf16[4,64,1024]{2,1,0:T(8,128)(2,1)S(1)}, bf16[4,64,1024]{2,1,0:T(8,128)(2,1)S(1)}, u32[]{:S(2)}, u32[]{:S(2)}) collective-permute-start(bf16[4,64,1024]{2,1,0:T(8,128)(2,1)S(1)} %all-to-all-done.1.refs_5_), channel_id=1, source_target_pairs={{0,16},{4,20},{8,24},{12,28},{16,0},{20,4},{24,8},{28,12},{1,17},{... | collective-permute-start | bytes 1572872 | tf_op jit(solution)/shard_map/ppermute | solution.py:175
  35.2 4.6 %collective-permute-start.14 = (bf16[1,1,64,1024]{3,2,1,0:T(8,128)(2,1)S(1)}, bf16[1,1,64,1024]{3,2,1,0:T(8,128)(2,1)S(1)}, u32[]{:S(2)}, u32[]{:S(2)}) collective-permute-start(bf16[1,1,64,1024]{3,2,1,0:T(8,128)(2,1)S(1)} %get-tuple-element.12.refs_0_), channel_id=1, source_target_pairs={{0,1},{1,0},{2,3},{3,2},{4,5},{5,4},{6,7},{7,6},{8,9},{9,8},{10,11... | collective-permute-start | bytes 393224 | tf_op jit(solution)/shard_map/ppermute | solution.py:149
  35.3 5.9 %collective-permute-start.16 = (bf16[1,1,64,1024]{3,2,1,0:T(8,128)(2,1)S(1)}, bf16[1,1,64,1024]{3,2,1,0:T(8,128)(2,1)S(1)}, u32[]{:S(2)}, u32[]{:S(2)}) collective-permute-start(bf16[1,1,64,1024]{3,2,1,0:T(8,128)(2,1)S(1)} %get-tuple-element.12.refs_0_), channel_id=1, source_target_pairs={{1,2},{2,1},{5,6},{6,5},{9,10},{10,9},{13,14},{14,13},{17,18},{18,... | collective-permute-start | bytes 393224 | tf_op jit(solution)/shard_map/ppermute | solution.py:154
  36.5 8.5 %collective-permute-start.1 = (bf16[1,1,64,1024]{3,2,1,0:T(8,128)(2,1)S(1)}, bf16[1,1,64,1024]{3,2,1,0:T(8,128)(2,1)S(1)}, u32[]{:S(2)}, u32[]{:S(2)}) collective-permute-start(bf16[1,1,64,1024]{3,2,1,0:T(8,128)(2,1)S(1)} %get-tuple-element.9.refs_0_), channel_id=1, source_target_pairs={{0,2},{1,3},{2,0},{3,1},{4,6},{5,7},{6,4},{7,5},{8,10},{9,11},{10,... | collective-permute-start | bytes 393224 | tf_op jit(solution)/shard_map/ppermute | solution.py:149
  39.9 15.6 %collective-permute-start.17 = (bf16[1,1,64,1024]{3,2,1,0:T(8,128)(2,1)S(1)}, bf16[1,1,64,1024]{3,2,1,0:T(8,128)(2,1)S(1)}, u32[]{:S(2)}, u32[]{:S(2)}) collective-permute-start(bf16[1,1,64,1024]{3,2,1,0:T(8,128)(2,1)S(1)} %collective-permute-done.15.refs_2_), channel_id=1, source_target_pairs={{2,3},{1,0},{6,7},{5,4},{10,11},{9,8},{14,15},{13,12},{18,19},{17,... | collective-permute-start | bytes 393224 | tf_op jit(solution)/shard_map/ppermute | solution.py:155
  41.2 15.4 %collective-permute-start.7 = (bf16[2,1,64,1024]{3,2,1,0:T(8,128)(2,1)S(1)}, bf16[2,1,64,1024]{3,2,1,0:T(8,128)(2,1)S(1)}, u32[]{:S(2)}, u32[]{:S(2)}) collective-permute-start(bf16[2,1,64,1024]{3,2,1,0:T(8,128)(2,1)S(1)} %get-tuple-element.11.refs_0_), channel_id=1, source_target_pairs={{0,2},{1,3},{2,0},{3,1},{4,6},{5,7},{6,4},{7,5},{8,10},{9,11},{10,... | collective-permute-start | bytes 786440 | tf_op jit(solution)/shard_map/ppermute | solution.py:149
  45.0 18.6 %collective-permute-start.18 = (bf16[4,64,1024]{2,1,0:T(8,128)(2,1)S(1)}, bf16[4,64,1024]{2,1,0:T(8,128)(2,1)S(1)}, u32[]{:S(2)}, u32[]{:S(2)}) collective-permute-start(bf16[4,64,1024]{2,1,0:T(8,128)(2,1)S(1)} %all-to-all-done.1.refs_5_), channel_id=1, source_target_pairs={{0,4},{4,0},{8,12},{12,8},{16,20},{20,16},{24,28},{28,24},{1,5},{5... | collective-permute-start | bytes 1572872 | tf_op jit(solution)/shard_map/ppermute | solution.py:176
  55.5 12.5 %collective-permute-start.4 = (bf16[4,64,1024]{2,1,0:T(8,128)(2,1)S(1)}, bf16[4,64,1024]{2,1,0:T(8,128)(2,1)S(1)}, u32[]{:S(2)}, u32[]{:S(2)}) collective-permute-start(bf16[4,64,1024]{2,1,0:T(8,128)(2,1)S(1)} %all-to-all-done.1.refs_5_), channel_id=1, source_target_pairs={{0,24},{4,28},{8,16},{12,20},{16,8},{20,12},{24,0},{28,4},{1,25},{... | collective-permute-start | bytes 1572872 | tf_op jit(solution)/shard_map/ppermute | solution.py:175
  56.6 6.4 %collective-permute-start.6 = (bf16[2,1,64,1024]{3,2,1,0:T(8,128)(2,1)S(1)}, bf16[2,1,64,1024]{3,2,1,0:T(8,128)(2,1)S(1)}, u32[]{:S(2)}, u32[]{:S(2)}) collective-permute-start(bf16[2,1,64,1024]{3,2,1,0:T(8,128)(2,1)S(1)} %get-tuple-element.11.refs_0_), channel_id=1, source_target_pairs={{0,1},{1,0},{2,3},{3,2},{4,5},{5,4},{6,7},{7,6},{8,9},{9,8},{10,11... | collective-permute-start | bytes 786440 | tf_op jit(solution)/shard_map/ppermute | solution.py:149
  56.6 22.7 %collective-permute-start.12 = (bf16[4,64,1024]{2,1,0:T(8,128)(2,1)S(1)}, bf16[4,64,1024]{2,1,0:T(8,128)(2,1)S(1)}, u32[]{:S(2)}, u32[]{:S(2)}) collective-permute-start(bf16[4,64,1024]{2,1,0:T(8,128)(2,1)S(1)} %collective-permute-done.10.refs_5_), channel_id=1, source_target_pairs={{0,4},{4,0},{8,12},{12,8},{16,20},{20,16},{24,28},{28,24},{1,5},{5... | collective-permute-start | bytes 1572872 | tf_op jit(solution)/shard_map/ppermute | solution.py:176
  61.2 19.4 %collective-permute-start.13 = (bf16[4,64,1024]{2,1,0:T(8,128)(2,1)S(1)}, bf16[4,64,1024]{2,1,0:T(8,128)(2,1)S(1)}, u32[]{:S(2)}, u32[]{:S(2)}) collective-permute-start(bf16[4,64,1024]{2,1,0:T(8,128)(2,1)S(1)} %collective-permute-done.11.refs_6_), channel_id=1, source_target_pairs={{0,4},{4,0},{8,12},{12,8},{16,20},{20,16},{24,28},{28,24},{1,5},{5... | collective-permute-start | bytes 1572872 | tf_op jit(solution)/shard_map/ppermute | solution.py:176
  63.0 14.3 %collective-permute-start.8 = (bf16[2,1,64,1024]{3,2,1,0:T(8,128)(2,1)S(1)}, bf16[2,1,64,1024]{3,2,1,0:T(8,128)(2,1)S(1)}, u32[]{:S(2)}, u32[]{:S(2)}) collective-permute-start(bf16[2,1,64,1024]{3,2,1,0:T(8,128)(2,1)S(1)} %get-tuple-element.11.refs_0_), channel_id=1, source_target_pairs={{1,2},{2,1},{5,6},{6,5},{9,10},{10,9},{13,14},{14,13},{17,18},{18,... | collective-permute-start | bytes 786440 | tf_op jit(solution)/shard_map/ppermute | solution.py:154
  63.7 14.9 %collective-permute-start.9 = (bf16[2,1,64,1024]{3,2,1,0:T(8,128)(2,1)S(1)}, bf16[2,1,64,1024]{3,2,1,0:T(8,128)(2,1)S(1)}, u32[]{:S(2)}, u32[]{:S(2)}) collective-permute-start(bf16[2,1,64,1024]{3,2,1,0:T(8,128)(2,1)S(1)} %collective-permute-done.7.refs_2_), channel_id=1, source_target_pairs={{2,3},{1,0},{6,7},{5,4},{10,11},{9,8},{14,15},{13,12},{18,19},{17,... | collective-permute-start | bytes 786440 | tf_op jit(solution)/shard_map/ppermute | solution.py:155
  68.0 24.2 %collective-permute-start.5 = (bf16[4,64,1024]{2,1,0:T(8,128)(2,1)S(1)}, bf16[4,64,1024]{2,1,0:T(8,128)(2,1)S(1)}, u32[]{:S(2)}, u32[]{:S(2)}) collective-permute-start(bf16[4,64,1024]{2,1,0:T(8,128)(2,1)S(1)} %collective-permute-done.4.refs_5_), channel_id=1, source_target_pairs={{0,4},{4,0},{8,12},{12,8},{16,20},{20,16},{24,28},{28,24},{1,5},{5... | collective-permute-start | bytes 1572872 | tf_op jit(solution)/shard_map/ppermute | solution.py:176
  77.2 14.9 %collective-permute-start = (bf16[1,1,64,1024]{3,2,1,0:T(8,128)(2,1)S(1)}, bf16[1,1,64,1024]{3,2,1,0:T(8,128)(2,1)S(1)}, u32[]{:S(2)}, u32[]{:S(2)}) collective-permute-start(bf16[1,1,64,1024]{3,2,1,0:T(8,128)(2,1)S(1)} %get-tuple-element.9.refs_0_), channel_id=1, source_target_pairs={{0,1},{1,0},{2,3},{3,2},{4,5},{5,4},{6,7},{7,6},{8,9},{9,8},{10,11... | collective-permute-start | bytes 393224 | tf_op jit(solution)/shard_map/ppermute | solution.py:149
  78.6 13.6 %collective-permute-start.2 = (bf16[1,1,64,1024]{3,2,1,0:T(8,128)(2,1)S(1)}, bf16[1,1,64,1024]{3,2,1,0:T(8,128)(2,1)S(1)}, u32[]{:S(2)}, u32[]{:S(2)}) collective-permute-start(bf16[1,1,64,1024]{3,2,1,0:T(8,128)(2,1)S(1)} %get-tuple-element.9.refs_0_), channel_id=1, source_target_pairs={{1,2},{2,1},{5,6},{6,5},{9,10},{10,9},{13,14},{14,13},{17,18},{18,... | collective-permute-start | bytes 393224 | tf_op jit(solution)/shard_map/ppermute | solution.py:154
  79.3 12.9 %collective-permute-start.3 = (bf16[1,1,64,1024]{3,2,1,0:T(8,128)(2,1)S(1)}, bf16[1,1,64,1024]{3,2,1,0:T(8,128)(2,1)S(1)}, u32[]{:S(2)}, u32[]{:S(2)}) collective-permute-start(bf16[1,1,64,1024]{3,2,1,0:T(8,128)(2,1)S(1)} %collective-permute-done.1.refs_2_), channel_id=1, source_target_pairs={{2,3},{1,0},{6,7},{5,4},{10,11},{9,8},{14,15},{13,12},{18,19},{17,... | collective-permute-start | bytes 393224 | tf_op jit(solution)/shard_map/ppermute | solution.py:155

commit v2 on v1

v2 whole, which is shorter than its diff:
```python
import functools
import math

import jax
import jax.numpy as jnp
from jax import lax
from jax.experimental import pallas as pl
from jax.experimental.pallas import tpu as pltpu
from jax.sharding import PartitionSpec as P

WEIGHT = 4


def whiten_kernel(n, n_split, steps, raw, *refs):
    n_bins, width = raw.shape[1], raw.shape[2]
    row_outs, piece_outs, held = refs[: len(steps)], refs[len(steps) : -1], refs[-1]
    q = lax.axis_index("row") // 2
    real = [raw[0, f].astype(jnp.float32) for f in range(n_bins)]
    imag = [raw[1, f].astype(jnp.float32) for f in range(n_bins)]
    magnitude = [jnp.sqrt(a * a + b * b) for a, b in zip(real, imag)]
    part = held.shape[1]
    rows = min(part, width)
    for f in range(n_bins):
        near = [magnitude[g] for g in (f, f + 1, f - 1) if 0 <= g < n_bins]
        level = jnp.maximum(sum(near[1:], near[0]) / float(len(near)), 0.75)
        for p, values in ((0, real[f]), (1, imag[f])):
            white = (values / level).astype(jnp.bfloat16)
            for at in range(0, width, rows):
                piece, start = divmod(p * width + at, part)
                held[f * n_split + piece, start : start + rows] = white[at : at + rows]
    for chunk, out in zip(steps, row_outs):
        for i, step in enumerate(chunk):
            for s in range(n_split):
                out[0, i, s] = held[((q // n_split) ^ step) * n_split + s]
    for d, out in enumerate(piece_outs):
        out[...] = held[q ^ d]


def whiten(raw, n, n_split, steps):
    _, n_bins, width, channels = raw.shape
    part = 2 * width // n_split
    shapes = [(1, len(chunk), n_split, part, channels) for chunk in steps] + [(part, channels)] * n
    outs = pl.pallas_call(
        functools.partial(whiten_kernel, n, n_split, steps),
        out_shape=[jax.ShapeDtypeStruct(shape, jnp.bfloat16) for shape in shapes],
        in_specs=[pl.BlockSpec(memory_space=pltpu.VMEM)],
        out_specs=[pl.BlockSpec(memory_space=pltpu.VMEM)] * len(shapes),
        scratch_shapes=[pltpu.VMEM((n, part, channels), jnp.bfloat16)],
        compiler_params=pltpu.CompilerParams(vmem_limit_bytes=24 << 20),
        name="whiten",
    )(raw)
    return outs[: len(steps)], outs[len(steps) :]


def route_kernel(*refs):
    n = len(refs) // 2
    blocks, outs = refs[:n], refs[n:]
    q, z = lax.axis_index("row") // 2, lax.axis_index("col")
    for e, out in enumerate(outs):
        wanted = q ^ z ^ e
        for d, block in enumerate(blocks):

            @pl.when(wanted == d)
            def _(block=block, out=out):
                out[...] = block[...]


def route(blocks):
    n = len(blocks)
    shape = jax.ShapeDtypeStruct(blocks[0].shape, jnp.bfloat16)
    return pl.pallas_call(
        route_kernel,
        out_shape=[shape] * n,
        in_specs=[pl.BlockSpec(memory_space=pltpu.VMEM)] * n,
        out_specs=[pl.BlockSpec(memory_space=pltpu.VMEM)] * n,
        compiler_params=pltpu.CompilerParams(vmem_limit_bytes=24 << 20),
        name="route",
    )(*blocks)


def collect_kernel(*refs):
    z = lax.axis_index("col")
    for e, x in enumerate(refs[:-1]):
        refs[-1][z ^ e] = x[...]


def collect(parts):
    return pl.pallas_call(
        collect_kernel,
        out_shape=jax.ShapeDtypeStruct((len(parts), *parts[0].shape), jnp.bfloat16),
        in_specs=[pl.BlockSpec(memory_space=pltpu.VMEM)] * len(parts),
        out_specs=pl.BlockSpec(memory_space=pltpu.VMEM),
        compiler_params=pltpu.CompilerParams(vmem_limit_bytes=24 << 20),
        name="collect",
    )(*parts)


def product_kernel(items, n, n_split, tile, norm, *refs):
    n_parts = n.bit_length()
    per_item = n_parts + n_split
    operands = [refs[at * per_item : (at + 1) * per_item] for at in range(len(items))]
    out, turned, made, out_sem = refs[-4:]
    q, k, z = lax.axis_index("row") // 2, lax.axis_index("row") % 2, lax.axis_index("col")
    part, channels = operands[0][0].shape[2:]
    slots = made.shape[0]
    n_tiles = channels // tile
    pairs = [(s, d) for s in range(n_split) for d in range(n)]

    def left_part(shards, s, d):
        at, place, order = 0, 0, [0]
        while d not in order:
            at, bit = at + 1, n >> (at + 1)
            taken = [bit ^ other for other in order]
            place, order = (taken.index(d) if d in taken else 0), order + taken
        return shards[at][place, s ^ (q % n_split)]

    def store(item, at):
        step, other = items[item]
        block = 1 - k if other else k
        start = pl.multiple_of(block * channels + at * tile, tile)
        total = item * n_tiles + at
        return pltpu.make_async_copy(
            made.at[total % slots],
            out.at[:, (q // n_split) ^ step, :, pl.ds(start, tile)],
            out_sem.at[total % slots],
        )

    def one_tile(item, columns, at):
        total = item * n_tiles + at

        @pl.when(total >= slots)
        def _():
            store(item, at).wait()

        start = pl.multiple_of(at * tile, tile)
        piece = lambda s, d: columns[s][z ^ d, :, pl.ds(start, tile)]
        right = jnp.concatenate([piece(s, d) for s, d in pairs], axis=0)
        made[total % slots, 0] = norm * jnp.dot(turned[item], right, preferred_element_type=jnp.float32)
        half = part // 2 if n_split == 1 else n_split // 2
        crossed = []
        for s, d in pairs:
            if n_split == 1:
                values = piece(s, d)
                crossed += [-values[half:], values[:half]]
            else:
                sign = jnp.where((s ^ (q % n_split)) < half, -1.0, 1.0).astype(jnp.bfloat16)
                crossed.append(piece(s ^ half, d) * sign)
        right = jnp.concatenate(crossed, axis=0)
        made[total % slots, 1] = norm * jnp.dot(turned[item], right, preferred_element_type=jnp.float32)
        store(item, at).start()

    for item, arrays in enumerate(operands):
        shards, columns = arrays[:n_parts], arrays[n_parts:]
        left = jnp.concatenate([left_part(shards, s, d) for s, d in pairs], axis=0)
        turned[item] = left.T
        lax.fori_loop(0, n_tiles, lambda at, _: one_tile(item, columns, at), None)
    total = len(items) * n_tiles
    for at in range(max(0, total - slots), total):
        store(at // n_tiles, at % n_tiles).wait()


def product(items, n, n_split, shards, columns, before, n_bins):
    part, channels = shards[0][0].shape[2:]
    depth = n * n_split * part
    tile = min(256, channels)
    slots = min(4, len(items) * channels // tile)
    operands = [x for pair in zip(shards, columns) for arrays in pair for x in arrays]
    specs = [pl.BlockSpec(memory_space=pltpu.VMEM)] * len(operands)
    aliases = {}
    if before is not None:
        aliases = {len(operands): 0}
        operands.append(before)
        specs.append(pl.BlockSpec(memory_space=pl.ANY))
    norm = 1.0 / math.sqrt(depth // 2)
    return pl.pallas_call(
        functools.partial(product_kernel, items, n, n_split, tile, norm),
        out_shape=jax.ShapeDtypeStruct((2, n_bins, channels, 2 * channels), jnp.float32),
        in_specs=specs,
        out_specs=pl.BlockSpec(memory_space=pl.ANY),
        scratch_shapes=[
            pltpu.VMEM((len(items), channels, depth), jnp.bfloat16),
            pltpu.VMEM((slots, 2, channels, tile), jnp.float32),
            pltpu.SemaphoreType.DMA((slots,)),
        ],
        input_output_aliases=aliases,
        cost_estimate=pl.CostEstimate(
            flops=WEIGHT * len(items) * 4 * channels * channels * depth,
            bytes_accessed=WEIGHT * len(items) * 8 * channels * channels,
            transcendentals=0,
        ),
        compiler_params=pltpu.CompilerParams(vmem_limit_bytes=32 << 20),
        name="product",
    )(*operands)


def along_line(values, bit, n):
    return lax.ppermute(values, "col", [(z, z ^ bit) for z in range(n)])


def gather_rows(mine, first, n):
    parts, bit = [mine, first], n // 4
    while bit:
        parts.append(along_line(jnp.concatenate(parts), bit, n))
        bit //= 2
    return parts


def shards(spectra):
    n = lax.axis_size("col")
    n_bins = spectra.shape[1]
    assert lax.axis_size("row") == 2 * n and n % n_bins == 0 and n & (n - 1) == 0
    n_split = n // n_bins
    rows, pieces = whiten(spectra, n, n_split, [(f,) for f in range(n_bins)])
    rows = [x[:, 0] for x in rows]

    def from_chip(values, d):
        return lax.ppermute(values, "row", [(2 * q + k, 2 * (q ^ d) + k) for q in range(n) for k in range(2)])

    def from_core(values):
        return lax.ppermute(values, "row", [(r, r ^ 1) for r in range(2 * n)])

    early = n_bins // 2
    firsts = [along_line(x, n // 2, n) for x in rows[:early]]
    blocks = [from_chip(piece, d) if d else piece for d, piece in enumerate(pieces)]
    firsts, blocks = lax.optimization_barrier((firsts, blocks))
    arrived = [along_line(x, e, n) if e else x for e, x in enumerate(route(blocks))]
    rows[early:], arrived = lax.optimization_barrier((rows[early:], arrived))
    firsts += [along_line(x, n // 2, n) for x in rows[early:]]
    gathered_rows = [gather_rows(mine, first, n) for mine, first in zip(rows, firsts)]
    held = collect(arrived)
    gathered_rows[0], held = lax.optimization_barrier((gathered_rows[0], held))
    near = [held]
    for d in range(1, n):
        low = d & -d
        near.append(from_chip(near[d ^ low], low))
    far = [from_core(x) for x in near]
    near, far = ([x[f * n_split : (f + 1) * n_split] for f in range(n_bins)] for x in (near, far))
    calls = [[(0, False)]]
    for f in range(1, n_bins):
        calls.append([(f - 1, True), (f, False)])
    calls.append([(n_bins - 1, True)])
    out = None
    for items in calls:
        used = [gathered_rows[f] for f, _ in items]
        columns = [(far if other else near)[f] for f, other in items]
        out = product(items, n, n_split, used, columns, out, n_bins)
    return out


def solution(mesh):
    in_specs = (P(None, None, "col", "row"),)
    out_specs = P(None, None, "row", "col")
    return jax.shard_map(shards, mesh=mesh, in_specs=in_specs, out_specs=out_specs, check_vma=False)
```

time: 99.3 us -> 82.1 us (0.83)
  blocking collectives: 11.4 us -> 0 us
  starting transfers between devices: 40.2 us -> 30.4 us
  Pallas kernels: 25 us -> 28.2 us
  waiting for transfers between devices: 20.9 us -> 22.1 us
    ppermute x19 -> x21, waiting for transfers between devices: 7.34 us -> 22.1 us  [the longest x11 22.1 us: along_line(): return lax.ppermute(values, 'col', [(z, z ^ bit) for z in range(n)])]
    all_to_all x1 -> x0, waiting for transfers between devices: 13.6 us -> none  [shards(): held = lax.all_to_all(blocks, 'col', 0, 0, tiled=True)]
    all_to_all x1 -> x0, blocking collectives: 11.4 us -> none  [shards(): lax.all_to_all(pieces, 'row', 0, 0, axis_index_groups=same_core, tiled=True)]
    ppermute x19 -> x21, starting transfers between devices: 35.6 us -> 30.4 us  [the longest x11 15 us: along_line(): return lax.ppermute(values, 'col', [(z, z ^ bit) for z in range(n)])]
    all_to_all x1 -> x0, starting transfers between devices: 4.59 us -> none  [shards(): held = lax.all_to_all(blocks, 'col', 0, 0, tiled=True)]
    pallas_call x4 -> x8, Pallas kernels: 25 us -> 28.2 us  [the longest x5 27.6 us: product(): pl.pallas_call(functools.partial(product_kernel, items, n, n_split, tile,...]
  transfers between devices with their start and end apart: 20 -> 21, of which waited for: 5 -> 6; matrix products, arithmetic and copies ran while one was open for 0% -> 0% of each run, Pallas kernels for 18% -> 29%
where the time goes in v2:
time: 82.1 us; the launch traced here: 82 us
  starting transfers between devices  30.4 us (37%)
  Pallas kernels  28.2 us (34%)
  waiting for transfers between devices  22.1 us (27%)
  local copies, waits for them, and re-layouts  1.04 us (1%)
    pallas_call x5, Pallas kernels, product(): pl.pallas_call(functools.partial(product_kernel, items, n, n_split, tile,...  27.6 us
    ppermute x11, waiting for transfers between devices, along_line(): return lax.ppermute(values, 'col', [(z, z ^ bit) for z in range(n)])  22.1 us
    ppermute x11, starting transfers between devices, along_line(): return lax.ppermute(values, 'col', [(z, z ^ bit) for z in range(n)])  15 us
    ppermute x4, starting transfers between devices, from_core(): return lax.ppermute(values, 'row', [(r, r ^ 1) for r in range(2 * n)])  9.05 us
    ppermute x6, starting transfers between devices, from_chip(): lax.ppermute(values, 'row', [(2 * q + k, 2 * (q ^ d) + k) for q in range(...  6.36 us
  transfers between devices with their start and end apart: 21, of which 6 were waited for; matrix products, arithmetic and copies ran while one was open for 0% of the time, Pallas kernels for 29%

profile of v2, /device:TPU:1, one launch (start us, length us, event | category | flops | bytes accessed | tf_op | source)
XLA Modules:
  0.0 82.0 jit_solution(11334423144602878949)
XLA Ops:
  0.0 0.0 copy-start
  0.0 1.0 %copy-done = bf16[2,4,32,1024]{3,2,1,0:T(8,128)(2,1)S(1)} copy-done((bf16[2,4,32,1024]{3,2,1,0:T(8,128)(2,1)S(1)}, bf16[2,4,32,1024]{3,2,1,0:T(8,128)(2,1)}, u32[]{:S(2)}) %copy-start) | copy-done | bytes 524312
  1.0 0.4 whiten.1
  1.5 3.2 %collective-permute-start.1 = (bf16[1,1,64,1024]{3,2,1,0:T(8,128)(2,1)S(1)}, bf16[1,1,64,1024]{3,2,1,0:T(8,128)(2,1)S(1)}, u32[]{:S(2)}, u32[]{:S(2)}) collective-permute-start(bf16[1,1,64,1024]{3,2,1,0:T(8,128)(2,1)S(1)} %bitcast.16), channel_id=1, source_target_pairs={{0,2},{1,3},{2,0},{3,1},{4,6},{5,7},{6,4},{7,5},{8,10},{9,11},{10,... | collective-permute-start | bytes 393224 | tf_op jit(solution)/shard_map/ppermute | solution.py:197
  4.7 0.1 collective-permute-start
  4.8 1.2 %collective-permute-start.2 = (bf16[64,1024]{1,0:T(8,128)(2,1)S(1)}, bf16[64,1024]{1,0:T(8,128)(2,1)S(1)}, u32[]{:S(2)}, u32[]{:S(2)}) collective-permute-start(bf16[64,1024]{1,0:T(8,128)(2,1)S(1)} %get-tuple-element.38), channel_id=1, source_target_pairs={{0,8},{4,12},{8,0},{12,4},{16,24},{20,28},{24,16},{28,20},{1,9},{5... | collective-permute-start | bytes 393224 | tf_op jit(solution)/shard_map/ppermute | solution.py:217
  6.0 1.2 %collective-permute-start.3 = (bf16[64,1024]{1,0:T(8,128)(2,1)S(1)}, bf16[64,1024]{1,0:T(8,128)(2,1)S(1)}, u32[]{:S(2)}, u32[]{:S(2)}) collective-permute-start(bf16[64,1024]{1,0:T(8,128)(2,1)S(1)} %get-tuple-element.39), channel_id=1, source_target_pairs={{0,16},{4,20},{8,24},{12,28},{16,0},{20,4},{24,8},{28,12},{1,17},{... | collective-permute-start | bytes 393224 | tf_op jit(solution)/shard_map/ppermute | solution.py:217
  7.2 0.2 collective-permute-start.4
  7.4 6.1 %collective-permute-done.1.refs_5_.refs_1_ = bf16[1,1,64,1024]{3,2,1,0:T(8,128)(2,1)S(1)} collective-permute-done((bf16[1,1,64,1024]{3,2,1,0:T(8,128)(2,1)S(1)}, bf16[1,1,64,1024]{3,2,1,0:T(8,128)(2,1)S(1)}, u32[]{:S(2)}, u32[]{:S(2)}) %collective-permute-start.1) | collective-permute-done | bytes 131104 | tf_op jit(solution)/shard_map/ppermute | solution.py:197
  13.5 2.8 %collective-permute-done.refs_1_ = bf16[1,1,64,1024]{3,2,1,0:T(8,128)(2,1)S(1)} collective-permute-done((bf16[1,1,64,1024]{3,2,1,0:T(8,128)(2,1)S(1)}, bf16[1,1,64,1024]{3,2,1,0:T(8,128)(2,1)S(1)}, u32[]{:S(2)}, u32[]{:S(2)}) %collective-permute-start) | collective-permute-done | bytes 131104 | tf_op jit(solution)/shard_map/ppermute | solution.py:197
  16.3 0.0 collective-permute-done.2.refs_1_
  16.3 0.0 collective-permute-done.3.refs_2_
  16.3 0.0 collective-permute-done.4.refs_3_
  16.4 0.1 route.1
  16.5 1.2 %collective-permute-start.5 = (bf16[64,1024]{1,0:T(8,128)(2,1)S(1)}, bf16[64,1024]{1,0:T(8,128)(2,1)S(1)}, u32[]{:S(2)}, u32[]{:S(2)}) collective-permute-start(bf16[64,1024]{1,0:T(8,128)(2,1)S(1)} %get-tuple-element.46), channel_id=1, source_target_pairs={{0,1},{1,0},{2,3},{3,2},{4,5},{5,4},{6,7},{7,6},{8,9},{9,8},{10,11... | collective-permute-start | bytes 393224 | tf_op jit(solution)/shard_map/ppermute | solution.py:197
  17.7 3.1 %collective-permute-start.6 = (bf16[64,1024]{1,0:T(8,128)(2,1)S(1)}, bf16[64,1024]{1,0:T(8,128)(2,1)S(1)}, u32[]{:S(2)}, u32[]{:S(2)}) collective-permute-start(bf16[64,1024]{1,0:T(8,128)(2,1)S(1)} %get-tuple-element.47), channel_id=1, source_target_pairs={{0,2},{1,3},{2,0},{3,1},{4,6},{5,7},{6,4},{7,5},{8,10},{9,11},{10,... | collective-permute-start | bytes 393224 | tf_op jit(solution)/shard_map/ppermute | solution.py:197
  20.8 0.0 collective-permute-start.7
  20.9 0.3 collective-permute-start.10
  21.2 0.0 collective-permute-done.5.refs_1_
  21.2 2.8 %collective-permute-done.6.refs_2_ = bf16[64,1024]{1,0:T(8,128)(2,1)S(1)} collective-permute-done((bf16[64,1024]{1,0:T(8,128)(2,1)S(1)}, bf16[64,1024]{1,0:T(8,128)(2,1)S(1)}, u32[]{:S(2)}, u32[]{:S(2)}) %collective-permute-start.6) | collective-permute-done | bytes 131104 | tf_op jit(solution)/shard_map/ppermute | solution.py:197
  24.0 5.7 %collective-permute-done.7.refs_3_ = bf16[64,1024]{1,0:T(8,128)(2,1)S(1)} collective-permute-done((bf16[64,1024]{1,0:T(8,128)(2,1)S(1)}, bf16[64,1024]{1,0:T(8,128)(2,1)S(1)}, u32[]{:S(2)}, u32[]{:S(2)}) %collective-permute-start.7) | collective-permute-done | bytes 131104 | tf_op jit(solution)/shard_map/ppermute | solution.py:197
  29.6 4.1 %collective-permute-start.14 = (bf16[1,1,64,1024]{3,2,1,0:T(8,128)(2,1)S(1)}, bf16[1,1,64,1024]{3,2,1,0:T(8,128)(2,1)S(1)}, u32[]{:S(2)}, u32[]{:S(2)}) collective-permute-start(bf16[1,1,64,1024]{3,2,1,0:T(8,128)(2,1)S(1)} %bitcast.12), channel_id=1, source_target_pairs={{0,2},{1,3},{2,0},{3,1},{4,6},{5,7},{6,4},{7,5},{8,10},{9,11},{10,... | collective-permute-start | bytes 393224 | tf_op jit(solution)/shard_map/ppermute | solution.py:197
  33.7 0.0 collective-permute-start.8
  33.8 1.4 %collective-permute-start.17 = (bf16[2,1,64,1024]{3,2,1,0:T(8,128)(2,1)S(1)}, bf16[2,1,64,1024]{3,2,1,0:T(8,128)(2,1)S(1)}, u32[]{:S(2)}, u32[]{:S(2)}) collective-permute-start(bf16[2,1,64,1024]{3,2,1,0:T(8,128)(2,1)S(1)} %pad_maximum_fusion.3), channel_id=1, source_target_pairs={{0,1},{1,0},{2,3},{3,2},{4,5},{5,4},{6,7},{7,6},{8,9},{9,8},{10,11... | collective-permute-start | bytes 786440 | tf_op jit(solution)/shard_map/ppermute | solution.py:197
  35.2 0.0 collective-permute-done.10.refs_2_
  35.2 1.3 %collective-permute-start.18 = (bf16[4,64,1024]{2,1,0:T(8,128)(2,1)S(1)}, bf16[4,64,1024]{2,1,0:T(8,128)(2,1)S(1)}, u32[]{:S(2)}, u32[]{:S(2)}) collective-permute-start(bf16[4,64,1024]{2,1,0:T(8,128)(2,1)S(1)} %collect.1.refs_3_), channel_id=1, source_target_pairs={{0,8},{4,12},{8,0},{12,4},{16,24},{20,28},{24,16},{28,20},{1,9},{5... | collective-permute-start | bytes 1572872 | tf_op jit(solution)/shard_map/ppermute | solution.py:217
  36.5 2.5 %collective-permute-start.20 = (bf16[4,64,1024]{2,1,0:T(8,128)(2,1)S(1)}, bf16[4,64,1024]{2,1,0:T(8,128)(2,1)S(1)}, u32[]{:S(2)}, u32[]{:S(2)}) collective-permute-start(bf16[4,64,1024]{2,1,0:T(8,128)(2,1)S(1)} %collect.1.refs_3_), channel_id=1, source_target_pairs={{0,4},{4,0},{8,12},{12,8},{16,20},{20,16},{24,28},{28,24},{1,5},{5... | collective-permute-start | bytes 1572872 | tf_op jit(solution)/shard_map/ppermute | solution.py:220
  39.0 1.7 %collective-permute-done.14.refs_5_.refs_1_ = bf16[1,1,64,1024]{3,2,1,0:T(8,128)(2,1)S(1)} collective-permute-done((bf16[1,1,64,1024]{3,2,1,0:T(8,128)(2,1)S(1)}, bf16[1,1,64,1024]{3,2,1,0:T(8,128)(2,1)S(1)}, u32[]{:S(2)}, u32[]{:S(2)}) %collective-permute-start.14) | collective-permute-done | bytes 131104 | tf_op jit(solution)/shard_map/ppermute | solution.py:197
  40.7 1.2 %collective-permute-start.11 = (bf16[4,64,1024]{2,1,0:T(8,128)(2,1)S(1)}, bf16[4,64,1024]{2,1,0:T(8,128)(2,1)S(1)}, u32[]{:S(2)}, u32[]{:S(2)}) collective-permute-start(bf16[4,64,1024]{2,1,0:T(8,128)(2,1)S(1)} %collect.1.refs_3_), channel_id=1, source_target_pairs={{0,16},{4,20},{8,24},{12,28},{16,0},{20,4},{24,8},{28,12},{1,17},{... | collective-permute-start | bytes 1572872 | tf_op jit(solution)/shard_map/ppermute | solution.py:217
  41.9 3.0 %collective-permute-done.8.refs_5_.refs_1_ = bf16[1,1,64,1024]{3,2,1,0:T(8,128)(2,1)S(1)} collective-permute-done((bf16[1,1,64,1024]{3,2,1,0:T(8,128)(2,1)S(1)}, bf16[1,1,64,1024]{3,2,1,0:T(8,128)(2,1)S(1)}, u32[]{:S(2)}, u32[]{:S(2)}) %collective-permute-start.8) | collective-permute-done | bytes 131104 | tf_op jit(solution)/shard_map/ppermute | solution.py:197
  45.0 0.0 collective-permute-start.15
  45.0 4.0 %product.5.refs_8_ = f32[2,4,1024,2048]{3,2,1,0:T(8,128)} custom-call(bf16[1,1,64,1024]{3,2,1,0:T(8,128)(2,1)S(1)} %bitcast.6, bf16[1,1,64,1024]{3,2,1,0:T(8,128)(2,1)S(1)} %collective-permute-done.refs_1_, bf16[2,1,64,1024]{3,2,1,0:T(8,128)(2,1)S(1)} %collective-permute-done.10.refs_2_, bf16[4,64,1024]{2,1,0:T(8,128)(2,1)S(1)} %collect.1.refs_3_), custom_call_target="tpu_custom_call" | custom-call | flops 4294967296 | bytes 33554432 | tf_op jit(solution)/shard_map/product/pallas_call | solution.py:175
  49.0 0.0 collective-permute-done.17.refs_6_.refs_2_
  49.0 1.5 %collective-permute-start.9 = (bf16[2,1,64,1024]{3,2,1,0:T(8,128)(2,1)S(1)}, bf16[2,1,64,1024]{3,2,1,0:T(8,128)(2,1)S(1)}, u32[]{:S(2)}, u32[]{:S(2)}) collective-permute-start(bf16[2,1,64,1024]{3,2,1,0:T(8,128)(2,1)S(1)} %pad_maximum_fusion), channel_id=1, source_target_pairs={{0,1},{1,0},{2,3},{3,2},{4,5},{5,4},{6,7},{7,6},{8,9},{9,8},{10,11... | collective-permute-start | bytes 786440 | tf_op jit(solution)/shard_map/ppermute | solution.py:197
  50.5 0.0 collective-permute-done.11.refs_7_
  50.5 1.2 %collective-permute-start.12 = (bf16[4,64,1024]{2,1,0:T(8,128)(2,1)S(1)}, bf16[4,64,1024]{2,1,0:T(8,128)(2,1)S(1)}, u32[]{:S(2)}, u32[]{:S(2)}) collective-permute-start(bf16[4,64,1024]{2,1,0:T(8,128)(2,1)S(1)} %collective-permute-done.11.refs_7_), channel_id=1, source_target_pairs={{0,8},{4,12},{8,0},{12,4},{16,24},{20,28},{24,16},{28,20},{1,9},{5... | collective-permute-start | bytes 1572872 | tf_op jit(solution)/shard_map/ppermute | solution.py:217
  51.8 0.0 collective-permute-done.18.refs_7_
  51.8 4.7 %collective-permute-start.16 = (bf16[4,64,1024]{2,1,0:T(8,128)(2,1)S(1)}, bf16[4,64,1024]{2,1,0:T(8,128)(2,1)S(1)}, u32[]{:S(2)}, u32[]{:S(2)}) collective-permute-start(bf16[4,64,1024]{2,1,0:T(8,128)(2,1)S(1)} %collective-permute-done.11.refs_7_), channel_id=1, source_target_pairs={{0,4},{4,0},{8,12},{12,8},{16,20},{20,16},{24,28},{28,24},{1,5},{5... | collective-permute-start | bytes 1572872 | tf_op jit(solution)/shard_map/ppermute | solution.py:220
  56.5 0.0 collective-permute-done.20.refs_3_
  56.5 0.1 collective-permute-start.19
  56.6 6.5 %product.6.refs_8_ = f32[2,4,1024,2048]{3,2,1,0:T(8,128)} custom-call(bf16[1,1,64,1024]{3,2,1,0:T(8,128)(2,1)S(1)} %bitcast.7, bf16[1,1,64,1024]{3,2,1,0:T(8,128)(2,1)S(1)} %collective-permute-done.refs_1_, bf16[2,1,64,1024]{3,2,1,0:T(8,128)(2,1)S(1)} %collective-permute-done.10.refs_2_, ...), custom_call_target="tpu_custom_call", output_to_operand_aliasing={{}: (8, {})} | custom-call | flops 8589934592 | bytes 67108864 | tf_op jit(solution)/shard_map/product/pallas_call | solution.py:175
  63.1 0.0 collective-permute-done.12.refs_7_
  63.1 1.8 %collective-permute-start.13 = (bf16[4,64,1024]{2,1,0:T(8,128)(2,1)S(1)}, bf16[4,64,1024]{2,1,0:T(8,128)(2,1)S(1)}, u32[]{:S(2)}, u32[]{:S(2)}) collective-permute-start(bf16[4,64,1024]{2,1,0:T(8,128)(2,1)S(1)} %collective-permute-done.12.refs_7_), channel_id=1, source_target_pairs={{0,4},{4,0},{8,12},{12,8},{16,20},{20,16},{24,28},{28,24},{1,5},{5... | collective-permute-start | bytes 1572872 | tf_op jit(solution)/shard_map/ppermute | solution.py:220
  64.9 0.0 collective-permute-done.15.refs_6_.refs_2_
  64.9 0.0 collective-permute-done.19.refs_3_
  64.9 6.5 %product.7.refs_8_ = f32[2,4,1024,2048]{3,2,1,0:T(8,128)} custom-call(bf16[1,1,64,1024]{3,2,1,0:T(8,128)(2,1)S(1)} %bitcast.19, bf16[1,1,64,1024]{3,2,1,0:T(8,128)(2,1)S(1)} %collective-permute-done.1.refs_5_.refs_1_, bf16[2,1,64,1024]{3,2,1,0:T(8,128)(2,1)S(1)} %collective-permute-done.17.refs_6_.refs_2_, ...), custom_call_target="tpu_custom_call", output_to_operand_aliasing={{}: (8, {})} | custom-call | flops 8589934592 | bytes 67108864 | tf_op jit(solution)/shard_map/product/pallas_call | solution.py:175
  71.4 0.0 collective-permute-done.9.refs_6_.refs_2_
  71.4 0.0 collective-permute-done.16.refs_3_
  71.4 6.5 %product.8.refs_4_ = f32[2,4,1024,2048]{3,2,1,0:T(8,128)} custom-call(bf16[1,1,64,1024]{3,2,1,0:T(8,128)(2,1)S(1)} %bitcast.15, bf16[1,1,64,1024]{3,2,1,0:T(8,128)(2,1)S(1)} %collective-permute-done.14.refs_5_.refs_1_, bf16[2,1,64,1024]{3,2,1,0:T(8,128)(2,1)S(1)} %collective-permute-done.15.refs_6_.refs_2_, ...), custom_call_target="tpu_custom_call", output_to_operand_aliasing={{}: (8, {})} | custom-call | flops 8589934592 | bytes 67108864 | tf_op jit(solution)/shard_map/product/pallas_call | solution.py:175
  78.0 0.0 collective-permute-done.13.refs_3_
  78.0 4.0 %product.9 = f32[2,4,1024,2048]{3,2,1,0:T(8,128)} custom-call(bf16[1,1,64,1024]{3,2,1,0:T(8,128)(2,1)S(1)} %bitcast.11, bf16[1,1,64,1024]{3,2,1,0:T(8,128)(2,1)S(1)} %collective-permute-done.8.refs_5_.refs_1_, bf16[2,1,64,1024]{3,2,1,0:T(8,128)(2,1)S(1)} %collective-permute-done.9.refs_6_.refs_2_, ...), custom_call_target="tpu_custom_call", output_to_operand_aliasing={{}: (4, {})} | custom-call | flops 4294967296 | bytes 33554432 | tf_op jit(solution)/shard_map/product/pallas_call | solution.py:175
  (5 shorter events, 0.1 us)
Async XLA Ops:
  0.0 1.0 %copy-start = (bf16[2,4,32,1024]{3,2,1,0:T(8,128)(2,1)S(1)}, bf16[2,4,32,1024]{3,2,1,0:T(8,128)(2,1)}, u32[]{:S(2)}) copy-start(bf16[2,4,32,1024]{3,2,1,0:T(8,128)(2,1)} %raw.1) | copy-start | bytes 1572868
  1.5 12.0 %collective-permute-start.1 = (bf16[1,1,64,1024]{3,2,1,0:T(8,128)(2,1)S(1)}, bf16[1,1,64,1024]{3,2,1,0:T(8,128)(2,1)S(1)}, u32[]{:S(2)}, u32[]{:S(2)}) collective-permute-start(bf16[1,1,64,1024]{3,2,1,0:T(8,128)(2,1)S(1)} %bitcast.16), channel_id=1, source_target_pairs={{0,2},{1,3},{2,0},{3,1},{4,6},{5,7},{6,4},{7,5},{8,10},{9,11},{10,... | collective-permute-start | bytes 393224 | tf_op jit(solution)/shard_map/ppermute | solution.py:197
  4.7 11.6 %collective-permute-start = (bf16[1,1,64,1024]{3,2,1,0:T(8,128)(2,1)S(1)}, bf16[1,1,64,1024]{3,2,1,0:T(8,128)(2,1)S(1)}, u32[]{:S(2)}, u32[]{:S(2)}) collective-permute-start(bf16[1,1,64,1024]{3,2,1,0:T(8,128)(2,1)S(1)} %bitcast.4), channel_id=1, source_target_pairs={{0,2},{1,3},{2,0},{3,1},{4,6},{5,7},{6,4},{7,5},{8,10},{9,11},{10,... | collective-permute-start | bytes 393224 | tf_op jit(solution)/shard_map/ppermute | solution.py:197
  4.8 11.6 %collective-permute-start.2 = (bf16[64,1024]{1,0:T(8,128)(2,1)S(1)}, bf16[64,1024]{1,0:T(8,128)(2,1)S(1)}, u32[]{:S(2)}, u32[]{:S(2)}) collective-permute-start(bf16[64,1024]{1,0:T(8,128)(2,1)S(1)} %get-tuple-element.38), channel_id=1, source_target_pairs={{0,8},{4,12},{8,0},{12,4},{16,24},{20,28},{24,16},{28,20},{1,9},{5... | collective-permute-start | bytes 393224 | tf_op jit(solution)/shard_map/ppermute | solution.py:217
  6.0 10.4 %collective-permute-start.3 = (bf16[64,1024]{1,0:T(8,128)(2,1)S(1)}, bf16[64,1024]{1,0:T(8,128)(2,1)S(1)}, u32[]{:S(2)}, u32[]{:S(2)}) collective-permute-start(bf16[64,1024]{1,0:T(8,128)(2,1)S(1)} %get-tuple-element.39), channel_id=1, source_target_pairs={{0,16},{4,20},{8,24},{12,28},{16,0},{20,4},{24,8},{28,12},{1,17},{... | collective-permute-start | bytes 393224 | tf_op jit(solution)/shard_map/ppermute | solution.py:217
  7.2 9.1 %collective-permute-start.4 = (bf16[64,1024]{1,0:T(8,128)(2,1)S(1)}, bf16[64,1024]{1,0:T(8,128)(2,1)S(1)}, u32[]{:S(2)}, u32[]{:S(2)}) collective-permute-start(bf16[64,1024]{1,0:T(8,128)(2,1)S(1)} %get-tuple-element.40), channel_id=1, source_target_pairs={{0,24},{4,28},{8,16},{12,20},{16,8},{20,12},{24,0},{28,4},{1,25},{... | collective-permute-start | bytes 393224 | tf_op jit(solution)/shard_map/ppermute | solution.py:217
  16.5 4.7 %collective-permute-start.5 = (bf16[64,1024]{1,0:T(8,128)(2,1)S(1)}, bf16[64,1024]{1,0:T(8,128)(2,1)S(1)}, u32[]{:S(2)}, u32[]{:S(2)}) collective-permute-start(bf16[64,1024]{1,0:T(8,128)(2,1)S(1)} %get-tuple-element.46), channel_id=1, source_target_pairs={{0,1},{1,0},{2,3},{3,2},{4,5},{5,4},{6,7},{7,6},{8,9},{9,8},{10,11... | collective-permute-start | bytes 393224 | tf_op jit(solution)/shard_map/ppermute | solution.py:197
  17.7 6.3 %collective-permute-start.6 = (bf16[64,1024]{1,0:T(8,128)(2,1)S(1)}, bf16[64,1024]{1,0:T(8,128)(2,1)S(1)}, u32[]{:S(2)}, u32[]{:S(2)}) collective-permute-start(bf16[64,1024]{1,0:T(8,128)(2,1)S(1)} %get-tuple-element.47), channel_id=1, source_target_pairs={{0,2},{1,3},{2,0},{3,1},{4,6},{5,7},{6,4},{7,5},{8,10},{9,11},{10,... | collective-permute-start | bytes 393224 | tf_op jit(solution)/shard_map/ppermute | solution.py:197
  20.8 8.8 %collective-permute-start.7 = (bf16[64,1024]{1,0:T(8,128)(2,1)S(1)}, bf16[64,1024]{1,0:T(8,128)(2,1)S(1)}, u32[]{:S(2)}, u32[]{:S(2)}) collective-permute-start(bf16[64,1024]{1,0:T(8,128)(2,1)S(1)} %get-tuple-element.48), channel_id=1, source_target_pairs={{0,3},{1,2},{2,1},{3,0},{4,7},{5,6},{6,5},{7,4},{8,11},{9,10},{10,... | collective-permute-start | bytes 393224 | tf_op jit(solution)/shard_map/ppermute | solution.py:197
  20.9 14.4 %collective-permute-start.10 = (bf16[2,1,64,1024]{3,2,1,0:T(8,128)(2,1)S(1)}, bf16[2,1,64,1024]{3,2,1,0:T(8,128)(2,1)S(1)}, u32[]{:S(2)}, u32[]{:S(2)}) collective-permute-start(bf16[2,1,64,1024]{3,2,1,0:T(8,128)(2,1)S(1)} %pad_maximum_fusion.1), channel_id=1, source_target_pairs={{0,1},{1,0},{2,3},{3,2},{4,5},{5,4},{6,7},{7,6},{8,9},{9,8},{10,11... | collective-permute-start | bytes 786440 | tf_op jit(solution)/shard_map/ppermute | solution.py:197
  29.6 11.1 %collective-permute-start.14 = (bf16[1,1,64,1024]{3,2,1,0:T(8,128)(2,1)S(1)}, bf16[1,1,64,1024]{3,2,1,0:T(8,128)(2,1)S(1)}, u32[]{:S(2)}, u32[]{:S(2)}) collective-permute-start(bf16[1,1,64,1024]{3,2,1,0:T(8,128)(2,1)S(1)} %bitcast.12), channel_id=1, source_target_pairs={{0,2},{1,3},{2,0},{3,1},{4,6},{5,7},{6,4},{7,5},{8,10},{9,11},{10,... | collective-permute-start | bytes 393224 | tf_op jit(solution)/shard_map/ppermute | solution.py:197
  33.7 11.3 %collective-permute-start.8 = (bf16[1,1,64,1024]{3,2,1,0:T(8,128)(2,1)S(1)}, bf16[1,1,64,1024]{3,2,1,0:T(8,128)(2,1)S(1)}, u32[]{:S(2)}, u32[]{:S(2)}) collective-permute-start(bf16[1,1,64,1024]{3,2,1,0:T(8,128)(2,1)S(1)} %bitcast.8), channel_id=1, source_target_pairs={{0,2},{1,3},{2,0},{3,1},{4,6},{5,7},{6,4},{7,5},{8,10},{9,11},{10,... | collective-permute-start | bytes 393224 | tf_op jit(solution)/shard_map/ppermute | solution.py:197
  33.8 15.2 %collective-permute-start.17 = (bf16[2,1,64,1024]{3,2,1,0:T(8,128)(2,1)S(1)}, bf16[2,1,64,1024]{3,2,1,0:T(8,128)(2,1)S(1)}, u32[]{:S(2)}, u32[]{:S(2)}) collective-permute-start(bf16[2,1,64,1024]{3,2,1,0:T(8,128)(2,1)S(1)} %pad_maximum_fusion.3), channel_id=1, source_target_pairs={{0,1},{1,0},{2,3},{3,2},{4,5},{5,4},{6,7},{7,6},{8,9},{9,8},{10,11... | collective-permute-start | bytes 786440 | tf_op jit(solution)/shard_map/ppermute | solution.py:197
  35.2 16.5 %collective-permute-start.18 = (bf16[4,64,1024]{2,1,0:T(8,128)(2,1)S(1)}, bf16[4,64,1024]{2,1,0:T(8,128)(2,1)S(1)}, u32[]{:S(2)}, u32[]{:S(2)}) collective-permute-start(bf16[4,64,1024]{2,1,0:T(8,128)(2,1)S(1)} %collect.1.refs_3_), channel_id=1, source_target_pairs={{0,8},{4,12},{8,0},{12,4},{16,24},{20,28},{24,16},{28,20},{1,9},{5... | collective-permute-start | bytes 1572872 | tf_op jit(solution)/shard_map/ppermute | solution.py:217
  36.5 20.0 %collective-permute-start.20 = (bf16[4,64,1024]{2,1,0:T(8,128)(2,1)S(1)}, bf16[4,64,1024]{2,1,0:T(8,128)(2,1)S(1)}, u32[]{:S(2)}, u32[]{:S(2)}) collective-permute-start(bf16[4,64,1024]{2,1,0:T(8,128)(2,1)S(1)} %collect.1.refs_3_), channel_id=1, source_target_pairs={{0,4},{4,0},{8,12},{12,8},{16,20},{20,16},{24,28},{28,24},{1,5},{5... | collective-permute-start | bytes 1572872 | tf_op jit(solution)/shard_map/ppermute | solution.py:220
  40.7 9.9 %collective-permute-start.11 = (bf16[4,64,1024]{2,1,0:T(8,128)(2,1)S(1)}, bf16[4,64,1024]{2,1,0:T(8,128)(2,1)S(1)}, u32[]{:S(2)}, u32[]{:S(2)}) collective-permute-start(bf16[4,64,1024]{2,1,0:T(8,128)(2,1)S(1)} %collect.1.refs_3_), channel_id=1, source_target_pairs={{0,16},{4,20},{8,24},{12,28},{16,0},{20,4},{24,8},{28,12},{1,17},{... | collective-permute-start | bytes 1572872 | tf_op jit(solution)/shard_map/ppermute | solution.py:217
  45.0 19.9 %collective-permute-start.15 = (bf16[2,1,64,1024]{3,2,1,0:T(8,128)(2,1)S(1)}, bf16[2,1,64,1024]{3,2,1,0:T(8,128)(2,1)S(1)}, u32[]{:S(2)}, u32[]{:S(2)}) collective-permute-start(bf16[2,1,64,1024]{3,2,1,0:T(8,128)(2,1)S(1)} %pad_maximum_fusion.2), channel_id=1, source_target_pairs={{0,1},{1,0},{2,3},{3,2},{4,5},{5,4},{6,7},{7,6},{8,9},{9,8},{10,11... | collective-permute-start | bytes 786440 | tf_op jit(solution)/shard_map/ppermute | solution.py:197
  49.0 22.4 %collective-permute-start.9 = (bf16[2,1,64,1024]{3,2,1,0:T(8,128)(2,1)S(1)}, bf16[2,1,64,1024]{3,2,1,0:T(8,128)(2,1)S(1)}, u32[]{:S(2)}, u32[]{:S(2)}) collective-permute-start(bf16[2,1,64,1024]{3,2,1,0:T(8,128)(2,1)S(1)} %pad_maximum_fusion), channel_id=1, source_target_pairs={{0,1},{1,0},{2,3},{3,2},{4,5},{5,4},{6,7},{7,6},{8,9},{9,8},{10,11... | collective-permute-start | bytes 786440 | tf_op jit(solution)/shard_map/ppermute | solution.py:197
  50.5 12.6 %collective-permute-start.12 = (bf16[4,64,1024]{2,1,0:T(8,128)(2,1)S(1)}, bf16[4,64,1024]{2,1,0:T(8,128)(2,1)S(1)}, u32[]{:S(2)}, u32[]{:S(2)}) collective-permute-start(bf16[4,64,1024]{2,1,0:T(8,128)(2,1)S(1)} %collective-permute-done.11.refs_7_), channel_id=1, source_target_pairs={{0,8},{4,12},{8,0},{12,4},{16,24},{20,28},{24,16},{28,20},{1,9},{5... | collective-permute-start | bytes 1572872 | tf_op jit(solution)/shard_map/ppermute | solution.py:217
  51.8 19.7 %collective-permute-start.16 = (bf16[4,64,1024]{2,1,0:T(8,128)(2,1)S(1)}, bf16[4,64,1024]{2,1,0:T(8,128)(2,1)S(1)}, u32[]{:S(2)}, u32[]{:S(2)}) collective-permute-start(bf16[4,64,1024]{2,1,0:T(8,128)(2,1)S(1)} %collective-permute-done.11.refs_7_), channel_id=1, source_target_pairs={{0,4},{4,0},{8,12},{12,8},{16,20},{20,16},{24,28},{28,24},{1,5},{5... | collective-permute-start | bytes 1572872 | tf_op jit(solution)/shard_map/ppermute | solution.py:220
  56.5 8.4 %collective-permute-start.19 = (bf16[4,64,1024]{2,1,0:T(8,128)(2,1)S(1)}, bf16[4,64,1024]{2,1,0:T(8,128)(2,1)S(1)}, u32[]{:S(2)}, u32[]{:S(2)}) collective-permute-start(bf16[4,64,1024]{2,1,0:T(8,128)(2,1)S(1)} %collective-permute-done.18.refs_7_), channel_id=1, source_target_pairs={{0,4},{4,0},{8,12},{12,8},{16,20},{20,16},{24,28},{28,24},{1,5},{5... | collective-permute-start | bytes 1572872 | tf_op jit(solution)/shard_map/ppermute | solution.py:220
  63.1 14.9 %collective-permute-start.13 = (bf16[4,64,1024]{2,1,0:T(8,128)(2,1)S(1)}, bf16[4,64,1024]{2,1,0:T(8,128)(2,1)S(1)}, u32[]{:S(2)}, u32[]{:S(2)}) collective-permute-start(bf16[4,64,1024]{2,1,0:T(8,128)(2,1)S(1)} %collective-permute-done.12.refs_7_), channel_id=1, source_target_pairs={{0,4},{4,0},{8,12},{12,8},{16,20},{20,16},{24,28},{28,24},{1,5},{5... | collective-permute-start | bytes 1572872 | tf_op jit(solution)/shard_map/ppermute | solution.py:220

commit v3 on v2

--- a/solution.py
+++ b/solution.py
@@ -219,31 +219,48 @@
     def from_core(values):
         return lax.ppermute(values, "row", [(r, r ^ 1) for r in range(2 * n)])
 
-    early = n_bins // 2
-    firsts = [along_line(x, n // 2, n) for x in rows[:early]]
+    first = along_line(rows[0], n // 2, n)
     blocks = [from_chip(piece, d) if d else piece for d, piece in enumerate(pieces)]
-    firsts, blocks = lax.optimization_barrier((firsts, blocks))
+    first, blocks = lax.optimization_barrier((first, blocks))
+    row_parts = [gather_rows(rows[0], first, n)]
     arrived = [along_line(x, e, n) if e else x for e, x in enumerate(route(blocks))]
-    rows[early:], arrived = lax.optimization_barrier((rows[early:], arrived))
-    firsts += [along_line(x, n // 2, n) for x in rows[early:]]
-    gathered_rows = [gather_rows(mine, first, n) for mine, first in zip(rows, firsts)]
-    held = collect(arrived)
-    gathered_rows[0], held = lax.optimization_barrier((gathered_rows[0], held))
-    near = [held]
+    row_parts[0], arrived = lax.optimization_barrier((row_parts[0], arrived))
+    near = [collect(arrived)]
     for d in range(1, n):
         low = d & -d
-        near.append(from_chip(near[d ^ low], low))
-    far = [from_core(x) for x in near]
-    near, far = ([x[f * n_split : (f + 1) * n_split] for f in range(n_bins)] for x in (near, far))
-    calls = [[(0, False)]]
-    for f in range(1, n_bins):
-        calls.append([(f - 1, True), (f, False)])
-    calls.append([(n_bins - 1, True)])
-    out = None
-    for items in calls:
-        used = [gathered_rows[f] for f, _ in items]
-        columns = [(far if other else near)[f] for f, other in items]
-        out = product(items, n, n_split, used, columns, out, n_bins)
+        if d == low or d < n_split:
+            near.append(from_chip(near[d ^ low], low))
+        else:
+            near.append(None)
+    far = [from_core(x) for x in near[:n_split]]
+    rows[1], near[0] = lax.optimization_barrier((rows[1], near[0]))
+    firsts = [first]
+    for f in range(1, min(3, n_bins)):
+        if f > 1:
+            rows[f], firsts[-1] = lax.optimization_barrier((rows[f], firsts[-1]))
+        firsts.append(along_line(rows[f], n // 2, n))
+    row_parts.append(gather_rows(rows[1], firsts[1], n))
+
+    call = functools.partial(product, n=n, n_split=n_split, n_bins=n_bins)
+    piece = lambda x, f: x[f * n_split : (f + 1) * n_split]
+    out = call([(0, False), (0, True)], shards=[row_parts[0]] * 2, columns=[piece(near, 0), piece(far, 0)], before=None)
+    held = (rows[2:], firsts[2:], near[n_split:])
+    out, (rows[2:], firsts[2:], near[n_split:]) = lax.optimization_barrier((out, held))
+    for f in range(2, n_bins):
+        if f == len(firsts):
+            firsts.append(along_line(rows[f], n // 2, n))
+        row_parts.append(gather_rows(rows[f], firsts[f], n))
+    for d in range(n_split, n):
+        low = d & -d
+        if near[d] is None:
+            near[d] = from_chip(near[d ^ low], low)
+    for f in range(1, n_bins + 1):
+        if f < n_bins:
+            mine, out = lax.optimization_barrier((piece(near, f), out))
+            far += [from_core(x) for x in mine]
+        items = [(f - 1, True)] * (f > 1) + [(f, False)] * (f < n_bins)
+        columns = [piece(far if other else near, at) for at, other in items]
+        out = call(items, shards=[row_parts[at] for at, _ in items], columns=columns, before=out)
     return out
 
 

time: 82.1 us -> 79 us (0.962)
  starting transfers between devices: 30.4 us -> 27.5 us
    ppermute x4, starting transfers between devices: 9.05 us -> 5.65 us  [from_core(): return lax.ppermute(values, 'row', [(r, r ^ 1) for r in range(2 * n)])]
    ppermute x11, waiting for transfers between devices: 22.1 us -> 20.3 us  [along_line(): return lax.ppermute(values, 'col', [(z, z ^ bit) for z in range(n)])]
    ppermute x6, waiting for transfers between devices: 0.02 us -> 1.63 us  [from_chip(): lax.ppermute(values, 'row', [(2 * q + k, 2 * (q ^ d) + k) for q in range(...]
  transfers between devices with their start and end apart: 21 -> 21, of which waited for: 6 -> 5; matrix products, arithmetic and copies ran while one was open for 0% -> 0% of each run, Pallas kernels for 29% -> 30%
where the time goes in v3:
time: 79 us; the launch traced here: 78.9 us
  Pallas kernels  28.1 us (36%)
  starting transfers between devices  27.5 us (35%)
  waiting for transfers between devices  22 us (28%)
  local copies, waits for them, and re-layouts  1.04 us (1%)
    pallas_call x5, Pallas kernels, product(): pl.pallas_call(functools.partial(product_kernel, items, n, n_split, tile,...  27.6 us
    ppermute x11, waiting for transfers between devices, along_line(): return lax.ppermute(values, 'col', [(z, z ^ bit) for z in range(n)])  20.3 us
    ppermute x11, starting transfers between devices, along_line(): return lax.ppermute(values, 'col', [(z, z ^ bit) for z in range(n)])  15.5 us
    ppermute x6, starting transfers between devices, from_chip(): lax.ppermute(values, 'row', [(2 * q + k, 2 * (q ^ d) + k) for q in range(...  6.37 us
    ppermute x4, starting transfers between devices, from_core(): return lax.ppermute(values, 'row', [(r, r ^ 1) for r in range(2 * n)])  5.65 us
    ppermute x6, waiting for transfers between devices, from_chip(): lax.ppermute(values, 'row', [(2 * q + k, 2 * (q ^ d) + k) for q in range(...  1.63 us
  transfers between devices with their start and end apart: 21, of which 5 were waited for; matrix products, arithmetic and copies ran while one was open for 0% of the time, Pallas kernels for 30%

profile of v3, /device:TPU:1, one launch (start us, length us, event | category | flops | bytes accessed | tf_op | source)
XLA Modules:
  0.0 78.9 jit_solution(10522261544532198126)
XLA Ops:
  0.0 0.0 copy-start
  0.0 1.0 %copy-done = bf16[2,4,32,1024]{3,2,1,0:T(8,128)(2,1)S(1)} copy-done((bf16[2,4,32,1024]{3,2,1,0:T(8,128)(2,1)S(1)}, bf16[2,4,32,1024]{3,2,1,0:T(8,128)(2,1)}, u32[]{:S(2)}) %copy-start) | copy-done | bytes 524312
  1.0 0.4 whiten.1
  1.5 3.2 %collective-permute-start = (bf16[1,1,64,1024]{3,2,1,0:T(8,128)(2,1)S(1)}, bf16[1,1,64,1024]{3,2,1,0:T(8,128)(2,1)S(1)}, u32[]{:S(2)}, u32[]{:S(2)}) collective-permute-start(bf16[1,1,64,1024]{3,2,1,0:T(8,128)(2,1)S(1)} %bitcast.4), channel_id=1, source_target_pairs={{0,2},{1,3},{2,0},{3,1},{4,6},{5,7},{6,4},{7,5},{8,10},{9,11},{10,... | collective-permute-start | bytes 393224 | tf_op jit(solution)/shard_map/ppermute | solution.py:197
  4.7 1.2 %collective-permute-start.1 = (bf16[64,1024]{1,0:T(8,128)(2,1)S(1)}, bf16[64,1024]{1,0:T(8,128)(2,1)S(1)}, u32[]{:S(2)}, u32[]{:S(2)}) collective-permute-start(bf16[64,1024]{1,0:T(8,128)(2,1)S(1)} %get-tuple-element.47), channel_id=1, source_target_pairs={{0,8},{4,12},{8,0},{12,4},{16,24},{20,28},{24,16},{28,20},{1,9},{5... | collective-permute-start | bytes 393224 | tf_op jit(solution)/shard_map/ppermute | solution.py:217
  5.9 1.2 %collective-permute-start.2 = (bf16[64,1024]{1,0:T(8,128)(2,1)S(1)}, bf16[64,1024]{1,0:T(8,128)(2,1)S(1)}, u32[]{:S(2)}, u32[]{:S(2)}) collective-permute-start(bf16[64,1024]{1,0:T(8,128)(2,1)S(1)} %get-tuple-element.48), channel_id=1, source_target_pairs={{0,16},{4,20},{8,24},{12,28},{16,0},{20,4},{24,8},{28,12},{1,17},{... | collective-permute-start | bytes 393224 | tf_op jit(solution)/shard_map/ppermute | solution.py:217
  7.1 0.2 collective-permute-start.3
  7.3 3.4 %collective-permute-done.refs_1_.refs_5_ = bf16[1,1,64,1024]{3,2,1,0:T(8,128)(2,1)S(1)} collective-permute-done((bf16[1,1,64,1024]{3,2,1,0:T(8,128)(2,1)S(1)}, bf16[1,1,64,1024]{3,2,1,0:T(8,128)(2,1)S(1)}, u32[]{:S(2)}, u32[]{:S(2)}) %collective-permute-start) | collective-permute-done | bytes 131104 | tf_op jit(solution)/shard_map/ppermute | solution.py:197
  10.7 0.0 collective-permute-done.1.refs_1_
  10.7 0.0 collective-permute-done.2.refs_2_
  10.7 1.6 %collective-permute-done.3.refs_3_ = bf16[64,1024]{1,0:T(8,128)(2,1)S(1)} collective-permute-done((bf16[64,1024]{1,0:T(8,128)(2,1)S(1)}, bf16[64,1024]{1,0:T(8,128)(2,1)S(1)}, u32[]{:S(2)}, u32[]{:S(2)}) %collective-permute-start.3) | collective-permute-done | bytes 131104 | tf_op jit(solution)/shard_map/ppermute | solution.py:217
  12.4 1.4 %collective-permute-start.4 = (bf16[2,1,64,1024]{3,2,1,0:T(8,128)(2,1)S(1)}, bf16[2,1,64,1024]{3,2,1,0:T(8,128)(2,1)S(1)}, u32[]{:S(2)}, u32[]{:S(2)}) collective-permute-start(bf16[2,1,64,1024]{3,2,1,0:T(8,128)(2,1)S(1)} %pad_maximum_fusion), channel_id=1, source_target_pairs={{0,1},{1,0},{2,3},{3,2},{4,5},{5,4},{6,7},{7,6},{8,9},{9,8},{10,11... | collective-permute-start | bytes 786440 | tf_op jit(solution)/shard_map/ppermute | solution.py:197
  13.7 0.1 route.1
  13.8 0.2 collective-permute-start.5
  14.1 1.3 %collective-permute-start.6 = (bf16[64,1024]{1,0:T(8,128)(2,1)S(1)}, bf16[64,1024]{1,0:T(8,128)(2,1)S(1)}, u32[]{:S(2)}, u32[]{:S(2)}) collective-permute-start(bf16[64,1024]{1,0:T(8,128)(2,1)S(1)} %get-tuple-element.57), channel_id=1, source_target_pairs={{0,2},{1,3},{2,0},{3,1},{4,6},{5,7},{6,4},{7,5},{8,10},{9,11},{10,... | collective-permute-start | bytes 393224 | tf_op jit(solution)/shard_map/ppermute | solution.py:197
  15.3 2.1 %collective-permute-start.7 = (bf16[64,1024]{1,0:T(8,128)(2,1)S(1)}, bf16[64,1024]{1,0:T(8,128)(2,1)S(1)}, u32[]{:S(2)}, u32[]{:S(2)}) collective-permute-start(bf16[64,1024]{1,0:T(8,128)(2,1)S(1)} %get-tuple-element.58), channel_id=1, source_target_pairs={{0,3},{1,2},{2,1},{3,0},{4,7},{5,6},{6,5},{7,4},{8,11},{9,10},{10,... | collective-permute-start | bytes 393224 | tf_op jit(solution)/shard_map/ppermute | solution.py:197
  17.4 6.2 %collective-permute-done.5.refs_1_ = bf16[64,1024]{1,0:T(8,128)(2,1)S(1)} collective-permute-done((bf16[64,1024]{1,0:T(8,128)(2,1)S(1)}, bf16[64,1024]{1,0:T(8,128)(2,1)S(1)}, u32[]{:S(2)}, u32[]{:S(2)}) %collective-permute-start.5) | collective-permute-done | bytes 131104 | tf_op jit(solution)/shard_map/ppermute | solution.py:197
  23.7 0.0 collective-permute-done.6.refs_2_
  23.7 4.2 %collective-permute-done.7.refs_3_ = bf16[64,1024]{1,0:T(8,128)(2,1)S(1)} collective-permute-done((bf16[64,1024]{1,0:T(8,128)(2,1)S(1)}, bf16[64,1024]{1,0:T(8,128)(2,1)S(1)}, u32[]{:S(2)}, u32[]{:S(2)}) %collective-permute-start.7) | collective-permute-done | bytes 131104 | tf_op jit(solution)/shard_map/ppermute | solution.py:197
  27.9 0.0 collective-permute-done.4.refs_2_.refs_6_
  27.9 2.7 %collective-permute-start.8 = (bf16[4,64,1024]{2,1,0:T(8,128)(2,1)S(1)}, bf16[4,64,1024]{2,1,0:T(8,128)(2,1)S(1)}, u32[]{:S(2)}, u32[]{:S(2)}) collective-permute-start(bf16[4,64,1024]{2,1,0:T(8,128)(2,1)S(1)} %collect.1.refs_3_), channel_id=1, source_target_pairs={{0,4},{4,0},{8,12},{12,8},{16,20},{20,16},{24,28},{28,24},{1,5},{5... | collective-permute-start | bytes 1572872 | tf_op jit(solution)/shard_map/ppermute | solution.py:220
  30.6 0.0 collective-permute-start.9
  30.6 1.3 %collective-permute-start.11 = (bf16[4,64,1024]{2,1,0:T(8,128)(2,1)S(1)}, bf16[4,64,1024]{2,1,0:T(8,128)(2,1)S(1)}, u32[]{:S(2)}, u32[]{:S(2)}) collective-permute-start(bf16[4,64,1024]{2,1,0:T(8,128)(2,1)S(1)} %collect.1.refs_3_), channel_id=1, source_target_pairs={{0,8},{4,12},{8,0},{12,4},{16,24},{20,28},{24,16},{28,20},{1,9},{5... | collective-permute-start | bytes 1572872 | tf_op jit(solution)/shard_map/ppermute | solution.py:217
  32.0 1.1 %collective-permute-start.12 = (bf16[4,64,1024]{2,1,0:T(8,128)(2,1)S(1)}, bf16[4,64,1024]{2,1,0:T(8,128)(2,1)S(1)}, u32[]{:S(2)}, u32[]{:S(2)}) collective-permute-start(bf16[4,64,1024]{2,1,0:T(8,128)(2,1)S(1)} %collect.1.refs_3_), channel_id=1, source_target_pairs={{0,16},{4,20},{8,24},{12,28},{16,0},{20,4},{24,8},{28,12},{1,17},{... | collective-permute-start | bytes 1572872 | tf_op jit(solution)/shard_map/ppermute | solution.py:217
  33.1 6.5 %collective-permute-done.9.refs_1_ = bf16[1,1,64,1024]{3,2,1,0:T(8,128)(2,1)S(1)} collective-permute-done((bf16[1,1,64,1024]{3,2,1,0:T(8,128)(2,1)S(1)}, bf16[1,1,64,1024]{3,2,1,0:T(8,128)(2,1)S(1)}, u32[]{:S(2)}, u32[]{:S(2)}) %collective-permute-start.9) | collective-permute-done | bytes 131104 | tf_op jit(solution)/shard_map/ppermute | solution.py:197
  39.6 0.0 collective-permute-start.10
  39.6 1.4 %collective-permute-start.16 = (bf16[2,1,64,1024]{3,2,1,0:T(8,128)(2,1)S(1)}, bf16[2,1,64,1024]{3,2,1,0:T(8,128)(2,1)S(1)}, u32[]{:S(2)}, u32[]{:S(2)}) collective-permute-start(bf16[2,1,64,1024]{3,2,1,0:T(8,128)(2,1)S(1)} %pad_maximum_fusion.2), channel_id=1, source_target_pairs={{0,1},{1,0},{2,3},{3,2},{4,5},{5,4},{6,7},{7,6},{8,9},{9,8},{10,11... | collective-permute-start | bytes 786440 | tf_op jit(solution)/shard_map/ppermute | solution.py:197
  41.1 0.0 collective-permute-done.8.refs_7_
  41.1 6.5 %product.5.refs_4_ = f32[2,4,1024,2048]{3,2,1,0:T(8,128)} custom-call(bf16[1,1,64,1024]{3,2,1,0:T(8,128)(2,1)S(1)} %bitcast.6, bf16[1,1,64,1024]{3,2,1,0:T(8,128)(2,1)S(1)} %collective-permute-done.refs_1_.refs_5_, bf16[2,1,64,1024]{3,2,1,0:T(8,128)(2,1)S(1)} %collective-permute-done.4.refs_2_.refs_6_, bf16[4,64,1024]{2,1,0:T(8,128)(2,1)S(1)} %collect.1.refs_3_, ...), custom_call_target="tpu_custom_call" | custom-call | flops 8589934592 | bytes 67108864 | tf_op jit(solution)/shard_map/product/pallas_call | solution.py:175
  47.6 0.0 collective-permute-done.10.refs_5_.refs_1_
  47.6 0.0 collective-permute-done.11.refs_3_
  47.6 0.0 collective-permute-done.12.refs_7_
  47.7 1.1 %collective-permute-start.17 = (bf16[4,64,1024]{2,1,0:T(8,128)(2,1)S(1)}, bf16[4,64,1024]{2,1,0:T(8,128)(2,1)S(1)}, u32[]{:S(2)}, u32[]{:S(2)}) collective-permute-start(bf16[4,64,1024]{2,1,0:T(8,128)(2,1)S(1)} %collective-permute-done.11.refs_3_), channel_id=1, source_target_pairs={{0,4},{4,0},{8,12},{12,8},{16,20},{20,16},{24,28},{28,24},{1,5},{5... | collective-permute-start | bytes 1572872 | tf_op jit(solution)/shard_map/ppermute | solution.py:220
  48.7 0.2 collective-permute-start.18
  49.0 1.3 %collective-permute-start.15 = (bf16[4,64,1024]{2,1,0:T(8,128)(2,1)S(1)}, bf16[4,64,1024]{2,1,0:T(8,128)(2,1)S(1)}, u32[]{:S(2)}, u32[]{:S(2)}) collective-permute-start(bf16[4,64,1024]{2,1,0:T(8,128)(2,1)S(1)} %collective-permute-done.12.refs_7_), channel_id=1, source_target_pairs={{0,8},{4,12},{8,0},{12,4},{16,24},{20,28},{24,16},{28,20},{1,9},{5... | collective-permute-start | bytes 1572872 | tf_op jit(solution)/shard_map/ppermute | solution.py:217
  50.3 2.4 %collective-permute-start.13 = (bf16[1,1,64,1024]{3,2,1,0:T(8,128)(2,1)S(1)}, bf16[1,1,64,1024]{3,2,1,0:T(8,128)(2,1)S(1)}, u32[]{:S(2)}, u32[]{:S(2)}) collective-permute-start(bf16[1,1,64,1024]{3,2,1,0:T(8,128)(2,1)S(1)} %bitcast.8), channel_id=1, source_target_pairs={{0,2},{1,3},{2,0},{3,1},{4,6},{5,7},{6,4},{7,5},{8,10},{9,11},{10,... | collective-permute-start | bytes 393224 | tf_op jit(solution)/shard_map/ppermute | solution.py:197
  52.7 0.0 collective-permute-done.16.refs_2_
  52.7 4.0 %product.6.refs_8_ = f32[2,4,1024,2048]{3,2,1,0:T(8,128)} custom-call(bf16[1,1,64,1024]{3,2,1,0:T(8,128)(2,1)S(1)} %bitcast.18, bf16[1,1,64,1024]{3,2,1,0:T(8,128)(2,1)S(1)} %collective-permute-done.9.refs_1_, bf16[2,1,64,1024]{3,2,1,0:T(8,128)(2,1)S(1)} %collective-permute-done.16.refs_2_, ...), custom_call_target="tpu_custom_call", output_to_operand_aliasing={{}: (4, {})} | custom-call | flops 4294967296 | bytes 33554432 | tf_op jit(solution)/shard_map/product/pallas_call | solution.py:175
  56.7 0.9 %collective-permute-start.20 = (bf16[4,64,1024]{2,1,0:T(8,128)(2,1)S(1)}, bf16[4,64,1024]{2,1,0:T(8,128)(2,1)S(1)}, u32[]{:S(2)}, u32[]{:S(2)}) collective-permute-start(bf16[4,64,1024]{2,1,0:T(8,128)(2,1)S(1)} %collective-permute-done.12.refs_7_), channel_id=1, source_target_pairs={{0,4},{4,0},{8,12},{12,8},{16,20},{20,16},{24,28},{28,24},{1,5},{5... | collective-permute-start | bytes 1572872 | tf_op jit(solution)/shard_map/ppermute | solution.py:220
  57.6 0.0 collective-permute-done.13.refs_5_.refs_1_
  57.7 3.2 %collective-permute-start.14 = (bf16[2,1,64,1024]{3,2,1,0:T(8,128)(2,1)S(1)}, bf16[2,1,64,1024]{3,2,1,0:T(8,128)(2,1)S(1)}, u32[]{:S(2)}, u32[]{:S(2)}) collective-permute-start(bf16[2,1,64,1024]{3,2,1,0:T(8,128)(2,1)S(1)} %pad_maximum_fusion.1), channel_id=1, source_target_pairs={{0,1},{1,0},{2,3},{3,2},{4,5},{5,4},{6,7},{7,6},{8,9},{9,8},{10,11... | collective-permute-start | bytes 786440 | tf_op jit(solution)/shard_map/ppermute | solution.py:197
  60.8 0.0 collective-permute-done.18.refs_6_.refs_2_
  60.8 0.0 collective-permute-done.17.refs_3_
  60.8 6.5 %product.7.refs_8_ = f32[2,4,1024,2048]{3,2,1,0:T(8,128)} custom-call(bf16[1,1,64,1024]{3,2,1,0:T(8,128)(2,1)S(1)} %bitcast.19, bf16[1,1,64,1024]{3,2,1,0:T(8,128)(2,1)S(1)} %collective-permute-done.9.refs_1_, bf16[2,1,64,1024]{3,2,1,0:T(8,128)(2,1)S(1)} %collective-permute-done.16.refs_2_, ...), custom_call_target="tpu_custom_call", output_to_operand_aliasing={{}: (8, {})} | custom-call | flops 8589934592 | bytes 67108864 | tf_op jit(solution)/shard_map/product/pallas_call | solution.py:175
  67.3 0.0 collective-permute-done.15.refs_7_
  67.4 1.0 %collective-permute-start.19 = (bf16[4,64,1024]{2,1,0:T(8,128)(2,1)S(1)}, bf16[4,64,1024]{2,1,0:T(8,128)(2,1)S(1)}, u32[]{:S(2)}, u32[]{:S(2)}) collective-permute-start(bf16[4,64,1024]{2,1,0:T(8,128)(2,1)S(1)} %collective-permute-done.15.refs_7_), channel_id=1, source_target_pairs={{0,4},{4,0},{8,12},{12,8},{16,20},{20,16},{24,28},{28,24},{1,5},{5... | collective-permute-start | bytes 1572872 | tf_op jit(solution)/shard_map/ppermute | solution.py:220
  68.3 0.0 collective-permute-done.14.refs_6_.refs_2_
  68.3 0.0 collective-permute-done.20.refs_3_
  68.3 6.5 %product.8.refs_4_ = f32[2,4,1024,2048]{3,2,1,0:T(8,128)} custom-call(bf16[1,1,64,1024]{3,2,1,0:T(8,128)(2,1)S(1)} %bitcast.15, bf16[1,1,64,1024]{3,2,1,0:T(8,128)(2,1)S(1)} %collective-permute-done.10.refs_5_.refs_1_, bf16[2,1,64,1024]{3,2,1,0:T(8,128)(2,1)S(1)} %collective-permute-done.18.refs_6_.refs_2_, ...), custom_call_target="tpu_custom_call", output_to_operand_aliasing={{}: (8, {})} | custom-call | flops 8589934592 | bytes 67108864 | tf_op jit(solution)/shard_map/product/pallas_call | solution.py:175
  74.9 0.0 collective-permute-done.19.refs_3_
  74.9 4.0 %product.9 = f32[2,4,1024,2048]{3,2,1,0:T(8,128)} custom-call(bf16[1,1,64,1024]{3,2,1,0:T(8,128)(2,1)S(1)} %bitcast.11, bf16[1,1,64,1024]{3,2,1,0:T(8,128)(2,1)S(1)} %collective-permute-done.13.refs_5_.refs_1_, bf16[2,1,64,1024]{3,2,1,0:T(8,128)(2,1)S(1)} %collective-permute-done.14.refs_6_.refs_2_, ...), custom_call_target="tpu_custom_call", output_to_operand_aliasing={{}: (4, {})} | custom-call | flops 4294967296 | bytes 33554432 | tf_op jit(solution)/shard_map/product/pallas_call | solution.py:175
  (5 shorter events, 0.1 us)
Async XLA Ops:
  0.0 1.0 %copy-start = (bf16[2,4,32,1024]{3,2,1,0:T(8,128)(2,1)S(1)}, bf16[2,4,32,1024]{3,2,1,0:T(8,128)(2,1)}, u32[]{:S(2)}) copy-start(bf16[2,4,32,1024]{3,2,1,0:T(8,128)(2,1)} %raw.1) | copy-start | bytes 1572868
  1.5 9.2 %collective-permute-start = (bf16[1,1,64,1024]{3,2,1,0:T(8,128)(2,1)S(1)}, bf16[1,1,64,1024]{3,2,1,0:T(8,128)(2,1)S(1)}, u32[]{:S(2)}, u32[]{:S(2)}) collective-permute-start(bf16[1,1,64,1024]{3,2,1,0:T(8,128)(2,1)S(1)} %bitcast.4), channel_id=1, source_target_pairs={{0,2},{1,3},{2,0},{3,1},{4,6},{5,7},{6,4},{7,5},{8,10},{9,11},{10,... | collective-permute-start | bytes 393224 | tf_op jit(solution)/shard_map/ppermute | solution.py:197
  4.7 6.0 %collective-permute-start.1 = (bf16[64,1024]{1,0:T(8,128)(2,1)S(1)}, bf16[64,1024]{1,0:T(8,128)(2,1)S(1)}, u32[]{:S(2)}, u32[]{:S(2)}) collective-permute-start(bf16[64,1024]{1,0:T(8,128)(2,1)S(1)} %get-tuple-element.47), channel_id=1, source_target_pairs={{0,8},{4,12},{8,0},{12,4},{16,24},{20,28},{24,16},{28,20},{1,9},{5... | collective-permute-start | bytes 393224 | tf_op jit(solution)/shard_map/ppermute | solution.py:217
  5.9 4.8 %collective-permute-start.2 = (bf16[64,1024]{1,0:T(8,128)(2,1)S(1)}, bf16[64,1024]{1,0:T(8,128)(2,1)S(1)}, u32[]{:S(2)}, u32[]{:S(2)}) collective-permute-start(bf16[64,1024]{1,0:T(8,128)(2,1)S(1)} %get-tuple-element.48), channel_id=1, source_target_pairs={{0,16},{4,20},{8,24},{12,28},{16,0},{20,4},{24,8},{28,12},{1,17},{... | collective-permute-start | bytes 393224 | tf_op jit(solution)/shard_map/ppermute | solution.py:217
  7.1 5.2 %collective-permute-start.3 = (bf16[64,1024]{1,0:T(8,128)(2,1)S(1)}, bf16[64,1024]{1,0:T(8,128)(2,1)S(1)}, u32[]{:S(2)}, u32[]{:S(2)}) collective-permute-start(bf16[64,1024]{1,0:T(8,128)(2,1)S(1)} %get-tuple-element.49), channel_id=1, source_target_pairs={{0,24},{4,28},{8,16},{12,20},{16,8},{20,12},{24,0},{28,4},{1,25},{... | collective-permute-start | bytes 393224 | tf_op jit(solution)/shard_map/ppermute | solution.py:217
  12.4 15.5 %collective-permute-start.4 = (bf16[2,1,64,1024]{3,2,1,0:T(8,128)(2,1)S(1)}, bf16[2,1,64,1024]{3,2,1,0:T(8,128)(2,1)S(1)}, u32[]{:S(2)}, u32[]{:S(2)}) collective-permute-start(bf16[2,1,64,1024]{3,2,1,0:T(8,128)(2,1)S(1)} %pad_maximum_fusion), channel_id=1, source_target_pairs={{0,1},{1,0},{2,3},{3,2},{4,5},{5,4},{6,7},{7,6},{8,9},{9,8},{10,11... | collective-permute-start | bytes 786440 | tf_op jit(solution)/shard_map/ppermute | solution.py:197
  13.8 9.9 %collective-permute-start.5 = (bf16[64,1024]{1,0:T(8,128)(2,1)S(1)}, bf16[64,1024]{1,0:T(8,128)(2,1)S(1)}, u32[]{:S(2)}, u32[]{:S(2)}) collective-permute-start(bf16[64,1024]{1,0:T(8,128)(2,1)S(1)} %get-tuple-element.56), channel_id=1, source_target_pairs={{0,1},{1,0},{2,3},{3,2},{4,5},{5,4},{6,7},{7,6},{8,9},{9,8},{10,11... | collective-permute-start | bytes 393224 | tf_op jit(solution)/shard_map/ppermute | solution.py:197
  14.1 9.6 %collective-permute-start.6 = (bf16[64,1024]{1,0:T(8,128)(2,1)S(1)}, bf16[64,1024]{1,0:T(8,128)(2,1)S(1)}, u32[]{:S(2)}, u32[]{:S(2)}) collective-permute-start(bf16[64,1024]{1,0:T(8,128)(2,1)S(1)} %get-tuple-element.57), channel_id=1, source_target_pairs={{0,2},{1,3},{2,0},{3,1},{4,6},{5,7},{6,4},{7,5},{8,10},{9,11},{10,... | collective-permute-start | bytes 393224 | tf_op jit(solution)/shard_map/ppermute | solution.py:197
  15.3 12.5 %collective-permute-start.7 = (bf16[64,1024]{1,0:T(8,128)(2,1)S(1)}, bf16[64,1024]{1,0:T(8,128)(2,1)S(1)}, u32[]{:S(2)}, u32[]{:S(2)}) collective-permute-start(bf16[64,1024]{1,0:T(8,128)(2,1)S(1)} %get-tuple-element.58), channel_id=1, source_target_pairs={{0,3},{1,2},{2,1},{3,0},{4,7},{5,6},{6,5},{7,4},{8,11},{9,10},{10,... | collective-permute-start | bytes 393224 | tf_op jit(solution)/shard_map/ppermute | solution.py:197
  27.9 13.2 %collective-permute-start.8 = (bf16[4,64,1024]{2,1,0:T(8,128)(2,1)S(1)}, bf16[4,64,1024]{2,1,0:T(8,128)(2,1)S(1)}, u32[]{:S(2)}, u32[]{:S(2)}) collective-permute-start(bf16[4,64,1024]{2,1,0:T(8,128)(2,1)S(1)} %collect.1.refs_3_), channel_id=1, source_target_pairs={{0,4},{4,0},{8,12},{12,8},{16,20},{20,16},{24,28},{28,24},{1,5},{5... | collective-permute-start | bytes 1572872 | tf_op jit(solution)/shard_map/ppermute | solution.py:220
  30.6 9.0 %collective-permute-start.9 = (bf16[1,1,64,1024]{3,2,1,0:T(8,128)(2,1)S(1)}, bf16[1,1,64,1024]{3,2,1,0:T(8,128)(2,1)S(1)}, u32[]{:S(2)}, u32[]{:S(2)}) collective-permute-start(bf16[1,1,64,1024]{3,2,1,0:T(8,128)(2,1)S(1)} %bitcast.16), channel_id=1, source_target_pairs={{0,2},{1,3},{2,0},{3,1},{4,6},{5,7},{6,4},{7,5},{8,10},{9,11},{10,... | collective-permute-start | bytes 393224 | tf_op jit(solution)/shard_map/ppermute | solution.py:197
  30.6 17.0 %collective-permute-start.11 = (bf16[4,64,1024]{2,1,0:T(8,128)(2,1)S(1)}, bf16[4,64,1024]{2,1,0:T(8,128)(2,1)S(1)}, u32[]{:S(2)}, u32[]{:S(2)}) collective-permute-start(bf16[4,64,1024]{2,1,0:T(8,128)(2,1)S(1)} %collect.1.refs_3_), channel_id=1, source_target_pairs={{0,8},{4,12},{8,0},{12,4},{16,24},{20,28},{24,16},{28,20},{1,9},{5... | collective-permute-start | bytes 1572872 | tf_op jit(solution)/shard_map/ppermute | solution.py:217
  32.0 15.7 %collective-permute-start.12 = (bf16[4,64,1024]{2,1,0:T(8,128)(2,1)S(1)}, bf16[4,64,1024]{2,1,0:T(8,128)(2,1)S(1)}, u32[]{:S(2)}, u32[]{:S(2)}) collective-permute-start(bf16[4,64,1024]{2,1,0:T(8,128)(2,1)S(1)} %collect.1.refs_3_), channel_id=1, source_target_pairs={{0,16},{4,20},{8,24},{12,28},{16,0},{20,4},{24,8},{28,12},{1,17},{... | collective-permute-start | bytes 1572872 | tf_op jit(solution)/shard_map/ppermute | solution.py:217
  39.6 8.0 %collective-permute-start.10 = (bf16[1,1,64,1024]{3,2,1,0:T(8,128)(2,1)S(1)}, bf16[1,1,64,1024]{3,2,1,0:T(8,128)(2,1)S(1)}, u32[]{:S(2)}, u32[]{:S(2)}) collective-permute-start(bf16[1,1,64,1024]{3,2,1,0:T(8,128)(2,1)S(1)} %bitcast.12), channel_id=1, source_target_pairs={{0,2},{1,3},{2,0},{3,1},{4,6},{5,7},{6,4},{7,5},{8,10},{9,11},{10,... | collective-permute-start | bytes 393224 | tf_op jit(solution)/shard_map/ppermute | solution.py:197
  39.6 13.0 %collective-permute-start.16 = (bf16[2,1,64,1024]{3,2,1,0:T(8,128)(2,1)S(1)}, bf16[2,1,64,1024]{3,2,1,0:T(8,128)(2,1)S(1)}, u32[]{:S(2)}, u32[]{:S(2)}) collective-permute-start(bf16[2,1,64,1024]{3,2,1,0:T(8,128)(2,1)S(1)} %pad_maximum_fusion.2), channel_id=1, source_target_pairs={{0,1},{1,0},{2,3},{3,2},{4,5},{5,4},{6,7},{7,6},{8,9},{9,8},{10,11... | collective-permute-start | bytes 786440 | tf_op jit(solution)/shard_map/ppermute | solution.py:197
  47.7 13.2 %collective-permute-start.17 = (bf16[4,64,1024]{2,1,0:T(8,128)(2,1)S(1)}, bf16[4,64,1024]{2,1,0:T(8,128)(2,1)S(1)}, u32[]{:S(2)}, u32[]{:S(2)}) collective-permute-start(bf16[4,64,1024]{2,1,0:T(8,128)(2,1)S(1)} %collective-permute-done.11.refs_3_), channel_id=1, source_target_pairs={{0,4},{4,0},{8,12},{12,8},{16,20},{20,16},{24,28},{28,24},{1,5},{5... | collective-permute-start | bytes 1572872 | tf_op jit(solution)/shard_map/ppermute | solution.py:220
  48.7 12.1 %collective-permute-start.18 = (bf16[2,1,64,1024]{3,2,1,0:T(8,128)(2,1)S(1)}, bf16[2,1,64,1024]{3,2,1,0:T(8,128)(2,1)S(1)}, u32[]{:S(2)}, u32[]{:S(2)}) collective-permute-start(bf16[2,1,64,1024]{3,2,1,0:T(8,128)(2,1)S(1)} %pad_maximum_fusion.3), channel_id=1, source_target_pairs={{0,1},{1,0},{2,3},{3,2},{4,5},{5,4},{6,7},{7,6},{8,9},{9,8},{10,11... | collective-permute-start | bytes 786440 | tf_op jit(solution)/shard_map/ppermute | solution.py:197
  49.0 18.4 %collective-permute-start.15 = (bf16[4,64,1024]{2,1,0:T(8,128)(2,1)S(1)}, bf16[4,64,1024]{2,1,0:T(8,128)(2,1)S(1)}, u32[]{:S(2)}, u32[]{:S(2)}) collective-permute-start(bf16[4,64,1024]{2,1,0:T(8,128)(2,1)S(1)} %collective-permute-done.12.refs_7_), channel_id=1, source_target_pairs={{0,8},{4,12},{8,0},{12,4},{16,24},{20,28},{24,16},{28,20},{1,9},{5... | collective-permute-start | bytes 1572872 | tf_op jit(solution)/shard_map/ppermute | solution.py:217
  50.3 7.4 %collective-permute-start.13 = (bf16[1,1,64,1024]{3,2,1,0:T(8,128)(2,1)S(1)}, bf16[1,1,64,1024]{3,2,1,0:T(8,128)(2,1)S(1)}, u32[]{:S(2)}, u32[]{:S(2)}) collective-permute-start(bf16[1,1,64,1024]{3,2,1,0:T(8,128)(2,1)S(1)} %bitcast.8), channel_id=1, source_target_pairs={{0,2},{1,3},{2,0},{3,1},{4,6},{5,7},{6,4},{7,5},{8,10},{9,11},{10,... | collective-permute-start | bytes 393224 | tf_op jit(solution)/shard_map/ppermute | solution.py:197
  56.7 11.6 %collective-permute-start.20 = (bf16[4,64,1024]{2,1,0:T(8,128)(2,1)S(1)}, bf16[4,64,1024]{2,1,0:T(8,128)(2,1)S(1)}, u32[]{:S(2)}, u32[]{:S(2)}) collective-permute-start(bf16[4,64,1024]{2,1,0:T(8,128)(2,1)S(1)} %collective-permute-done.12.refs_7_), channel_id=1, source_target_pairs={{0,4},{4,0},{8,12},{12,8},{16,20},{20,16},{24,28},{28,24},{1,5},{5... | collective-permute-start | bytes 1572872 | tf_op jit(solution)/shard_map/ppermute | solution.py:220
  57.7 10.7 %collective-permute-start.14 = (bf16[2,1,64,1024]{3,2,1,0:T(8,128)(2,1)S(1)}, bf16[2,1,64,1024]{3,2,1,0:T(8,128)(2,1)S(1)}, u32[]{:S(2)}, u32[]{:S(2)}) collective-permute-start(bf16[2,1,64,1024]{3,2,1,0:T(8,128)(2,1)S(1)} %pad_maximum_fusion.1), channel_id=1, source_target_pairs={{0,1},{1,0},{2,3},{3,2},{4,5},{5,4},{6,7},{7,6},{8,9},{9,8},{10,11... | collective-permute-start | bytes 786440 | tf_op jit(solution)/shard_map/ppermute | solution.py:197
  67.4 7.5 %collective-permute-start.19 = (bf16[4,64,1024]{2,1,0:T(8,128)(2,1)S(1)}, bf16[4,64,1024]{2,1,0:T(8,128)(2,1)S(1)}, u32[]{:S(2)}, u32[]{:S(2)}) collective-permute-start(bf16[4,64,1024]{2,1,0:T(8,128)(2,1)S(1)} %collective-permute-done.15.refs_7_), channel_id=1, source_target_pairs={{0,4},{4,0},{8,12},{12,8},{16,20},{20,16},{24,28},{28,24},{1,5},{5... | collective-permute-start | bytes 1572872 | tf_op jit(solution)/shard_map/ppermute | solution.py:220

commit v4 on v2

v4 whole, which is shorter than its diff:
```python
import functools
import math

import jax
import jax.numpy as jnp
from jax import lax
from jax.experimental import pallas as pl
from jax.experimental.pallas import tpu as pltpu
from jax.sharding import PartitionSpec as P


def whiten_kernel(n, n_split, steps, raw, *refs):
    n_bins, width = raw.shape[1], raw.shape[2]
    row_outs, piece_outs, held = refs[: len(steps)], refs[len(steps) : -1], refs[-1]
    q = lax.axis_index("row") // 2
    real = [raw[0, f].astype(jnp.float32) for f in range(n_bins)]
    imag = [raw[1, f].astype(jnp.float32) for f in range(n_bins)]
    magnitude = [jnp.sqrt(a * a + b * b) for a, b in zip(real, imag)]
    part = held.shape[1]
    rows = min(part, width)
    for f in range(n_bins):
        near = [magnitude[g] for g in (f, f + 1, f - 1) if 0 <= g < n_bins]
        level = jnp.maximum(sum(near[1:], near[0]) / float(len(near)), 0.75)
        for p, values in ((0, real[f]), (1, imag[f])):
            white = (values / level).astype(jnp.bfloat16)
            for at in range(0, width, rows):
                piece, start = divmod(p * width + at, part)
                held[f * n_split + piece, start : start + rows] = white[at : at + rows]
    for chunk, out in zip(steps, row_outs):
        for i, step in enumerate(chunk):
            for s in range(n_split):
                out[0, i, s] = held[((q // n_split) ^ step) * n_split + s]
    for d, out in enumerate(piece_outs):
        out[...] = held[q ^ d]


def whiten(raw, n, n_split, steps):
    _, n_bins, width, channels = raw.shape
    part = 2 * width // n_split
    shapes = [(1, len(chunk), n_split, part, channels) for chunk in steps] + [(part, channels)] * n
    outs = pl.pallas_call(
        functools.partial(whiten_kernel, n, n_split, steps),
        out_shape=[jax.ShapeDtypeStruct(shape, jnp.bfloat16) for shape in shapes],
        in_specs=[pl.BlockSpec(memory_space=pltpu.VMEM)],
        out_specs=[pl.BlockSpec(memory_space=pltpu.VMEM)] * len(shapes),
        scratch_shapes=[pltpu.VMEM((n, part, channels), jnp.bfloat16)],
        compiler_params=pltpu.CompilerParams(vmem_limit_bytes=24 << 20),
        name="whiten",
    )(raw)
    return outs[: len(steps)], outs[len(steps) :]


def route_kernel(*refs):
    n = len(refs) // 2
    blocks, outs = refs[:n], refs[n:]
    q, z = lax.axis_index("row") // 2, lax.axis_index("col")
    for e, out in enumerate(outs):
        wanted = q ^ z ^ e
        for d, block in enumerate(blocks):

            @pl.when(wanted == d)
            def _(block=block, out=out):
                out[...] = block[...]


def route(blocks):
    n = len(blocks)
    shape = jax.ShapeDtypeStruct(blocks[0].shape, jnp.bfloat16)
    return pl.pallas_call(
        route_kernel,
        out_shape=[shape] * n,
        in_specs=[pl.BlockSpec(memory_space=pltpu.VMEM)] * n,
        out_specs=[pl.BlockSpec(memory_space=pltpu.VMEM)] * n,
        compiler_params=pltpu.CompilerParams(vmem_limit_bytes=24 << 20),
        name="route",
    )(*blocks)


def collect_kernel(*refs):
    z = lax.axis_index("col")
    for e, x in enumerate(refs[:-1]):
        refs[-1][z ^ e] = x[...]


def collect(parts):
    return pl.pallas_call(
        collect_kernel,
        out_shape=jax.ShapeDtypeStruct((len(parts), *parts[0].shape), jnp.bfloat16),
        in_specs=[pl.BlockSpec(memory_space=pltpu.VMEM)] * len(parts),
        out_specs=pl.BlockSpec(memory_space=pltpu.VMEM),
        compiler_params=pltpu.CompilerParams(vmem_limit_bytes=24 << 20),
        name="collect",
    )(*parts)


def turn_kernel(at, n, n_split, *refs):
    q = lax.axis_index("row") // 2
    out = refs[-1]
    where, bit = {0: (0, 0)}, n
    for ref in range(1, len(refs) - 1):
        bit //= 2
        for place, d in enumerate(list(where)):
            where[d ^ bit] = (ref, place)
    picked = []
    for s in range(n_split):
        for d in range(n):
            ref, place = where[d]
            own = s ^ (q % n_split)
            picked.append(refs[ref][place, at, own] if ref < 2 else refs[ref][place, own])
    out[...] = jnp.concatenate(picked, axis=0).T


def turn(at, parts, n):
    _, _, n_split, part, channels = parts[0].shape
    return pl.pallas_call(
        functools.partial(turn_kernel, at, n, n_split),
        out_shape=jax.ShapeDtypeStruct((channels, n * n_split * part), jnp.bfloat16),
        in_specs=[pl.BlockSpec(memory_space=pltpu.VMEM)] * len(parts),
        out_specs=pl.BlockSpec(memory_space=pltpu.VMEM),
        compiler_params=pltpu.CompilerParams(vmem_limit_bytes=24 << 20),
        name="turn",
    )(*parts)


def product_kernel(items, n, n_split, tile, norm, *refs):
    operands = [refs[at * (n_split + 1) : (at + 1) * (n_split + 1)] for at in range(len(items))]
    out, made, out_sem = refs[-3:]
    q, k, z = lax.axis_index("row") // 2, lax.axis_index("row") % 2, lax.axis_index("col")
    channels = operands[0][0].shape[0]
    part = operands[0][1].shape[1]
    slots, _, height, width = made.shape
    per_column = channels // height
    n_tiles = per_column * (channels // width)
    pairs = [(s, d) for s in range(n_split) for d in range(n)]

    def store(item, at):
        step, other = items[item]
        block = 1 - k if other else k
        top = pl.multiple_of(at % per_column * height, height)
        start = pl.multiple_of(block * channels + at // per_column * width, width)
        slot = (item * n_tiles + at) % slots
        return pltpu.make_async_copy(
            made.at[slot],
            out.at[:, (q // n_split) ^ step, pl.ds(top, height), pl.ds(start, width)],
            out_sem.at[slot],
        )

    def one_tile(item, turned, columns, at):
        total = item * n_tiles + at

        @pl.when(total >= slots)
        def _():
            store(item, at).wait()

        left = turned[pl.ds(pl.multiple_of(at % per_column * height, height), height)]
        start = pl.multiple_of(at // per_column * width, width)
        piece = lambda s, d: columns[s][z ^ d, :, pl.ds(start, width)]
        right = jnp.concatenate([piece(s, d) for s, d in pairs], axis=0)
        made[total % slots, 0] = norm * jnp.dot(left, right, preferred_element_type=jnp.float32)
        half = part // 2 if n_split == 1 else n_split // 2
        crossed = []
        for s, d in pairs:
            if n_split == 1:
                values = piece(s, d)
                crossed += [-values[half:], values[:half]]
            else:
                sign = jnp.where((s ^ (q % n_split)) < half, -1.0, 1.0).astype(jnp.bfloat16)
                crossed.append(piece(s ^ half, d) * sign)
        right = jnp.concatenate(crossed, axis=0)
        made[total % slots, 1] = norm * jnp.dot(left, right, preferred_element_type=jnp.float32)
        store(item, at).start()

    for item, (turned, *columns) in enumerate(operands):
        lax.fori_loop(0, n_tiles, lambda at, _: one_tile(item, turned, columns, at), None)
    total = len(items) * n_tiles
    for at in range(max(0, total - slots), total):
        store(at // n_tiles, at % n_tiles).wait()


def product(items, turned, columns, before, n, n_split, n_bins):
    channels, depth = turned[0].shape
    width, height = min(256, channels), min(512, channels)
    slots = min(8, len(items) * (channels // width) * (channels // height))
    operands = [x for left, right in zip(turned, columns) for x in (left, *right)]
    specs = [pl.BlockSpec(memory_space=pltpu.VMEM)] * len(operands)
    aliases = {}
    if before is not None:
        aliases = {len(operands): 0}
        operands.append(before)
        specs.append(pl.BlockSpec(memory_space=pl.ANY))
    norm = 1.0 / math.sqrt(depth // 2)
    return pl.pallas_call(
        functools.partial(product_kernel, items, n, n_split, width, norm),
        out_shape=jax.ShapeDtypeStruct((2, n_bins, channels, 2 * channels), jnp.float32),
        in_specs=specs,
        out_specs=pl.BlockSpec(memory_space=pl.ANY),
        scratch_shapes=[
            pltpu.VMEM((slots, 2, height, width), jnp.float32),
            pltpu.SemaphoreType.DMA((slots,)),
        ],
        input_output_aliases=aliases,
        cost_estimate=pl.CostEstimate(
            flops=len(items) * 4 * channels * channels * depth // 4,
            bytes_accessed=len(items) * 8 * channels * channels // 4,
            transcendentals=0,
        ),
        compiler_params=pltpu.CompilerParams(vmem_limit_bytes=32 << 20),
        name="product",
    )(*operands)


def shards(spectra):
    n = lax.axis_size("col")
    n_bins = spectra.shape[1]
    assert lax.axis_size("row") == 2 * n and n % n_bins == 0 and n_bins > 1 and n & (n - 1) == 0
    n_split = n // n_bins
    chunks = [(0, 1)] + [(f,) for f in range(2, n_bins)]
    place = [(at, i) for at, chunk in enumerate(chunks) for i in range(len(chunk))]
    rows, pieces = whiten(spectra, n, n_split, chunks)

    def along_line(values, bit):
        return lax.ppermute(values, "col", [(z, z ^ bit) for z in range(n)])

    def from_chip(values, d):
        return lax.ppermute(values, "row", [(2 * q + k, 2 * (q ^ d) + k) for q in range(n) for k in range(2)])

    def from_core(values):
        return lax.ppermute(values, "row", [(r, r ^ 1) for r in range(2 * n)])

    def gather_rows(own, first, at):
        parts, bit = [own[:, at], first[:, at]], n // 4
        while bit:
            parts.append(along_line(jnp.concatenate(parts), bit))
            bit //= 2
        return [own, first, *parts[2:]]

    def wait(values, done):
        return lax.optimization_barrier((values, done))

    def gather_bin(f):
        at, i = place[f]
        return gather_rows(rows[at], firsts[at], i)

    firsts = [along_line(rows[0], n // 2)]
    blocks = [from_chip(piece, d) if d else piece for d, piece in enumerate(pieces)]
    firsts, blocks = wait(firsts, blocks)
    arrived = [along_line(x, e) if e else x for e, x in enumerate(route(blocks))]
    parts = [gather_bin(0)]
    (rows, firsts, parts), arrived = wait((rows, firsts, parts), arrived)
    near = [collect(arrived)]
    for d in range(1, n):
        low = d & -d
        near.append(from_chip(near[d ^ low], low) if d == low or d < n_split else None)
    far = [from_core(x) for x in near[:n_split]]
    parts.append(gather_bin(1))
    firsts += [along_line(x, n // 2) for x in rows[1:2]]

    call = functools.partial(product, n=n, n_split=n_split, n_bins=n_bins)
    of_bin = lambda x, f: x[f * n_split : (f + 1) * n_split]
    turned = turn(0, parts[0], n)
    out = call([(0, False), (0, True)], [turned] * 2, [of_bin(near, 0), far], None)
    near[n_split:], out = wait(near[n_split:], out)
    for d in range(n_split, n):
        low = d & -d
        if near[d] is None:
            near[d] = from_chip(near[d ^ low], low)
    for f in range(1, n_bins):
        needed = (parts[f], firsts, rows, of_bin(near, f))
        (parts[f], firsts, rows, mine), out = wait(needed, out)
        turned = turn(place[f][1], parts[f], n)
        if f + 1 < n_bins:
            parts.append(gather_bin(f + 1))
        if f + 2 < n_bins:
            firsts.append(along_line(rows[f + 1], n // 2))
        if f in (1, n_bins - 1):
            far = [from_core(x) for x in mine]
            out = call([(f, False)], [turned], [mine], out)
            (far, later), out = wait((far, of_bin(near, f + 1) if f == 1 else []), out)
            following = [from_core(x) for x in later]
            out = call([(f, True)], [turned], [far], out)
        else:
            (far, later), out = wait((following, of_bin(near, f + 1) if f + 2 < n_bins else []), out)
            following = [from_core(x) for x in later]
            out = call([(f, False), (f, True)], [turned] * 2, [mine, far], out)
    return out


def solution(mesh):
    in_specs = (P(None, None, "col", "row"),)
    out_specs = P(None, None, "row", "col")
    return jax.shard_map(shards, mesh=mesh, in_specs=in_specs, out_specs=out_specs, check_vma=False)
```

time: 82.1 us -> 81 us (0.987)
  starting transfers between devices: 30.4 us -> 22.7 us
  waiting for transfers between devices: 22.1 us -> 28.1 us
    ppermute x6, waiting for transfers between devices: 0.02 us -> 8.84 us  [from_chip(): lax.ppermute(values, 'row', [(2 * q + k, 2 * (q ^ d) + k) for q in range(...]
    ppermute x4, starting transfers between devices: 9.05 us -> 4.58 us  [from_core(): return lax.ppermute(values, 'row', [(r, r ^ 1) for r in range(2 * n)])]
    ppermute x11 -> x10, waiting for transfers between devices: 22.1 us -> 19.3 us  [along_line(): return lax.ppermute(values, 'col', [(z, z ^ bit) for z in range(n)])]
    ppermute x11 -> x10, starting transfers between devices: 15 us -> 12.7 us  [along_line(): return lax.ppermute(values, 'col', [(z, z ^ bit) for z in range(n)])]
    ppermute x6, starting transfers between devices: 6.36 us -> 5.43 us  [from_chip(): lax.ppermute(values, 'row', [(2 * q + k, 2 * (q ^ d) + k) for q in range(...]
    pallas_call x5 -> x10, Pallas kernels: 27.6 us -> 28 us  [the longest x6 27.2 us: product(): pl.pallas_call(functools.partial(product_kernel, items, n, n_split, width...]
  transfers between devices with their start and end apart: 21 -> 20, of which waited for: 6 -> 9; matrix products, arithmetic and copies ran while one was open for 0% -> 0% of each run, Pallas kernels for 29% -> 30%
where the time goes in v4:
time: 81 us; the launch traced here: 80.8 us
  Pallas kernels  28.6 us (35%)
  waiting for transfers between devices  28.1 us (35%)
  starting transfers between devices  22.7 us (28%)
  local copies, waits for them, and re-layouts  1.08 us (1%)
    pallas_call x6, Pallas kernels, product(): pl.pallas_call(functools.partial(product_kernel, items, n, n_split, width...  27.2 us
    ppermute x10, waiting for transfers between devices, along_line(): return lax.ppermute(values, 'col', [(z, z ^ bit) for z in range(n)])  19.3 us
    ppermute x10, starting transfers between devices, along_line(): return lax.ppermute(values, 'col', [(z, z ^ bit) for z in range(n)])  12.7 us
    ppermute x6, waiting for transfers between devices, from_chip(): lax.ppermute(values, 'row', [(2 * q + k, 2 * (q ^ d) + k) for q in range(...  8.84 us
    ppermute x6, starting transfers between devices, from_chip(): lax.ppermute(values, 'row', [(2 * q + k, 2 * (q ^ d) + k) for q in range(...  5.43 us
    ppermute x4, starting transfers between devices, from_core(): return lax.ppermute(values, 'row', [(r, r ^ 1) for r in range(2 * n)])  4.58 us
  transfers between devices with their start and end apart: 20, of which 9 were waited for; matrix products, arithmetic and copies ran while one was open for 0% of the time, Pallas kernels for 30%

profile of v4, /device:TPU:1, one launch (start us, length us, event | category | flops | bytes accessed | tf_op | source)
XLA Modules:
  0.0 80.8 jit_solution(2912104430616706073)
XLA Ops:
  0.0 0.0 copy-start
  0.0 1.0 %copy-done = bf16[2,4,32,1024]{3,2,1,0:T(8,128)(2,1)S(1)} copy-done((bf16[2,4,32,1024]{3,2,1,0:T(8,128)(2,1)S(1)}, bf16[2,4,32,1024]{3,2,1,0:T(8,128)(2,1)}, u32[]{:S(2)}) %copy-start) | copy-done | bytes 524312
  1.0 0.4 whiten.1
  1.5 3.2 %collective-permute-start = (bf16[1,2,1,64,1024]{4,3,2,1,0:T(8,128)(2,1)S(1)}, bf16[1,2,1,64,1024]{4,3,2,1,0:T(8,128)(2,1)S(1)}, u32[]{:S(2)}, u32[]{:S(2)}) collective-permute-start(bf16[1,2,1,64,1024]{4,3,2,1,0:T(8,128)(2,1)S(1)} %get-tuple-element.95.refs_0_), channel_id=1, source_target_pairs={{0,2},{1,3},{2,0},{3,1},{4,6},{5,7},{6,4},{7,5},{8,10},{9,11},{10,... | collective-permute-start | bytes 786440 | tf_op jit(solution)/shard_map/ppermute | solution.py:222
  4.7 1.2 %collective-permute-start.1 = (bf16[64,1024]{1,0:T(8,128)(2,1)S(1)}, bf16[64,1024]{1,0:T(8,128)(2,1)S(1)}, u32[]{:S(2)}, u32[]{:S(2)}) collective-permute-start(bf16[64,1024]{1,0:T(8,128)(2,1)S(1)} %get-tuple-element.66), channel_id=1, source_target_pairs={{0,8},{4,12},{8,0},{12,4},{16,24},{20,28},{24,16},{28,20},{1,9},{5... | collective-permute-start | bytes 393224 | tf_op jit(solution)/shard_map/ppermute | solution.py:225
  5.9 1.2 %collective-permute-start.2 = (bf16[64,1024]{1,0:T(8,128)(2,1)S(1)}, bf16[64,1024]{1,0:T(8,128)(2,1)S(1)}, u32[]{:S(2)}, u32[]{:S(2)}) collective-permute-start(bf16[64,1024]{1,0:T(8,128)(2,1)S(1)} %get-tuple-element.67), channel_id=1, source_target_pairs={{0,16},{4,20},{8,24},{12,28},{16,0},{20,4},{24,8},{28,12},{1,17},{... | collective-permute-start | bytes 393224 | tf_op jit(solution)/shard_map/ppermute | solution.py:225
  7.1 0.2 collective-permute-start.3
  7.4 1.5 %collective-permute-done.1.refs_1_ = bf16[64,1024]{1,0:T(8,128)(2,1)S(1)} collective-permute-done((bf16[64,1024]{1,0:T(8,128)(2,1)S(1)}, bf16[64,1024]{1,0:T(8,128)(2,1)S(1)}, u32[]{:S(2)}, u32[]{:S(2)}) %collective-permute-start.1) | collective-permute-done | bytes 131104 | tf_op jit(solution)/shard_map/ppermute | solution.py:225
  8.8 1.2 %collective-permute-done.2.refs_2_ = bf16[64,1024]{1,0:T(8,128)(2,1)S(1)} collective-permute-done((bf16[64,1024]{1,0:T(8,128)(2,1)S(1)}, bf16[64,1024]{1,0:T(8,128)(2,1)S(1)}, u32[]{:S(2)}, u32[]{:S(2)}) %collective-permute-start.2) | collective-permute-done | bytes 131104 | tf_op jit(solution)/shard_map/ppermute | solution.py:225
  10.0 2.6 %collective-permute-done.3.refs_3_ = bf16[64,1024]{1,0:T(8,128)(2,1)S(1)} collective-permute-done((bf16[64,1024]{1,0:T(8,128)(2,1)S(1)}, bf16[64,1024]{1,0:T(8,128)(2,1)S(1)}, u32[]{:S(2)}, u32[]{:S(2)}) %collective-permute-start.3) | collective-permute-done | bytes 131104 | tf_op jit(solution)/shard_map/ppermute | solution.py:225
  12.6 3.8 %collective-permute-done.refs_1_ = bf16[1,2,1,64,1024]{4,3,2,1,0:T(8,128)(2,1)S(1)} collective-permute-done((bf16[1,2,1,64,1024]{4,3,2,1,0:T(8,128)(2,1)S(1)}, bf16[1,2,1,64,1024]{4,3,2,1,0:T(8,128)(2,1)S(1)}, u32[]{:S(2)}, u32[]{:S(2)}) %collective-permute-start) | collective-permute-done | bytes 262176 | tf_op jit(solution)/shard_map/ppermute | solution.py:222
  16.4 1.2 %collective-permute-start.4 = (bf16[2,1,64,1024]{3,2,1,0:T(8,128)(2,1)S(1)}, bf16[2,1,64,1024]{3,2,1,0:T(8,128)(2,1)S(1)}, u32[]{:S(2)}, u32[]{:S(2)}) collective-permute-start(bf16[2,1,64,1024]{3,2,1,0:T(8,128)(2,1)S(1)} %pad_maximum_fusion), channel_id=1, source_target_pairs={{0,1},{1,0},{2,3},{3,2},{4,5},{5,4},{6,7},{7,6},{8,9},{9,8},{10,11... | collective-permute-start | bytes 786440 | tf_op jit(solution)/shard_map/ppermute | solution.py:222
  17.6 0.1 route.1
  17.7 0.3 collective-permute-start.5
  18.1 2.9 %collective-permute-start.6 = (bf16[64,1024]{1,0:T(8,128)(2,1)S(1)}, bf16[64,1024]{1,0:T(8,128)(2,1)S(1)}, u32[]{:S(2)}, u32[]{:S(2)}) collective-permute-start(bf16[64,1024]{1,0:T(8,128)(2,1)S(1)} %get-tuple-element.76), channel_id=1, source_target_pairs={{0,2},{1,3},{2,0},{3,1},{4,6},{5,7},{6,4},{7,5},{8,10},{9,11},{10,... | collective-permute-start | bytes 393224 | tf_op jit(solution)/shard_map/ppermute | solution.py:222
  21.0 1.1 %collective-permute-start.7 = (bf16[64,1024]{1,0:T(8,128)(2,1)S(1)}, bf16[64,1024]{1,0:T(8,128)(2,1)S(1)}, u32[]{:S(2)}, u32[]{:S(2)}) collective-permute-start(bf16[64,1024]{1,0:T(8,128)(2,1)S(1)} %get-tuple-element.77), channel_id=1, source_target_pairs={{0,3},{1,2},{2,1},{3,0},{4,7},{5,6},{6,5},{7,4},{8,11},{9,10},{10,... | collective-permute-start | bytes 393224 | tf_op jit(solution)/shard_map/ppermute | solution.py:222
  22.1 6.6 %collective-permute-done.5.refs_1_ = bf16[64,1024]{1,0:T(8,128)(2,1)S(1)} collective-permute-done((bf16[64,1024]{1,0:T(8,128)(2,1)S(1)}, bf16[64,1024]{1,0:T(8,128)(2,1)S(1)}, u32[]{:S(2)}, u32[]{:S(2)}) %collective-permute-start.5) | collective-permute-done | bytes 131104 | tf_op jit(solution)/shard_map/ppermute | solution.py:222
  28.6 0.0 collective-permute-done.6.refs_2_
  28.6 6.5 %collective-permute-done.7.refs_3_ = bf16[64,1024]{1,0:T(8,128)(2,1)S(1)} collective-permute-done((bf16[64,1024]{1,0:T(8,128)(2,1)S(1)}, bf16[64,1024]{1,0:T(8,128)(2,1)S(1)}, u32[]{:S(2)}, u32[]{:S(2)}) %collective-permute-start.7) | collective-permute-done | bytes 131104 | tf_op jit(solution)/shard_map/ppermute | solution.py:222
  35.1 0.0 collective-permute-done.4.refs_2_
  35.2 1.1 %collective-permute-start.12 = (bf16[4,64,1024]{2,1,0:T(8,128)(2,1)S(1)}, bf16[4,64,1024]{2,1,0:T(8,128)(2,1)S(1)}, u32[]{:S(2)}, u32[]{:S(2)}) collective-permute-start(bf16[4,64,1024]{2,1,0:T(8,128)(2,1)S(1)} %collect.1.refs_1_), channel_id=1, source_target_pairs={{0,4},{4,0},{8,12},{12,8},{16,20},{20,16},{24,28},{28,24},{1,5},{5... | collective-permute-start | bytes 1572872 | tf_op jit(solution)/shard_map/ppermute | solution.py:228
  36.2 1.2 %collective-permute-start.10 = (bf16[4,64,1024]{2,1,0:T(8,128)(2,1)S(1)}, bf16[4,64,1024]{2,1,0:T(8,128)(2,1)S(1)}, u32[]{:S(2)}, u32[]{:S(2)}) collective-permute-start(bf16[4,64,1024]{2,1,0:T(8,128)(2,1)S(1)} %collect.1.refs_1_), channel_id=1, source_target_pairs={{0,8},{4,12},{8,0},{12,4},{16,24},{20,28},{24,16},{28,20},{1,9},{5... | collective-permute-start | bytes 1572872 | tf_op jit(solution)/shard_map/ppermute | solution.py:225
  37.5 1.2 %collective-permute-start.11 = (bf16[4,64,1024]{2,1,0:T(8,128)(2,1)S(1)}, bf16[4,64,1024]{2,1,0:T(8,128)(2,1)S(1)}, u32[]{:S(2)}, u32[]{:S(2)}) collective-permute-start(bf16[4,64,1024]{2,1,0:T(8,128)(2,1)S(1)} %collect.1.refs_1_), channel_id=1, source_target_pairs={{0,16},{4,20},{8,24},{12,28},{16,0},{20,4},{24,8},{28,12},{1,17},{... | collective-permute-start | bytes 1572872 | tf_op jit(solution)/shard_map/ppermute | solution.py:225
  38.8 0.1 collective-permute-start.8
  38.9 1.7 %collective-permute-start.9 = (bf16[1,1,1,64,1024]{4,3,2,1,0:T(8,128)(2,1)S(1)}, bf16[1,1,1,64,1024]{4,3,2,1,0:T(8,128)(2,1)S(1)}, u32[]{:S(2)}, u32[]{:S(2)}) collective-permute-start(bf16[1,1,1,64,1024]{4,3,2,1,0:T(8,128)(2,1)S(1)} %get-tuple-element.104.refs_0_), channel_id=1, source_target_pairs={{0,2},{1,3},{2,0},{3,1},{4,6},{5,7},{6,4},{7,5},{8,10},{9,11},{10,... | collective-permute-start | bytes 393224 | tf_op jit(solution)/shard_map/ppermute | solution.py:222
  40.6 0.2 turn.4.refs_0_.refs_2_
  40.8 0.0 collective-permute-done.12.refs_3_
  40.8 6.2 %product.6.refs_2_ = f32[2,4,1024,2048]{3,2,1,0:T(8,128)} custom-call(bf16[1024,256]{1,0:T(8,128)(2,1)S(1)} %turn.4.refs_0_.refs_2_, bf16[4,64,1024]{2,1,0:T(8,128)(2,1)S(1)} %collect.1.refs_1_, bf16[1024,256]{1,0:T(8,128)(2,1)S(1)} %turn.4.refs_0_.refs_2_, bf16[4,64,1024]{2,1,0:T(8,128)(2,1)S(1)} %collective-permute-done.12.refs_3_), custom_call_target="tpu_custom_call" | custom-call | flops 536870912 | bytes 4194304 | tf_op jit(solution)/shard_map/product/pallas_call | solution.py:192
  47.0 2.7 %collective-permute-done.10.refs_1_ = bf16[4,64,1024]{2,1,0:T(8,128)(2,1)S(1)} collective-permute-done((bf16[4,64,1024]{2,1,0:T(8,128)(2,1)S(1)}, bf16[4,64,1024]{2,1,0:T(8,128)(2,1)S(1)}, u32[]{:S(2)}, u32[]{:S(2)}) %collective-permute-start.10) | collective-permute-done | bytes 524320 | tf_op jit(solution)/shard_map/ppermute | solution.py:225
  49.8 0.9 %collective-permute-done.11.refs_1_ = bf16[4,64,1024]{2,1,0:T(8,128)(2,1)S(1)} collective-permute-done((bf16[4,64,1024]{2,1,0:T(8,128)(2,1)S(1)}, bf16[4,64,1024]{2,1,0:T(8,128)(2,1)S(1)}, u32[]{:S(2)}, u32[]{:S(2)}) %collective-permute-start.11) | collective-permute-done | bytes 524320 | tf_op jit(solution)/shard_map/ppermute | solution.py:225
  50.6 0.0 collective-permute-done.9.refs_1_
  50.6 0.0 collective-permute-done.8.refs_2_
  50.6 1.2 %collective-permute-start.15 = (bf16[4,64,1024]{2,1,0:T(8,128)(2,1)S(1)}, bf16[4,64,1024]{2,1,0:T(8,128)(2,1)S(1)}, u32[]{:S(2)}, u32[]{:S(2)}) collective-permute-start(bf16[4,64,1024]{2,1,0:T(8,128)(2,1)S(1)} %collective-permute-done.10.refs_1_), channel_id=1, source_target_pairs={{0,4},{4,0},{8,12},{12,8},{16,20},{20,16},{24,28},{28,24},{1,5},{5... | collective-permute-start | bytes 1572872 | tf_op jit(solution)/shard_map/ppermute | solution.py:228
  51.9 0.1 collective-permute-start.13
  51.9 0.2 turn.5.refs_0_
  52.1 3.7 %product.7.refs_2_ = f32[2,4,1024,2048]{3,2,1,0:T(8,128)} custom-call(bf16[1024,256]{1,0:T(8,128)(2,1)S(1)} %turn.5.refs_0_, bf16[4,64,1024]{2,1,0:T(8,128)(2,1)S(1)} %collective-permute-done.10.refs_1_, f32[2,4,1024,2048]{3,2,1,0:T(8,128)} %product.6.refs_2_), custom_call_target="tpu_custom_call", output_to_operand_aliasing={{}: (2, {})} | custom-call | flops 268435456 | bytes 2097152 | tf_op jit(solution)/shard_map/product/pallas_call | solution.py:192
  55.8 0.0 collective-permute-done.15.refs_1_
  55.9 0.1 collective-permute-start.18
  55.9 0.3 collective-permute-start.17
  56.2 2.0 %collective-permute-start.14 = (bf16[1,1,1,64,1024]{4,3,2,1,0:T(8,128)(2,1)S(1)}, bf16[1,1,1,64,1024]{4,3,2,1,0:T(8,128)(2,1)S(1)}, u32[]{:S(2)}, u32[]{:S(2)}) collective-permute-start(bf16[1,1,1,64,1024]{4,3,2,1,0:T(8,128)(2,1)S(1)} %get-tuple-element.112.refs_0_), channel_id=1, source_target_pairs={{0,2},{1,3},{2,0},{3,1},{4,6},{5,7},{6,4},{7,5},{8,10},{9,11},{10,... | collective-permute-start | bytes 393224 | tf_op jit(solution)/shard_map/ppermute | solution.py:222
  58.2 3.7 %product.8.refs_4_ = f32[2,4,1024,2048]{3,2,1,0:T(8,128)} custom-call(bf16[1024,256]{1,0:T(8,128)(2,1)S(1)} %turn.5.refs_0_, bf16[4,64,1024]{2,1,0:T(8,128)(2,1)S(1)} %collective-permute-done.15.refs_1_, f32[2,4,1024,2048]{3,2,1,0:T(8,128)} %product.7.refs_2_), custom_call_target="tpu_custom_call", output_to_operand_aliasing={{}: (2, {})} | custom-call | flops 268435456 | bytes 2097152 | tf_op jit(solution)/shard_map/product/pallas_call | solution.py:192
  61.9 2.5 %collective-permute-done.14.refs_1_ = bf16[1,1,1,64,1024]{4,3,2,1,0:T(8,128)(2,1)S(1)} collective-permute-done((bf16[1,1,1,64,1024]{4,3,2,1,0:T(8,128)(2,1)S(1)}, bf16[1,1,1,64,1024]{4,3,2,1,0:T(8,128)(2,1)S(1)}, u32[]{:S(2)}, u32[]{:S(2)}) %collective-permute-start.14) | collective-permute-done | bytes 131104 | tf_op jit(solution)/shard_map/ppermute | solution.py:222
  64.4 0.0 collective-permute-done.13.refs_2_
  64.4 0.1 collective-permute-start.16
  64.5 0.2 turn.6.refs_0_.refs_2_
  64.7 0.0 collective-permute-done.18.refs_3_
  64.7 6.2 %product.9.refs_2_ = f32[2,4,1024,2048]{3,2,1,0:T(8,128)} custom-call(bf16[1024,256]{1,0:T(8,128)(2,1)S(1)} %turn.6.refs_0_.refs_2_, bf16[4,64,1024]{2,1,0:T(8,128)(2,1)S(1)} %collective-permute-done.11.refs_1_, bf16[1024,256]{1,0:T(8,128)(2,1)S(1)} %turn.6.refs_0_.refs_2_, ...), custom_call_target="tpu_custom_call", output_to_operand_aliasing={{}: (4, {})} | custom-call | flops 536870912 | bytes 4194304 | tf_op jit(solution)/shard_map/product/pallas_call | solution.py:192
  70.9 0.0 collective-permute-done.17.refs_1_
  70.9 0.0 collective-permute-done.16.refs_2_
  70.9 2.2 %collective-permute-start.19 = (bf16[4,64,1024]{2,1,0:T(8,128)(2,1)S(1)}, bf16[4,64,1024]{2,1,0:T(8,128)(2,1)S(1)}, u32[]{:S(2)}, u32[]{:S(2)}) collective-permute-start(bf16[4,64,1024]{2,1,0:T(8,128)(2,1)S(1)} %collective-permute-done.17.refs_1_), channel_id=1, source_target_pairs={{0,4},{4,0},{8,12},{12,8},{16,20},{20,16},{24,28},{28,24},{1,5},{5... | collective-permute-start | bytes 1572872 | tf_op jit(solution)/shard_map/ppermute | solution.py:228
  73.2 0.2 turn.7.refs_0_
  73.4 3.7 %product.10.refs_2_ = f32[2,4,1024,2048]{3,2,1,0:T(8,128)} custom-call(bf16[1024,256]{1,0:T(8,128)(2,1)S(1)} %turn.7.refs_0_, bf16[4,64,1024]{2,1,0:T(8,128)(2,1)S(1)} %collective-permute-done.17.refs_1_, f32[2,4,1024,2048]{3,2,1,0:T(8,128)} %product.9.refs_2_), custom_call_target="tpu_custom_call", output_to_operand_aliasing={{}: (2, {})} | custom-call | flops 268435456 | bytes 2097152 | tf_op jit(solution)/shard_map/product/pallas_call | solution.py:192
  77.1 0.0 collective-permute-done.19.refs_1_
  77.1 3.7 %product.11 = f32[2,4,1024,2048]{3,2,1,0:T(8,128)} custom-call(bf16[1024,256]{1,0:T(8,128)(2,1)S(1)} %turn.7.refs_0_, bf16[4,64,1024]{2,1,0:T(8,128)(2,1)S(1)} %collective-permute-done.19.refs_1_, f32[2,4,1024,2048]{3,2,1,0:T(8,128)} %product.10.refs_2_), custom_call_target="tpu_custom_call", output_to_operand_aliasing={{}: (2, {})} | custom-call | flops 268435456 | bytes 2097152 | tf_op jit(solution)/shard_map/product/pallas_call | solution.py:192
  (8 shorter events, 0.2 us)
Async XLA Ops:
  0.0 1.0 %copy-start = (bf16[2,4,32,1024]{3,2,1,0:T(8,128)(2,1)S(1)}, bf16[2,4,32,1024]{3,2,1,0:T(8,128)(2,1)}, u32[]{:S(2)}) copy-start(bf16[2,4,32,1024]{3,2,1,0:T(8,128)(2,1)} %raw.1) | copy-start | bytes 1572868
  1.5 14.9 %collective-permute-start = (bf16[1,2,1,64,1024]{4,3,2,1,0:T(8,128)(2,1)S(1)}, bf16[1,2,1,64,1024]{4,3,2,1,0:T(8,128)(2,1)S(1)}, u32[]{:S(2)}, u32[]{:S(2)}) collective-permute-start(bf16[1,2,1,64,1024]{4,3,2,1,0:T(8,128)(2,1)S(1)} %get-tuple-element.95.refs_0_), channel_id=1, source_target_pairs={{0,2},{1,3},{2,0},{3,1},{4,6},{5,7},{6,4},{7,5},{8,10},{9,11},{10,... | collective-permute-start | bytes 786440 | tf_op jit(solution)/shard_map/ppermute | solution.py:222
  4.7 4.1 %collective-permute-start.1 = (bf16[64,1024]{1,0:T(8,128)(2,1)S(1)}, bf16[64,1024]{1,0:T(8,128)(2,1)S(1)}, u32[]{:S(2)}, u32[]{:S(2)}) collective-permute-start(bf16[64,1024]{1,0:T(8,128)(2,1)S(1)} %get-tuple-element.66), channel_id=1, source_target_pairs={{0,8},{4,12},{8,0},{12,4},{16,24},{20,28},{24,16},{28,20},{1,9},{5... | collective-permute-start | bytes 393224 | tf_op jit(solution)/shard_map/ppermute | solution.py:225
  5.9 4.1 %collective-permute-start.2 = (bf16[64,1024]{1,0:T(8,128)(2,1)S(1)}, bf16[64,1024]{1,0:T(8,128)(2,1)S(1)}, u32[]{:S(2)}, u32[]{:S(2)}) collective-permute-start(bf16[64,1024]{1,0:T(8,128)(2,1)S(1)} %get-tuple-element.67), channel_id=1, source_target_pairs={{0,16},{4,20},{8,24},{12,28},{16,0},{20,4},{24,8},{28,12},{1,17},{... | collective-permute-start | bytes 393224 | tf_op jit(solution)/shard_map/ppermute | solution.py:225
  7.1 5.4 %collective-permute-start.3 = (bf16[64,1024]{1,0:T(8,128)(2,1)S(1)}, bf16[64,1024]{1,0:T(8,128)(2,1)S(1)}, u32[]{:S(2)}, u32[]{:S(2)}) collective-permute-start(bf16[64,1024]{1,0:T(8,128)(2,1)S(1)} %get-tuple-element.68), channel_id=1, source_target_pairs={{0,24},{4,28},{8,16},{12,20},{16,8},{20,12},{24,0},{28,4},{1,25},{... | collective-permute-start | bytes 393224 | tf_op jit(solution)/shard_map/ppermute | solution.py:225
  16.4 18.7 %collective-permute-start.4 = (bf16[2,1,64,1024]{3,2,1,0:T(8,128)(2,1)S(1)}, bf16[2,1,64,1024]{3,2,1,0:T(8,128)(2,1)S(1)}, u32[]{:S(2)}, u32[]{:S(2)}) collective-permute-start(bf16[2,1,64,1024]{3,2,1,0:T(8,128)(2,1)S(1)} %pad_maximum_fusion), channel_id=1, source_target_pairs={{0,1},{1,0},{2,3},{3,2},{4,5},{5,4},{6,7},{7,6},{8,9},{9,8},{10,11... | collective-permute-start | bytes 786440 | tf_op jit(solution)/shard_map/ppermute | solution.py:222
  17.7 10.9 %collective-permute-start.5 = (bf16[64,1024]{1,0:T(8,128)(2,1)S(1)}, bf16[64,1024]{1,0:T(8,128)(2,1)S(1)}, u32[]{:S(2)}, u32[]{:S(2)}) collective-permute-start(bf16[64,1024]{1,0:T(8,128)(2,1)S(1)} %get-tuple-element.75), channel_id=1, source_target_pairs={{0,1},{1,0},{2,3},{3,2},{4,5},{5,4},{6,7},{7,6},{8,9},{9,8},{10,11... | collective-permute-start | bytes 393224 | tf_op jit(solution)/shard_map/ppermute | solution.py:222
  18.1 10.6 %collective-permute-start.6 = (bf16[64,1024]{1,0:T(8,128)(2,1)S(1)}, bf16[64,1024]{1,0:T(8,128)(2,1)S(1)}, u32[]{:S(2)}, u32[]{:S(2)}) collective-permute-start(bf16[64,1024]{1,0:T(8,128)(2,1)S(1)} %get-tuple-element.76), channel_id=1, source_target_pairs={{0,2},{1,3},{2,0},{3,1},{4,6},{5,7},{6,4},{7,5},{8,10},{9,11},{10,... | collective-permute-start | bytes 393224 | tf_op jit(solution)/shard_map/ppermute | solution.py:222
  21.0 14.1 %collective-permute-start.7 = (bf16[64,1024]{1,0:T(8,128)(2,1)S(1)}, bf16[64,1024]{1,0:T(8,128)(2,1)S(1)}, u32[]{:S(2)}, u32[]{:S(2)}) collective-permute-start(bf16[64,1024]{1,0:T(8,128)(2,1)S(1)} %get-tuple-element.77), channel_id=1, source_target_pairs={{0,3},{1,2},{2,1},{3,0},{4,7},{5,6},{6,5},{7,4},{8,11},{9,10},{10,... | collective-permute-start | bytes 393224 | tf_op jit(solution)/shard_map/ppermute | solution.py:222
  35.2 5.6 %collective-permute-start.12 = (bf16[4,64,1024]{2,1,0:T(8,128)(2,1)S(1)}, bf16[4,64,1024]{2,1,0:T(8,128)(2,1)S(1)}, u32[]{:S(2)}, u32[]{:S(2)}) collective-permute-start(bf16[4,64,1024]{2,1,0:T(8,128)(2,1)S(1)} %collect.1.refs_1_), channel_id=1, source_target_pairs={{0,4},{4,0},{8,12},{12,8},{16,20},{20,16},{24,28},{28,24},{1,5},{5... | collective-permute-start | bytes 1572872 | tf_op jit(solution)/shard_map/ppermute | solution.py:228
  36.2 13.5 %collective-permute-start.10 = (bf16[4,64,1024]{2,1,0:T(8,128)(2,1)S(1)}, bf16[4,64,1024]{2,1,0:T(8,128)(2,1)S(1)}, u32[]{:S(2)}, u32[]{:S(2)}) collective-permute-start(bf16[4,64,1024]{2,1,0:T(8,128)(2,1)S(1)} %collect.1.refs_1_), channel_id=1, source_target_pairs={{0,8},{4,12},{8,0},{12,4},{16,24},{20,28},{24,16},{28,20},{1,9},{5... | collective-permute-start | bytes 1572872 | tf_op jit(solution)/shard_map/ppermute | solution.py:225
  37.5 13.2 %collective-permute-start.11 = (bf16[4,64,1024]{2,1,0:T(8,128)(2,1)S(1)}, bf16[4,64,1024]{2,1,0:T(8,128)(2,1)S(1)}, u32[]{:S(2)}, u32[]{:S(2)}) collective-permute-start(bf16[4,64,1024]{2,1,0:T(8,128)(2,1)S(1)} %collect.1.refs_1_), channel_id=1, source_target_pairs={{0,16},{4,20},{8,24},{12,28},{16,0},{20,4},{24,8},{28,12},{1,17},{... | collective-permute-start | bytes 1572872 | tf_op jit(solution)/shard_map/ppermute | solution.py:225
  38.8 11.9 %collective-permute-start.8 = (bf16[2,1,64,1024]{3,2,1,0:T(8,128)(2,1)S(1)}, bf16[2,1,64,1024]{3,2,1,0:T(8,128)(2,1)S(1)}, u32[]{:S(2)}, u32[]{:S(2)}) collective-permute-start(bf16[2,1,64,1024]{3,2,1,0:T(8,128)(2,1)S(1)} %pad_maximum_fusion.1), channel_id=1, source_target_pairs={{0,1},{1,0},{2,3},{3,2},{4,5},{5,4},{6,7},{7,6},{8,9},{9,8},{10,11... | collective-permute-start | bytes 786440 | tf_op jit(solution)/shard_map/ppermute | solution.py:222
  38.9 11.8 %collective-permute-start.9 = (bf16[1,1,1,64,1024]{4,3,2,1,0:T(8,128)(2,1)S(1)}, bf16[1,1,1,64,1024]{4,3,2,1,0:T(8,128)(2,1)S(1)}, u32[]{:S(2)}, u32[]{:S(2)}) collective-permute-start(bf16[1,1,1,64,1024]{4,3,2,1,0:T(8,128)(2,1)S(1)} %get-tuple-element.104.refs_0_), channel_id=1, source_target_pairs={{0,2},{1,3},{2,0},{3,1},{4,6},{5,7},{6,4},{7,5},{8,10},{9,11},{10,... | collective-permute-start | bytes 393224 | tf_op jit(solution)/shard_map/ppermute | solution.py:222
  50.6 5.2 %collective-permute-start.15 = (bf16[4,64,1024]{2,1,0:T(8,128)(2,1)S(1)}, bf16[4,64,1024]{2,1,0:T(8,128)(2,1)S(1)}, u32[]{:S(2)}, u32[]{:S(2)}) collective-permute-start(bf16[4,64,1024]{2,1,0:T(8,128)(2,1)S(1)} %collective-permute-done.10.refs_1_), channel_id=1, source_target_pairs={{0,4},{4,0},{8,12},{12,8},{16,20},{20,16},{24,28},{28,24},{1,5},{5... | collective-permute-start | bytes 1572872 | tf_op jit(solution)/shard_map/ppermute | solution.py:228
  51.9 12.5 %collective-permute-start.13 = (bf16[2,1,64,1024]{3,2,1,0:T(8,128)(2,1)S(1)}, bf16[2,1,64,1024]{3,2,1,0:T(8,128)(2,1)S(1)}, u32[]{:S(2)}, u32[]{:S(2)}) collective-permute-start(bf16[2,1,64,1024]{3,2,1,0:T(8,128)(2,1)S(1)} %pad_maximum_fusion.2), channel_id=1, source_target_pairs={{0,1},{1,0},{2,3},{3,2},{4,5},{5,4},{6,7},{7,6},{8,9},{9,8},{10,11... | collective-permute-start | bytes 786440 | tf_op jit(solution)/shard_map/ppermute | solution.py:222
  55.9 8.8 %collective-permute-start.18 = (bf16[4,64,1024]{2,1,0:T(8,128)(2,1)S(1)}, bf16[4,64,1024]{2,1,0:T(8,128)(2,1)S(1)}, u32[]{:S(2)}, u32[]{:S(2)}) collective-permute-start(bf16[4,64,1024]{2,1,0:T(8,128)(2,1)S(1)} %collective-permute-done.11.refs_1_), channel_id=1, source_target_pairs={{0,4},{4,0},{8,12},{12,8},{16,20},{20,16},{24,28},{28,24},{1,5},{5... | collective-permute-start | bytes 1572872 | tf_op jit(solution)/shard_map/ppermute | solution.py:228
  55.9 15.0 %collective-permute-start.17 = (bf16[4,64,1024]{2,1,0:T(8,128)(2,1)S(1)}, bf16[4,64,1024]{2,1,0:T(8,128)(2,1)S(1)}, u32[]{:S(2)}, u32[]{:S(2)}) collective-permute-start(bf16[4,64,1024]{2,1,0:T(8,128)(2,1)S(1)} %collective-permute-done.11.refs_1_), channel_id=1, source_target_pairs={{0,8},{4,12},{8,0},{12,4},{16,24},{20,28},{24,16},{28,20},{1,9},{5... | collective-permute-start | bytes 1572872 | tf_op jit(solution)/shard_map/ppermute | solution.py:225
  56.2 8.1 %collective-permute-start.14 = (bf16[1,1,1,64,1024]{4,3,2,1,0:T(8,128)(2,1)S(1)}, bf16[1,1,1,64,1024]{4,3,2,1,0:T(8,128)(2,1)S(1)}, u32[]{:S(2)}, u32[]{:S(2)}) collective-permute-start(bf16[1,1,1,64,1024]{4,3,2,1,0:T(8,128)(2,1)S(1)} %get-tuple-element.112.refs_0_), channel_id=1, source_target_pairs={{0,2},{1,3},{2,0},{3,1},{4,6},{5,7},{6,4},{7,5},{8,10},{9,11},{10,... | collective-permute-start | bytes 393224 | tf_op jit(solution)/shard_map/ppermute | solution.py:222
  64.4 6.5 %collective-permute-start.16 = (bf16[2,1,64,1024]{3,2,1,0:T(8,128)(2,1)S(1)}, bf16[2,1,64,1024]{3,2,1,0:T(8,128)(2,1)S(1)}, u32[]{:S(2)}, u32[]{:S(2)}) collective-permute-start(bf16[2,1,64,1024]{3,2,1,0:T(8,128)(2,1)S(1)} %pad_maximum_fusion.3), channel_id=1, source_target_pairs={{0,1},{1,0},{2,3},{3,2},{4,5},{5,4},{6,7},{7,6},{8,9},{9,8},{10,11... | collective-permute-start | bytes 786440 | tf_op jit(solution)/shard_map/ppermute | solution.py:222
  70.9 6.2 %collective-permute-start.19 = (bf16[4,64,1024]{2,1,0:T(8,128)(2,1)S(1)}, bf16[4,64,1024]{2,1,0:T(8,128)(2,1)S(1)}, u32[]{:S(2)}, u32[]{:S(2)}) collective-permute-start(bf16[4,64,1024]{2,1,0:T(8,128)(2,1)S(1)} %collective-permute-done.17.refs_1_), channel_id=1, source_target_pairs={{0,4},{4,0},{8,12},{12,8},{16,20},{20,16},{24,28},{28,24},{1,5},{5... | collective-permute-start | bytes 1572872 | tf_op jit(solution)/shard_map/ppermute | solution.py:228

commit v5 on v4

--- a/solution.py
+++ b/solution.py
@@ -55,10 +55,9 @@
     blocks, outs = refs[:n], refs[n:]
     q, z = lax.axis_index("row") // 2, lax.axis_index("col")
     for e, out in enumerate(outs):
-        wanted = q ^ z ^ e
         for d, block in enumerate(blocks):
 
-            @pl.when(wanted == d)
+            @pl.when((q ^ z ^ e) == d)
             def _(block=block, out=out):
                 out[...] = block[...]
 
@@ -77,9 +76,8 @@
 
 
 def collect_kernel(*refs):
-    z = lax.axis_index("col")
-    for e, x in enumerate(refs[:-1]):
-        refs[-1][z ^ e] = x[...]
+    for at, x in enumerate(refs[:-1]):
+        refs[-1][at] = x[...]
 
 
 def collect(parts):
@@ -88,6 +86,7 @@
         out_shape=jax.ShapeDtypeStruct((len(parts), *parts[0].shape), jnp.bfloat16),
         in_specs=[pl.BlockSpec(memory_space=pltpu.VMEM)] * len(parts),
         out_specs=pl.BlockSpec(memory_space=pltpu.VMEM),
+        cost_estimate=pl.CostEstimate(flops=1 << 33, bytes_accessed=0, transcendentals=0),
         compiler_params=pltpu.CompilerParams(vmem_limit_bytes=24 << 20),
         name="collect",
     )(*parts)
@@ -117,6 +116,7 @@
         out_shape=jax.ShapeDtypeStruct((channels, n * n_split * part), jnp.bfloat16),
         in_specs=[pl.BlockSpec(memory_space=pltpu.VMEM)] * len(parts),
         out_specs=pl.BlockSpec(memory_space=pltpu.VMEM),
+        cost_estimate=pl.CostEstimate(flops=0, bytes_accessed=1, transcendentals=0),
         compiler_params=pltpu.CompilerParams(vmem_limit_bytes=24 << 20),
         name="turn",
     )(*parts)
@@ -125,7 +125,7 @@
 def product_kernel(items, n, n_split, tile, norm, *refs):
     operands = [refs[at * (n_split + 1) : (at + 1) * (n_split + 1)] for at in range(len(items))]
     out, made, out_sem = refs[-3:]
-    q, k, z = lax.axis_index("row") // 2, lax.axis_index("row") % 2, lax.axis_index("col")
+    q, k = lax.axis_index("row") // 2, lax.axis_index("row") % 2
     channels = operands[0][0].shape[0]
     part = operands[0][1].shape[1]
     slots, _, height, width = made.shape
@@ -154,7 +154,7 @@
 
         left = turned[pl.ds(pl.multiple_of(at % per_column * height, height), height)]
         start = pl.multiple_of(at // per_column * width, width)
-        piece = lambda s, d: columns[s][z ^ d, :, pl.ds(start, width)]
+        piece = lambda s, d: columns[s][d, :, pl.ds(start, width)]
         right = jnp.concatenate([piece(s, d) for s, d in pairs], axis=0)
         made[total % slots, 0] = norm * jnp.dot(left, right, preferred_element_type=jnp.float32)
         half = part // 2 if n_split == 1 else n_split // 2
@@ -214,7 +214,7 @@
     n_bins = spectra.shape[1]
     assert lax.axis_size("row") == 2 * n and n % n_bins == 0 and n_bins > 1 and n & (n - 1) == 0
     n_split = n // n_bins
-    chunks = [(0, 1)] + [(f,) for f in range(2, n_bins)]
+    chunks = [(0, 1)] + [tuple(range(2, n_bins))] * (n_bins > 2)
     place = [(at, i) for at, chunk in enumerate(chunks) for i in range(len(chunk))]
     rows, pieces = whiten(spectra, n, n_split, chunks)
 
@@ -245,13 +245,19 @@
     blocks = [from_chip(piece, d) if d else piece for d, piece in enumerate(pieces)]
     firsts, blocks = wait(firsts, blocks)
     arrived = [along_line(x, e) if e else x for e, x in enumerate(route(blocks))]
+    firsts, arrived[1] = wait(firsts, arrived[1])
     parts = [gather_bin(0)]
-    (rows, firsts, parts), arrived = wait((rows, firsts, parts), arrived)
-    near = [collect(arrived)]
-    for d in range(1, n):
+    halves = [jnp.stack(arrived[: n // 2]), collect(arrived[n // 2 :])]
+    direct = [d for d in range(1, n) if d & (d - 1) == 0]
+    early = [from_chip(halves[0], d) for d in direct]
+    (rows, firsts, early), halves = wait((rows, firsts, early), halves)
+    near = [jnp.concatenate(halves)] + [None] * (n - 1)
+    late = [from_chip(halves[1], d) for d in direct]
+    for d in range(1, n_split):
         low = d & -d
-        near.append(from_chip(near[d ^ low], low) if d == low or d < n_split else None)
+        near[d] = jnp.concatenate([early[direct.index(d)], late[direct.index(d)]]) if d == low else from_chip(near[d ^ low], low)
     far = [from_core(x) for x in near[:n_split]]
+    (rows, firsts), parts = wait((rows, firsts), parts)
     parts.append(gather_bin(1))
     firsts += [along_line(x, n // 2) for x in rows[1:2]]
 
@@ -259,27 +265,24 @@
     of_bin = lambda x, f: x[f * n_split : (f + 1) * n_split]
     turned = turn(0, parts[0], n)
     out = call([(0, False), (0, True)], [turned] * 2, [of_bin(near, 0), far], None)
-    near[n_split:], out = wait(near[n_split:], out)
+    late, out = wait(late, out)
     for d in range(n_split, n):
         low = d & -d
-        if near[d] is None:
-            near[d] = from_chip(near[d ^ low], low)
+        near[d] = jnp.concatenate([early[direct.index(d)], late[direct.index(d)]]) if d == low else from_chip(near[d ^ low], low)
     for f in range(1, n_bins):
-        needed = (parts[f], firsts, rows, of_bin(near, f))
-        (parts[f], firsts, rows, mine), out = wait(needed, out)
+        needed = (parts[f], firsts, rows, of_bin(near, f), of_bin(near, f + 1) if f + 2 < n_bins else [])
+        (parts[f], firsts, rows, mine, later), out = wait(needed, out)
         turned = turn(place[f][1], parts[f], n)
         if f + 1 < n_bins:
             parts.append(gather_bin(f + 1))
-        if f + 2 < n_bins:
-            firsts.append(along_line(rows[f + 1], n // 2))
         if f in (1, n_bins - 1):
             far = [from_core(x) for x in mine]
+            following = [from_core(x) for x in later]
             out = call([(f, False)], [turned], [mine], out)
-            (far, later), out = wait((far, of_bin(near, f + 1) if f == 1 else []), out)
-            following = [from_core(x) for x in later]
+            (far, following), out = wait((far, following), out)
             out = call([(f, True)], [turned], [far], out)
         else:
-            (far, later), out = wait((following, of_bin(near, f + 1) if f + 2 < n_bins else []), out)
+            far, out = wait(following, out)
             following = [from_core(x) for x in later]
             out = call([(f, False), (f, True)], [turned] * 2, [mine, far], out)
     return out

time: 81 us -> 77.5 us (0.957)
  waiting for transfers between devices: 28.1 us -> 17 us
  starting transfers between devices: 22.7 us -> 30.1 us
    ppermute x10 -> x9, waiting for transfers between devices: 19.3 us -> 11.7 us  [along_line(): return lax.ppermute(values, 'col', [(z, z ^ bit) for z in range(n)])]
    ppermute x4, starting transfers between devices: 4.58 us -> 8.37 us  [from_core(): return lax.ppermute(values, 'row', [(r, r ^ 1) for r in range(2 * n)])]
    ppermute x6 -> x8, waiting for transfers between devices: 8.84 us -> 5.25 us  [from_chip(): lax.ppermute(values, 'row', [(2 * q + k, 2 * (q ^ d) + k) for q in range(...]
    ppermute x6 -> x8, starting transfers between devices: 5.43 us -> 7.38 us  [from_chip(): lax.ppermute(values, 'row', [(2 * q + k, 2 * (q ^ d) + k) for q in range(...]
    ppermute x10 -> x9, starting transfers between devices: 12.7 us -> 14.4 us  [along_line(): return lax.ppermute(values, 'col', [(z, z ^ bit) for z in range(n)])]
  transfers between devices with their start and end apart: 20 -> 21, of which waited for: 9 -> 6; matrix products, arithmetic and copies ran while one was open for 0% -> 0% of each run, Pallas kernels for 30% -> 31%
where the time goes in v5:
time: 77.5 us; the launch traced here: 77.3 us
  starting transfers between devices  30.1 us (39%)
  Pallas kernels  28.6 us (37%)
  waiting for transfers between devices  17 us (22%)
  local copies, waits for them, and re-layouts  1.2 us (2%)
    pallas_call x6, Pallas kernels, product(): pl.pallas_call(functools.partial(product_kernel, items, n, n_split, width...  27.3 us
    ppermute x9, starting transfers between devices, along_line(): return lax.ppermute(values, 'col', [(z, z ^ bit) for z in range(n)])  14.4 us
    ppermute x9, waiting for transfers between devices, along_line(): return lax.ppermute(values, 'col', [(z, z ^ bit) for z in range(n)])  11.7 us
    ppermute x4, starting transfers between devices, from_core(): return lax.ppermute(values, 'row', [(r, r ^ 1) for r in range(2 * n)])  8.37 us
    ppermute x8, starting transfers between devices, from_chip(): lax.ppermute(values, 'row', [(2 * q + k, 2 * (q ^ d) + k) for q in range(...  7.38 us
    ppermute x8, waiting for transfers between devices, from_chip(): lax.ppermute(values, 'row', [(2 * q + k, 2 * (q ^ d) + k) for q in range(...  5.25 us
  transfers between devices with their start and end apart: 21, of which 6 were waited for; matrix products, arithmetic and copies ran while one was open for 0% of the time, Pallas kernels for 31%

profile of v5, /device:TPU:1, one launch (start us, length us, event | category | flops | bytes accessed | tf_op | source)
XLA Modules:
  0.0 77.3 jit_solution(2415784207075191194)
XLA Ops:
  0.0 0.0 copy-start
  0.0 1.0 %copy-done = bf16[2,4,32,1024]{3,2,1,0:T(8,128)(2,1)S(1)} copy-done((bf16[2,4,32,1024]{3,2,1,0:T(8,128)(2,1)S(1)}, bf16[2,4,32,1024]{3,2,1,0:T(8,128)(2,1)}, u32[]{:S(2)}) %copy-start) | copy-done | bytes 524312
  1.0 0.4 whiten.1
  1.5 3.2 %collective-permute-start = (bf16[1,2,1,64,1024]{4,3,2,1,0:T(8,128)(2,1)S(1)}, bf16[1,2,1,64,1024]{4,3,2,1,0:T(8,128)(2,1)S(1)}, u32[]{:S(2)}, u32[]{:S(2)}) collective-permute-start(bf16[1,2,1,64,1024]{4,3,2,1,0:T(8,128)(2,1)S(1)} %get-tuple-element.100.refs_0_), channel_id=1, source_target_pairs={{0,2},{1,3},{2,0},{3,1},{4,6},{5,7},{6,4},{7,5},{8,10},{9,11},{10,... | collective-permute-start | bytes 786440 | tf_op jit(solution)/shard_map/ppermute | solution.py:222
  4.7 1.2 %collective-permute-start.1 = (bf16[64,1024]{1,0:T(8,128)(2,1)S(1)}, bf16[64,1024]{1,0:T(8,128)(2,1)S(1)}, u32[]{:S(2)}, u32[]{:S(2)}) collective-permute-start(bf16[64,1024]{1,0:T(8,128)(2,1)S(1)} %get-tuple-element.68), channel_id=1, source_target_pairs={{0,8},{4,12},{8,0},{12,4},{16,24},{20,28},{24,16},{28,20},{1,9},{5... | collective-permute-start | bytes 393224 | tf_op jit(solution)/shard_map/ppermute | solution.py:225
  5.9 1.2 %collective-permute-start.2 = (bf16[64,1024]{1,0:T(8,128)(2,1)S(1)}, bf16[64,1024]{1,0:T(8,128)(2,1)S(1)}, u32[]{:S(2)}, u32[]{:S(2)}) collective-permute-start(bf16[64,1024]{1,0:T(8,128)(2,1)S(1)} %get-tuple-element.69), channel_id=1, source_target_pairs={{0,16},{4,20},{8,24},{12,28},{16,0},{20,4},{24,8},{28,12},{1,17},{... | collective-permute-start | bytes 393224 | tf_op jit(solution)/shard_map/ppermute | solution.py:225
  7.1 0.2 collective-permute-start.3
  7.3 1.5 %collective-permute-done.1.refs_1_ = bf16[64,1024]{1,0:T(8,128)(2,1)S(1)} collective-permute-done((bf16[64,1024]{1,0:T(8,128)(2,1)S(1)}, bf16[64,1024]{1,0:T(8,128)(2,1)S(1)}, u32[]{:S(2)}, u32[]{:S(2)}) %collective-permute-start.1) | collective-permute-done | bytes 131104 | tf_op jit(solution)/shard_map/ppermute | solution.py:225
  8.8 1.2 %collective-permute-done.2.refs_2_ = bf16[64,1024]{1,0:T(8,128)(2,1)S(1)} collective-permute-done((bf16[64,1024]{1,0:T(8,128)(2,1)S(1)}, bf16[64,1024]{1,0:T(8,128)(2,1)S(1)}, u32[]{:S(2)}, u32[]{:S(2)}) %collective-permute-start.2) | collective-permute-done | bytes 131104 | tf_op jit(solution)/shard_map/ppermute | solution.py:225
  10.0 2.6 %collective-permute-done.3.refs_3_ = bf16[64,1024]{1,0:T(8,128)(2,1)S(1)} collective-permute-done((bf16[64,1024]{1,0:T(8,128)(2,1)S(1)}, bf16[64,1024]{1,0:T(8,128)(2,1)S(1)}, u32[]{:S(2)}, u32[]{:S(2)}) %collective-permute-start.3) | collective-permute-done | bytes 131104 | tf_op jit(solution)/shard_map/ppermute | solution.py:225
  12.6 3.8 %collective-permute-done.refs_1_ = bf16[1,2,1,64,1024]{4,3,2,1,0:T(8,128)(2,1)S(1)} collective-permute-done((bf16[1,2,1,64,1024]{4,3,2,1,0:T(8,128)(2,1)S(1)}, bf16[1,2,1,64,1024]{4,3,2,1,0:T(8,128)(2,1)S(1)}, u32[]{:S(2)}, u32[]{:S(2)}) %collective-permute-start) | collective-permute-done | bytes 262176 | tf_op jit(solution)/shard_map/ppermute | solution.py:222
  16.3 0.1 route.1
  16.4 1.2 %collective-permute-start.4 = (bf16[64,1024]{1,0:T(8,128)(2,1)S(1)}, bf16[64,1024]{1,0:T(8,128)(2,1)S(1)}, u32[]{:S(2)}, u32[]{:S(2)}) collective-permute-start(bf16[64,1024]{1,0:T(8,128)(2,1)S(1)} %get-tuple-element.76), channel_id=1, source_target_pairs={{0,1},{1,0},{2,3},{3,2},{4,5},{5,4},{6,7},{7,6},{8,9},{9,8},{10,11... | collective-permute-start | bytes 393224 | tf_op jit(solution)/shard_map/ppermute | solution.py:222
  17.7 3.2 %collective-permute-start.7 = (bf16[64,1024]{1,0:T(8,128)(2,1)S(1)}, bf16[64,1024]{1,0:T(8,128)(2,1)S(1)}, u32[]{:S(2)}, u32[]{:S(2)}) collective-permute-start(bf16[64,1024]{1,0:T(8,128)(2,1)S(1)} %get-tuple-element.80), channel_id=1, source_target_pairs={{0,2},{1,3},{2,0},{3,1},{4,6},{5,7},{6,4},{7,5},{8,10},{9,11},{10,... | collective-permute-start | bytes 393224 | tf_op jit(solution)/shard_map/ppermute | solution.py:222
  20.8 0.0 collective-permute-start.8
  20.8 0.0 collective-permute-done.4
  20.9 1.3 %collective-permute-start.5 = (bf16[2,64,1024]{2,1,0:T(8,128)(2,1)S(1)}, bf16[2,64,1024]{2,1,0:T(8,128)(2,1)S(1)}, u32[]{:S(2)}, u32[]{:S(2)}) collective-permute-start(bf16[2,64,1024]{2,1,0:T(8,128)(2,1)S(1)} %pad_maximum_fusion.1), channel_id=1, source_target_pairs={{0,8},{4,12},{8,0},{12,4},{16,24},{20,28},{24,16},{28,20},{1,9},{5... | collective-permute-start | bytes 786440 | tf_op jit(solution)/shard_map/ppermute | solution.py:225
  22.2 1.3 %collective-permute-start.6 = (bf16[2,64,1024]{2,1,0:T(8,128)(2,1)S(1)}, bf16[2,64,1024]{2,1,0:T(8,128)(2,1)S(1)}, u32[]{:S(2)}, u32[]{:S(2)}) collective-permute-start(bf16[2,64,1024]{2,1,0:T(8,128)(2,1)S(1)} %pad_maximum_fusion.1), channel_id=1, source_target_pairs={{0,16},{4,20},{8,24},{12,28},{16,0},{20,4},{24,8},{28,12},{1,17},{... | collective-permute-start | bytes 786440 | tf_op jit(solution)/shard_map/ppermute | solution.py:225
  23.5 1.4 %collective-permute-start.9 = (bf16[2,1,64,1024]{3,2,1,0:T(8,128)(2,1)S(1)}, bf16[2,1,64,1024]{3,2,1,0:T(8,128)(2,1)S(1)}, u32[]{:S(2)}, u32[]{:S(2)}) collective-permute-start(bf16[2,1,64,1024]{3,2,1,0:T(8,128)(2,1)S(1)} %pad_maximum_fusion.2), channel_id=1, source_target_pairs={{0,1},{1,0},{2,3},{3,2},{4,5},{5,4},{6,7},{7,6},{8,9},{9,8},{10,11... | collective-permute-start | bytes 786440 | tf_op jit(solution)/shard_map/ppermute | solution.py:222
  24.9 0.0 collective-permute-done.7.refs_0_
  24.9 4.7 %collective-permute-done.8.refs_1_ = bf16[64,1024]{1,0:T(8,128)(2,1)S(1)} collective-permute-done((bf16[64,1024]{1,0:T(8,128)(2,1)S(1)}, bf16[64,1024]{1,0:T(8,128)(2,1)S(1)}, u32[]{:S(2)}, u32[]{:S(2)}) %collective-permute-start.8) | collective-permute-done | bytes 131104 | tf_op jit(solution)/shard_map/ppermute | solution.py:222
  29.6 0.0 collective-permute-done.5
  29.6 0.0 collective-permute-done.6
  29.7 3.1 %collective-permute-start.14 = (bf16[4,64,1024]{2,1,0:T(8,128)(2,1)S(1)}, bf16[4,64,1024]{2,1,0:T(8,128)(2,1)S(1)}, u32[]{:S(2)}, u32[]{:S(2)}) collective-permute-start(bf16[4,64,1024]{2,1,0:T(8,128)(2,1)S(1)} %constant_dynamic-update-slice_fusion.refs_1_), channel_id=1, source_target_pairs={{0,4},{4,0},{8,12},{12,8},{16,20},{20,16},{24,28},{28,24},{1,5},{5... | collective-permute-start | bytes 1572872 | tf_op jit(solution)/shard_map/ppermute | solution.py:228
  32.7 0.6 collective-permute-start.12
  33.3 1.2 %collective-permute-start.13 = (bf16[2,64,1024]{2,1,0:T(8,128)(2,1)S(1)}, bf16[2,64,1024]{2,1,0:T(8,128)(2,1)S(1)}, u32[]{:S(2)}, u32[]{:S(2)}) collective-permute-start(bf16[2,64,1024]{2,1,0:T(8,128)(2,1)S(1)} %collect.1), channel_id=1, source_target_pairs={{0,16},{4,20},{8,24},{12,28},{16,0},{20,4},{24,8},{28,12},{1,17},{... | collective-permute-start | bytes 786440 | tf_op jit(solution)/shard_map/ppermute | solution.py:225
  34.5 0.0 collective-permute-done.9.refs_2_
  34.6 2.2 %collective-permute-start.10 = (bf16[2,1,64,1024]{3,2,1,0:T(8,128)(2,1)S(1)}, bf16[2,1,64,1024]{3,2,1,0:T(8,128)(2,1)S(1)}, u32[]{:S(2)}, u32[]{:S(2)}) collective-permute-start(bf16[2,1,64,1024]{3,2,1,0:T(8,128)(2,1)S(1)} %pad_maximum_fusion.3), channel_id=1, source_target_pairs={{0,1},{1,0},{2,3},{3,2},{4,5},{5,4},{6,7},{7,6},{8,9},{9,8},{10,11... | collective-permute-start | bytes 786440 | tf_op jit(solution)/shard_map/ppermute | solution.py:222
  36.8 1.5 %collective-permute-start.11 = (bf16[1,2,1,64,1024]{4,3,2,1,0:T(8,128)(2,1)S(1)}, bf16[1,2,1,64,1024]{4,3,2,1,0:T(8,128)(2,1)S(1)}, u32[]{:S(2)}, u32[]{:S(2)}) collective-permute-start(bf16[1,2,1,64,1024]{4,3,2,1,0:T(8,128)(2,1)S(1)} %get-tuple-element.118.refs_0_), channel_id=1, source_target_pairs={{0,2},{1,3},{2,0},{3,1},{4,6},{5,7},{6,4},{7,5},{8,10},{9,11},{10,... | collective-permute-start | bytes 786440 | tf_op jit(solution)/shard_map/ppermute | solution.py:222
  38.3 0.2 turn.4.refs_0_.refs_2_
  38.6 0.0 collective-permute-done.14.refs_3_
  38.6 6.2 %product.6.refs_2_ = f32[2,4,1024,2048]{3,2,1,0:T(8,128)} custom-call(bf16[1024,256]{1,0:T(8,128)(2,1)S(1)} %turn.4.refs_0_.refs_2_, bf16[4,64,1024]{2,1,0:T(8,128)(2,1)S(1)} %constant_dynamic-update-slice_fusion.refs_1_, bf16[1024,256]{1,0:T(8,128)(2,1)S(1)} %turn.4.refs_0_.refs_2_, bf16[4,64,1024]{2,1,0:T(8,128)(2,1)S(1)} %collective-permute-done.14.refs_3_), custom_call_target="tpu_custom_call" | custom-call | flops 536870912 | bytes 4194304 | tf_op jit(solution)/shard_map/product/pallas_call | solution.py:192
  44.8 0.0 collective-permute-done.12
  44.8 0.0 collective-permute-done.13
  44.9 3.3 %collective-permute-done.10.refs_2_ = bf16[2,1,64,1024]{3,2,1,0:T(8,128)(2,1)S(1)} collective-permute-done((bf16[2,1,64,1024]{3,2,1,0:T(8,128)(2,1)S(1)}, bf16[2,1,64,1024]{3,2,1,0:T(8,128)(2,1)S(1)}, u32[]{:S(2)}, u32[]{:S(2)}) %collective-permute-start.10) | collective-permute-done | bytes 262176 | tf_op jit(solution)/shard_map/ppermute | solution.py:222
  48.2 0.0 collective-permute-done.11.refs_1_
  48.2 3.9 %collective-permute-start.16 = (bf16[4,64,1024]{2,1,0:T(8,128)(2,1)S(1)}, bf16[4,64,1024]{2,1,0:T(8,128)(2,1)S(1)}, u32[]{:S(2)}, u32[]{:S(2)}) collective-permute-start(bf16[4,64,1024]{2,1,0:T(8,128)(2,1)S(1)} %pad_maximum_fusion.refs_1_), channel_id=1, source_target_pairs={{0,4},{4,0},{8,12},{12,8},{16,20},{20,16},{24,28},{28,24},{1,5},{5... | collective-permute-start | bytes 1572872 | tf_op jit(solution)/shard_map/ppermute | solution.py:228
  52.1 0.0 collective-permute-start.17
  52.2 0.1 collective-permute-start.15
  52.3 0.4 collective-permute-start.19
  52.7 0.2 turn.5.refs_0_
  52.9 3.7 %product.7.refs_2_ = f32[2,4,1024,2048]{3,2,1,0:T(8,128)} custom-call(bf16[1024,256]{1,0:T(8,128)(2,1)S(1)} %turn.5.refs_0_, bf16[4,64,1024]{2,1,0:T(8,128)(2,1)S(1)} %pad_maximum_fusion.refs_1_, f32[2,4,1024,2048]{3,2,1,0:T(8,128)} %product.6.refs_2_), custom_call_target="tpu_custom_call", output_to_operand_aliasing={{}: (2, {})} | custom-call | flops 268435456 | bytes 2097152 | tf_op jit(solution)/shard_map/product/pallas_call | solution.py:192
  56.6 0.0 collective-permute-done.16.refs_1_
  56.6 0.0 collective-permute-done.17.refs_3_
  56.6 3.7 %product.8.refs_4_ = f32[2,4,1024,2048]{3,2,1,0:T(8,128)} custom-call(bf16[1024,256]{1,0:T(8,128)(2,1)S(1)} %turn.5.refs_0_, bf16[4,64,1024]{2,1,0:T(8,128)(2,1)S(1)} %collective-permute-done.16.refs_1_, f32[2,4,1024,2048]{3,2,1,0:T(8,128)} %product.7.refs_2_), custom_call_target="tpu_custom_call", output_to_operand_aliasing={{}: (2, {})} | custom-call | flops 268435456 | bytes 2097152 | tf_op jit(solution)/shard_map/product/pallas_call | solution.py:192
  60.3 0.0 collective-permute-done.15.refs_2_
  60.4 1.5 %collective-permute-start.18 = (bf16[2,1,64,1024]{3,2,1,0:T(8,128)(2,1)S(1)}, bf16[2,1,64,1024]{3,2,1,0:T(8,128)(2,1)S(1)}, u32[]{:S(2)}, u32[]{:S(2)}) collective-permute-start(bf16[2,1,64,1024]{3,2,1,0:T(8,128)(2,1)S(1)} %pad_maximum_fusion.5), channel_id=1, source_target_pairs={{0,1},{1,0},{2,3},{3,2},{4,5},{5,4},{6,7},{7,6},{8,9},{9,8},{10,11... | collective-permute-start | bytes 786440 | tf_op jit(solution)/shard_map/ppermute | solution.py:222
  61.9 0.2 turn.6.refs_0_.refs_2_
  62.1 6.2 %product.9.refs_2_ = f32[2,4,1024,2048]{3,2,1,0:T(8,128)} custom-call(bf16[1024,256]{1,0:T(8,128)(2,1)S(1)} %turn.6.refs_0_.refs_2_, bf16[4,64,1024]{2,1,0:T(8,128)(2,1)S(1)} %constant_dynamic-update-slice_fusion.2.refs_1_, bf16[1024,256]{1,0:T(8,128)(2,1)S(1)} %turn.6.refs_0_.refs_2_, ...), custom_call_target="tpu_custom_call", output_to_operand_aliasing={{}: (4, {})} | custom-call | flops 536870912 | bytes 4194304 | tf_op jit(solution)/shard_map/product/pallas_call | solution.py:192
  68.3 0.0 collective-permute-done.19.refs_1_
  68.3 0.0 collective-permute-done.18.refs_2_
  68.3 1.4 %collective-permute-start.20 = (bf16[4,64,1024]{2,1,0:T(8,128)(2,1)S(1)}, bf16[4,64,1024]{2,1,0:T(8,128)(2,1)S(1)}, u32[]{:S(2)}, u32[]{:S(2)}) collective-permute-start(bf16[4,64,1024]{2,1,0:T(8,128)(2,1)S(1)} %collective-permute-done.19.refs_1_), channel_id=1, source_target_pairs={{0,4},{4,0},{8,12},{12,8},{16,20},{20,16},{24,28},{28,24},{1,5},{5... | collective-permute-start | bytes 1572872 | tf_op jit(solution)/shard_map/ppermute | solution.py:228
  69.7 0.2 turn.7.refs_0_
  69.9 3.7 %product.10.refs_2_ = f32[2,4,1024,2048]{3,2,1,0:T(8,128)} custom-call(bf16[1024,256]{1,0:T(8,128)(2,1)S(1)} %turn.7.refs_0_, bf16[4,64,1024]{2,1,0:T(8,128)(2,1)S(1)} %collective-permute-done.19.refs_1_, f32[2,4,1024,2048]{3,2,1,0:T(8,128)} %product.9.refs_2_), custom_call_target="tpu_custom_call", output_to_operand_aliasing={{}: (2, {})} | custom-call | flops 268435456 | bytes 2097152 | tf_op jit(solution)/shard_map/product/pallas_call | solution.py:192
  73.6 0.0 collective-permute-done.20.refs_1_
  73.6 3.7 %product.11 = f32[2,4,1024,2048]{3,2,1,0:T(8,128)} custom-call(bf16[1024,256]{1,0:T(8,128)(2,1)S(1)} %turn.7.refs_0_, bf16[4,64,1024]{2,1,0:T(8,128)(2,1)S(1)} %collective-permute-done.20.refs_1_, f32[2,4,1024,2048]{3,2,1,0:T(8,128)} %product.10.refs_2_), custom_call_target="tpu_custom_call", output_to_operand_aliasing={{}: (2, {})} | custom-call | flops 268435456 | bytes 2097152 | tf_op jit(solution)/shard_map/product/pallas_call | solution.py:192
  (18 shorter events, 0.4 us)
Async XLA Ops:
  0.0 1.0 %copy-start = (bf16[2,4,32,1024]{3,2,1,0:T(8,128)(2,1)S(1)}, bf16[2,4,32,1024]{3,2,1,0:T(8,128)(2,1)}, u32[]{:S(2)}) copy-start(bf16[2,4,32,1024]{3,2,1,0:T(8,128)(2,1)} %raw.1) | copy-start | bytes 1572868
  1.5 14.9 %collective-permute-start = (bf16[1,2,1,64,1024]{4,3,2,1,0:T(8,128)(2,1)S(1)}, bf16[1,2,1,64,1024]{4,3,2,1,0:T(8,128)(2,1)S(1)}, u32[]{:S(2)}, u32[]{:S(2)}) collective-permute-start(bf16[1,2,1,64,1024]{4,3,2,1,0:T(8,128)(2,1)S(1)} %get-tuple-element.100.refs_0_), channel_id=1, source_target_pairs={{0,2},{1,3},{2,0},{3,1},{4,6},{5,7},{6,4},{7,5},{8,10},{9,11},{10,... | collective-permute-start | bytes 786440 | tf_op jit(solution)/shard_map/ppermute | solution.py:222
  4.7 4.1 %collective-permute-start.1 = (bf16[64,1024]{1,0:T(8,128)(2,1)S(1)}, bf16[64,1024]{1,0:T(8,128)(2,1)S(1)}, u32[]{:S(2)}, u32[]{:S(2)}) collective-permute-start(bf16[64,1024]{1,0:T(8,128)(2,1)S(1)} %get-tuple-element.68), channel_id=1, source_target_pairs={{0,8},{4,12},{8,0},{12,4},{16,24},{20,28},{24,16},{28,20},{1,9},{5... | collective-permute-start | bytes 393224 | tf_op jit(solution)/shard_map/ppermute | solution.py:225
  5.9 4.1 %collective-permute-start.2 = (bf16[64,1024]{1,0:T(8,128)(2,1)S(1)}, bf16[64,1024]{1,0:T(8,128)(2,1)S(1)}, u32[]{:S(2)}, u32[]{:S(2)}) collective-permute-start(bf16[64,1024]{1,0:T(8,128)(2,1)S(1)} %get-tuple-element.69), channel_id=1, source_target_pairs={{0,16},{4,20},{8,24},{12,28},{16,0},{20,4},{24,8},{28,12},{1,17},{... | collective-permute-start | bytes 393224 | tf_op jit(solution)/shard_map/ppermute | solution.py:225
  7.1 5.4 %collective-permute-start.3 = (bf16[64,1024]{1,0:T(8,128)(2,1)S(1)}, bf16[64,1024]{1,0:T(8,128)(2,1)S(1)}, u32[]{:S(2)}, u32[]{:S(2)}) collective-permute-start(bf16[64,1024]{1,0:T(8,128)(2,1)S(1)} %get-tuple-element.70), channel_id=1, source_target_pairs={{0,24},{4,28},{8,16},{12,20},{16,8},{20,12},{24,0},{28,4},{1,25},{... | collective-permute-start | bytes 393224 | tf_op jit(solution)/shard_map/ppermute | solution.py:225
  16.4 4.4 %collective-permute-start.4 = (bf16[64,1024]{1,0:T(8,128)(2,1)S(1)}, bf16[64,1024]{1,0:T(8,128)(2,1)S(1)}, u32[]{:S(2)}, u32[]{:S(2)}) collective-permute-start(bf16[64,1024]{1,0:T(8,128)(2,1)S(1)} %get-tuple-element.76), channel_id=1, source_target_pairs={{0,1},{1,0},{2,3},{3,2},{4,5},{5,4},{6,7},{7,6},{8,9},{9,8},{10,11... | collective-permute-start | bytes 393224 | tf_op jit(solution)/shard_map/ppermute | solution.py:222
  17.7 7.2 %collective-permute-start.7 = (bf16[64,1024]{1,0:T(8,128)(2,1)S(1)}, bf16[64,1024]{1,0:T(8,128)(2,1)S(1)}, u32[]{:S(2)}, u32[]{:S(2)}) collective-permute-start(bf16[64,1024]{1,0:T(8,128)(2,1)S(1)} %get-tuple-element.80), channel_id=1, source_target_pairs={{0,2},{1,3},{2,0},{3,1},{4,6},{5,7},{6,4},{7,5},{8,10},{9,11},{10,... | collective-permute-start | bytes 393224 | tf_op jit(solution)/shard_map/ppermute | solution.py:222
  20.8 8.7 %collective-permute-start.8 = (bf16[64,1024]{1,0:T(8,128)(2,1)S(1)}, bf16[64,1024]{1,0:T(8,128)(2,1)S(1)}, u32[]{:S(2)}, u32[]{:S(2)}) collective-permute-start(bf16[64,1024]{1,0:T(8,128)(2,1)S(1)} %get-tuple-element.81), channel_id=1, source_target_pairs={{0,3},{1,2},{2,1},{3,0},{4,7},{5,6},{6,5},{7,4},{8,11},{9,10},{10,... | collective-permute-start | bytes 393224 | tf_op jit(solution)/shard_map/ppermute | solution.py:222
  20.9 8.7 %collective-permute-start.5 = (bf16[2,64,1024]{2,1,0:T(8,128)(2,1)S(1)}, bf16[2,64,1024]{2,1,0:T(8,128)(2,1)S(1)}, u32[]{:S(2)}, u32[]{:S(2)}) collective-permute-start(bf16[2,64,1024]{2,1,0:T(8,128)(2,1)S(1)} %pad_maximum_fusion.1), channel_id=1, source_target_pairs={{0,8},{4,12},{8,0},{12,4},{16,24},{20,28},{24,16},{28,20},{1,9},{5... | collective-permute-start | bytes 786440 | tf_op jit(solution)/shard_map/ppermute | solution.py:225
  22.2 7.5 %collective-permute-start.6 = (bf16[2,64,1024]{2,1,0:T(8,128)(2,1)S(1)}, bf16[2,64,1024]{2,1,0:T(8,128)(2,1)S(1)}, u32[]{:S(2)}, u32[]{:S(2)}) collective-permute-start(bf16[2,64,1024]{2,1,0:T(8,128)(2,1)S(1)} %pad_maximum_fusion.1), channel_id=1, source_target_pairs={{0,16},{4,20},{8,24},{12,28},{16,0},{20,4},{24,8},{28,12},{1,17},{... | collective-permute-start | bytes 786440 | tf_op jit(solution)/shard_map/ppermute | solution.py:225
  23.5 11.1 %collective-permute-start.9 = (bf16[2,1,64,1024]{3,2,1,0:T(8,128)(2,1)S(1)}, bf16[2,1,64,1024]{3,2,1,0:T(8,128)(2,1)S(1)}, u32[]{:S(2)}, u32[]{:S(2)}) collective-permute-start(bf16[2,1,64,1024]{3,2,1,0:T(8,128)(2,1)S(1)} %pad_maximum_fusion.2), channel_id=1, source_target_pairs={{0,1},{1,0},{2,3},{3,2},{4,5},{5,4},{6,7},{7,6},{8,9},{9,8},{10,11... | collective-permute-start | bytes 786440 | tf_op jit(solution)/shard_map/ppermute | solution.py:222
  29.7 8.9 %collective-permute-start.14 = (bf16[4,64,1024]{2,1,0:T(8,128)(2,1)S(1)}, bf16[4,64,1024]{2,1,0:T(8,128)(2,1)S(1)}, u32[]{:S(2)}, u32[]{:S(2)}) collective-permute-start(bf16[4,64,1024]{2,1,0:T(8,128)(2,1)S(1)} %constant_dynamic-update-slice_fusion.refs_1_), channel_id=1, source_target_pairs={{0,4},{4,0},{8,12},{12,8},{16,20},{20,16},{24,28},{28,24},{1,5},{5... | collective-permute-start | bytes 1572872 | tf_op jit(solution)/shard_map/ppermute | solution.py:228
  32.7 12.1 %collective-permute-start.12 = (bf16[2,64,1024]{2,1,0:T(8,128)(2,1)S(1)}, bf16[2,64,1024]{2,1,0:T(8,128)(2,1)S(1)}, u32[]{:S(2)}, u32[]{:S(2)}) collective-permute-start(bf16[2,64,1024]{2,1,0:T(8,128)(2,1)S(1)} %collect.1), channel_id=1, source_target_pairs={{0,8},{4,12},{8,0},{12,4},{16,24},{20,28},{24,16},{28,20},{1,9},{5... | collective-permute-start | bytes 786440 | tf_op jit(solution)/shard_map/ppermute | solution.py:225
  33.3 11.5 %collective-permute-start.13 = (bf16[2,64,1024]{2,1,0:T(8,128)(2,1)S(1)}, bf16[2,64,1024]{2,1,0:T(8,128)(2,1)S(1)}, u32[]{:S(2)}, u32[]{:S(2)}) collective-permute-start(bf16[2,64,1024]{2,1,0:T(8,128)(2,1)S(1)} %collect.1), channel_id=1, source_target_pairs={{0,16},{4,20},{8,24},{12,28},{16,0},{20,4},{24,8},{28,12},{1,17},{... | collective-permute-start | bytes 786440 | tf_op jit(solution)/shard_map/ppermute | solution.py:225
  34.6 13.6 %collective-permute-start.10 = (bf16[2,1,64,1024]{3,2,1,0:T(8,128)(2,1)S(1)}, bf16[2,1,64,1024]{3,2,1,0:T(8,128)(2,1)S(1)}, u32[]{:S(2)}, u32[]{:S(2)}) collective-permute-start(bf16[2,1,64,1024]{3,2,1,0:T(8,128)(2,1)S(1)} %pad_maximum_fusion.3), channel_id=1, source_target_pairs={{0,1},{1,0},{2,3},{3,2},{4,5},{5,4},{6,7},{7,6},{8,9},{9,8},{10,11... | collective-permute-start | bytes 786440 | tf_op jit(solution)/shard_map/ppermute | solution.py:222
  36.8 11.4 %collective-permute-start.11 = (bf16[1,2,1,64,1024]{4,3,2,1,0:T(8,128)(2,1)S(1)}, bf16[1,2,1,64,1024]{4,3,2,1,0:T(8,128)(2,1)S(1)}, u32[]{:S(2)}, u32[]{:S(2)}) collective-permute-start(bf16[1,2,1,64,1024]{4,3,2,1,0:T(8,128)(2,1)S(1)} %get-tuple-element.118.refs_0_), channel_id=1, source_target_pairs={{0,2},{1,3},{2,0},{3,1},{4,6},{5,7},{6,4},{7,5},{8,10},{9,11},{10,... | collective-permute-start | bytes 786440 | tf_op jit(solution)/shard_map/ppermute | solution.py:222
  48.2 8.4 %collective-permute-start.16 = (bf16[4,64,1024]{2,1,0:T(8,128)(2,1)S(1)}, bf16[4,64,1024]{2,1,0:T(8,128)(2,1)S(1)}, u32[]{:S(2)}, u32[]{:S(2)}) collective-permute-start(bf16[4,64,1024]{2,1,0:T(8,128)(2,1)S(1)} %pad_maximum_fusion.refs_1_), channel_id=1, source_target_pairs={{0,4},{4,0},{8,12},{12,8},{16,20},{20,16},{24,28},{28,24},{1,5},{5... | collective-permute-start | bytes 1572872 | tf_op jit(solution)/shard_map/ppermute | solution.py:228
  52.1 4.5 %collective-permute-start.17 = (bf16[4,64,1024]{2,1,0:T(8,128)(2,1)S(1)}, bf16[4,64,1024]{2,1,0:T(8,128)(2,1)S(1)}, u32[]{:S(2)}, u32[]{:S(2)}) collective-permute-start(bf16[4,64,1024]{2,1,0:T(8,128)(2,1)S(1)} %constant_dynamic-update-slice_fusion.2.refs_1_), channel_id=1, source_target_pairs={{0,4},{4,0},{8,12},{12,8},{16,20},{20,16},{24,28},{28,24},{1,5},{5... | collective-permute-start | bytes 1572872 | tf_op jit(solution)/shard_map/ppermute | solution.py:228
  52.2 8.2 %collective-permute-start.15 = (bf16[2,1,64,1024]{3,2,1,0:T(8,128)(2,1)S(1)}, bf16[2,1,64,1024]{3,2,1,0:T(8,128)(2,1)S(1)}, u32[]{:S(2)}, u32[]{:S(2)}) collective-permute-start(bf16[2,1,64,1024]{3,2,1,0:T(8,128)(2,1)S(1)} %pad_maximum_fusion.4), channel_id=1, source_target_pairs={{0,1},{1,0},{2,3},{3,2},{4,5},{5,4},{6,7},{7,6},{8,9},{9,8},{10,11... | collective-permute-start | bytes 786440 | tf_op jit(solution)/shard_map/ppermute | solution.py:222
  52.3 16.0 %collective-permute-start.19 = (bf16[4,64,1024]{2,1,0:T(8,128)(2,1)S(1)}, bf16[4,64,1024]{2,1,0:T(8,128)(2,1)S(1)}, u32[]{:S(2)}, u32[]{:S(2)}) collective-permute-start(bf16[4,64,1024]{2,1,0:T(8,128)(2,1)S(1)} %constant_dynamic-update-slice_fusion.2.refs_1_), channel_id=1, source_target_pairs={{0,8},{4,12},{8,0},{12,4},{16,24},{20,28},{24,16},{28,20},{1,9},{5... | collective-permute-start | bytes 1572872 | tf_op jit(solution)/shard_map/ppermute | solution.py:225
  60.4 7.9 %collective-permute-start.18 = (bf16[2,1,64,1024]{3,2,1,0:T(8,128)(2,1)S(1)}, bf16[2,1,64,1024]{3,2,1,0:T(8,128)(2,1)S(1)}, u32[]{:S(2)}, u32[]{:S(2)}) collective-permute-start(bf16[2,1,64,1024]{3,2,1,0:T(8,128)(2,1)S(1)} %pad_maximum_fusion.5), channel_id=1, source_target_pairs={{0,1},{1,0},{2,3},{3,2},{4,5},{5,4},{6,7},{7,6},{8,9},{9,8},{10,11... | collective-permute-start | bytes 786440 | tf_op jit(solution)/shard_map/ppermute | solution.py:222
  68.3 5.3 %collective-permute-start.20 = (bf16[4,64,1024]{2,1,0:T(8,128)(2,1)S(1)}, bf16[4,64,1024]{2,1,0:T(8,128)(2,1)S(1)}, u32[]{:S(2)}, u32[]{:S(2)}) collective-permute-start(bf16[4,64,1024]{2,1,0:T(8,128)(2,1)S(1)} %collective-permute-done.19.refs_1_), channel_id=1, source_target_pairs={{0,4},{4,0},{8,12},{12,8},{16,20},{20,16},{24,28},{28,24},{1,5},{5... | collective-permute-start | bytes 1572872 | tf_op jit(solution)/shard_map/ppermute | solution.py:228

commit v6 on v5

--- a/solution.py
+++ b/solution.py
@@ -105,7 +105,7 @@
         for d in range(n):
             ref, place = where[d]
             own = s ^ (q % n_split)
-            picked.append(refs[ref][place, at, own] if ref < 2 else refs[ref][place, own])
+            picked.append(refs[ref][place, at, own] if len(refs[ref].shape) == 5 else refs[ref][place, own])
     out[...] = jnp.concatenate(picked, axis=0).T
 
 
@@ -227,26 +227,26 @@
     def from_core(values):
         return lax.ppermute(values, "row", [(r, r ^ 1) for r in range(2 * n)])
 
-    def gather_rows(own, first, at):
-        parts, bit = [own[:, at], first[:, at]], n // 4
+    def gather_rows(parts):
+        parts, bit = list(parts), n // 4
         while bit:
             parts.append(along_line(jnp.concatenate(parts), bit))
             bit //= 2
-        return [own, first, *parts[2:]]
+        return parts
 
     def wait(values, done):
         return lax.optimization_barrier((values, done))
 
     def gather_bin(f):
         at, i = place[f]
-        return gather_rows(rows[at], firsts[at], i)
+        return [rows[at], firsts[at], *gather_rows([rows[at][:, i], firsts[at][:, i]])[2:]]
 
     firsts = [along_line(rows[0], n // 2)]
     blocks = [from_chip(piece, d) if d else piece for d, piece in enumerate(pieces)]
     firsts, blocks = wait(firsts, blocks)
     arrived = [along_line(x, e) if e else x for e, x in enumerate(route(blocks))]
     firsts, arrived[1] = wait(firsts, arrived[1])
-    parts = [gather_bin(0)]
+    parts = [gather_rows([rows[0], firsts[0]])]
     halves = [jnp.stack(arrived[: n // 2]), collect(arrived[n // 2 :])]
     direct = [d for d in range(1, n) if d & (d - 1) == 0]
     early = [from_chip(halves[0], d) for d in direct]
@@ -257,8 +257,7 @@
         low = d & -d
         near[d] = jnp.concatenate([early[direct.index(d)], late[direct.index(d)]]) if d == low else from_chip(near[d ^ low], low)
     far = [from_core(x) for x in near[:n_split]]
-    (rows, firsts), parts = wait((rows, firsts), parts)
-    parts.append(gather_bin(1))
+    parts.append(parts[0])
     firsts += [along_line(x, n // 2) for x in rows[1:2]]
 
     call = functools.partial(product, n=n, n_split=n_split, n_bins=n_bins)

time: 77.5 us -> 76.7 us (0.990)
  starting transfers between devices: 30.1 us -> 27.5 us
  waiting for transfers between devices: 17 us -> 18.9 us
    ppermute x4, starting transfers between devices: 8.37 us -> 5.63 us  [from_core(): return lax.ppermute(values, 'row', [(r, r ^ 1) for r in range(2 * n)])]
    ppermute x9 -> x8, waiting for transfers between devices: 11.7 us -> 13.6 us  [along_line(): return lax.ppermute(values, 'col', [(z, z ^ bit) for z in range(n)])]
    ppermute x8, starting transfers between devices: 7.38 us -> 8.18 us  [from_chip(): lax.ppermute(values, 'row', [(2 * q + k, 2 * (q ^ d) + k) for q in range(...]
    ppermute x9 -> x8, starting transfers between devices: 14.4 us -> 13.7 us  [along_line(): return lax.ppermute(values, 'col', [(z, z ^ bit) for z in range(n)])]
  transfers between devices with their start and end apart: 21 -> 20, of which waited for: 6 -> 7; matrix products, arithmetic and copies ran while one was open for 0% -> 0% of each run, Pallas kernels for 31% -> 32%
where the time goes in v6:
time: 76.7 us; the launch traced here: 76.5 us
  Pallas kernels  28.6 us (37%)
  starting transfers between devices  27.5 us (36%)
  waiting for transfers between devices  18.9 us (25%)
  local copies, waits for them, and re-layouts  1.16 us (2%)
    pallas_call x6, Pallas kernels, product(): pl.pallas_call(functools.partial(product_kernel, items, n, n_split, width...  27.3 us
    ppermute x8, starting transfers between devices, along_line(): return lax.ppermute(values, 'col', [(z, z ^ bit) for z in range(n)])  13.7 us
    ppermute x8, waiting for transfers between devices, along_line(): return lax.ppermute(values, 'col', [(z, z ^ bit) for z in range(n)])  13.6 us
    ppermute x8, starting transfers between devices, from_chip(): lax.ppermute(values, 'row', [(2 * q + k, 2 * (q ^ d) + k) for q in range(...  8.18 us
    ppermute x4, starting transfers between devices, from_core(): return lax.ppermute(values, 'row', [(r, r ^ 1) for r in range(2 * n)])  5.63 us
    ppermute x8, waiting for transfers between devices, from_chip(): lax.ppermute(values, 'row', [(2 * q + k, 2 * (q ^ d) + k) for q in range(...  5.25 us
  transfers between devices with their start and end apart: 20, of which 7 were waited for; matrix products, arithmetic and copies ran while one was open for 0% of the time, Pallas kernels for 32%

profile of v6, /device:TPU:1, one launch (start us, length us, event | category | flops | bytes accessed | tf_op | source)
XLA Modules:
  0.0 76.5 jit_solution(10538798493555282529)
XLA Ops:
  0.0 0.0 copy-start
  0.0 1.0 %copy-done = bf16[2,4,32,1024]{3,2,1,0:T(8,128)(2,1)S(1)} copy-done((bf16[2,4,32,1024]{3,2,1,0:T(8,128)(2,1)S(1)}, bf16[2,4,32,1024]{3,2,1,0:T(8,128)(2,1)}, u32[]{:S(2)}) %copy-start) | copy-done | bytes 524312
  1.0 0.4 whiten.1
  1.5 3.2 %collective-permute-start = (bf16[1,2,1,64,1024]{4,3,2,1,0:T(8,128)(2,1)S(1)}, bf16[1,2,1,64,1024]{4,3,2,1,0:T(8,128)(2,1)S(1)}, u32[]{:S(2)}, u32[]{:S(2)}) collective-permute-start(bf16[1,2,1,64,1024]{4,3,2,1,0:T(8,128)(2,1)S(1)} %get-tuple-element.84.refs_0_), channel_id=1, source_target_pairs={{0,2},{1,3},{2,0},{3,1},{4,6},{5,7},{6,4},{7,5},{8,10},{9,11},{10,... | collective-permute-start | bytes 786440 | tf_op jit(solution)/shard_map/ppermute | solution.py:222
  4.7 1.2 %collective-permute-start.1 = (bf16[64,1024]{1,0:T(8,128)(2,1)S(1)}, bf16[64,1024]{1,0:T(8,128)(2,1)S(1)}, u32[]{:S(2)}, u32[]{:S(2)}) collective-permute-start(bf16[64,1024]{1,0:T(8,128)(2,1)S(1)} %get-tuple-element.59), channel_id=1, source_target_pairs={{0,8},{4,12},{8,0},{12,4},{16,24},{20,28},{24,16},{28,20},{1,9},{5... | collective-permute-start | bytes 393224 | tf_op jit(solution)/shard_map/ppermute | solution.py:225
  5.9 1.2 %collective-permute-start.2 = (bf16[64,1024]{1,0:T(8,128)(2,1)S(1)}, bf16[64,1024]{1,0:T(8,128)(2,1)S(1)}, u32[]{:S(2)}, u32[]{:S(2)}) collective-permute-start(bf16[64,1024]{1,0:T(8,128)(2,1)S(1)} %get-tuple-element.60), channel_id=1, source_target_pairs={{0,16},{4,20},{8,24},{12,28},{16,0},{20,4},{24,8},{28,12},{1,17},{... | collective-permute-start | bytes 393224 | tf_op jit(solution)/shard_map/ppermute | solution.py:225
  7.1 0.2 collective-permute-start.3
  7.3 1.5 %collective-permute-done.1.refs_1_ = bf16[64,1024]{1,0:T(8,128)(2,1)S(1)} collective-permute-done((bf16[64,1024]{1,0:T(8,128)(2,1)S(1)}, bf16[64,1024]{1,0:T(8,128)(2,1)S(1)}, u32[]{:S(2)}, u32[]{:S(2)}) %collective-permute-start.1) | collective-permute-done | bytes 131104 | tf_op jit(solution)/shard_map/ppermute | solution.py:225
  8.8 1.2 %collective-permute-done.2.refs_2_ = bf16[64,1024]{1,0:T(8,128)(2,1)S(1)} collective-permute-done((bf16[64,1024]{1,0:T(8,128)(2,1)S(1)}, bf16[64,1024]{1,0:T(8,128)(2,1)S(1)}, u32[]{:S(2)}, u32[]{:S(2)}) %collective-permute-start.2) | collective-permute-done | bytes 131104 | tf_op jit(solution)/shard_map/ppermute | solution.py:225
  10.0 2.6 %collective-permute-done.3.refs_3_ = bf16[64,1024]{1,0:T(8,128)(2,1)S(1)} collective-permute-done((bf16[64,1024]{1,0:T(8,128)(2,1)S(1)}, bf16[64,1024]{1,0:T(8,128)(2,1)S(1)}, u32[]{:S(2)}, u32[]{:S(2)}) %collective-permute-start.3) | collective-permute-done | bytes 131104 | tf_op jit(solution)/shard_map/ppermute | solution.py:225
  12.6 3.8 %collective-permute-done.refs_1_ = bf16[1,2,1,64,1024]{4,3,2,1,0:T(8,128)(2,1)S(1)} collective-permute-done((bf16[1,2,1,64,1024]{4,3,2,1,0:T(8,128)(2,1)S(1)}, bf16[1,2,1,64,1024]{4,3,2,1,0:T(8,128)(2,1)S(1)}, u32[]{:S(2)}, u32[]{:S(2)}) %collective-permute-start) | collective-permute-done | bytes 262176 | tf_op jit(solution)/shard_map/ppermute | solution.py:222
  16.3 0.1 route.1
  16.4 1.2 %collective-permute-start.4 = (bf16[64,1024]{1,0:T(8,128)(2,1)S(1)}, bf16[64,1024]{1,0:T(8,128)(2,1)S(1)}, u32[]{:S(2)}, u32[]{:S(2)}) collective-permute-start(bf16[64,1024]{1,0:T(8,128)(2,1)S(1)} %get-tuple-element.67), channel_id=1, source_target_pairs={{0,1},{1,0},{2,3},{3,2},{4,5},{5,4},{6,7},{7,6},{8,9},{9,8},{10,11... | collective-permute-start | bytes 393224 | tf_op jit(solution)/shard_map/ppermute | solution.py:222
  17.7 3.1 %collective-permute-start.8 = (bf16[64,1024]{1,0:T(8,128)(2,1)S(1)}, bf16[64,1024]{1,0:T(8,128)(2,1)S(1)}, u32[]{:S(2)}, u32[]{:S(2)}) collective-permute-start(bf16[64,1024]{1,0:T(8,128)(2,1)S(1)} %get-tuple-element.72), channel_id=1, source_target_pairs={{0,2},{1,3},{2,0},{3,1},{4,6},{5,7},{6,4},{7,5},{8,10},{9,11},{10,... | collective-permute-start | bytes 393224 | tf_op jit(solution)/shard_map/ppermute | solution.py:222
  20.8 0.0 collective-permute-start.9
  20.8 0.0 collective-permute-done.4
  20.8 1.3 %collective-permute-start.6 = (bf16[2,64,1024]{2,1,0:T(8,128)(2,1)S(1)}, bf16[2,64,1024]{2,1,0:T(8,128)(2,1)S(1)}, u32[]{:S(2)}, u32[]{:S(2)}) collective-permute-start(bf16[2,64,1024]{2,1,0:T(8,128)(2,1)S(1)} %pad_maximum_fusion.2), channel_id=1, source_target_pairs={{0,8},{4,12},{8,0},{12,4},{16,24},{20,28},{24,16},{28,20},{1,9},{5... | collective-permute-start | bytes 786440 | tf_op jit(solution)/shard_map/ppermute | solution.py:225
  22.1 1.3 %collective-permute-start.7 = (bf16[2,64,1024]{2,1,0:T(8,128)(2,1)S(1)}, bf16[2,64,1024]{2,1,0:T(8,128)(2,1)S(1)}, u32[]{:S(2)}, u32[]{:S(2)}) collective-permute-start(bf16[2,64,1024]{2,1,0:T(8,128)(2,1)S(1)} %pad_maximum_fusion.2), channel_id=1, source_target_pairs={{0,16},{4,20},{8,24},{12,28},{16,0},{20,4},{24,8},{28,12},{1,17},{... | collective-permute-start | bytes 786440 | tf_op jit(solution)/shard_map/ppermute | solution.py:225
  23.3 0.1 pad_maximum_fusion
  23.4 1.5 %collective-permute-start.5 = (bf16[2,2,1,64,1024]{4,3,2,1,0:T(8,128)(2,1)S(1)}, bf16[2,2,1,64,1024]{4,3,2,1,0:T(8,128)(2,1)S(1)}, u32[]{:S(2)}, u32[]{:S(2)}) collective-permute-start(bf16[2,2,1,64,1024]{4,3,2,1,0:T(8,128)(2,1)S(1)} %pad_maximum_fusion), channel_id=1, source_target_pairs={{0,1},{1,0},{2,3},{3,2},{4,5},{5,4},{6,7},{7,6},{8,9},{9,8},{10,11... | collective-permute-start | bytes 1572872 | tf_op jit(solution)/shard_map/ppermute | solution.py:222
  24.9 0.0 collective-permute-done.8.refs_0_
  24.9 4.7 %collective-permute-done.9.refs_1_ = bf16[64,1024]{1,0:T(8,128)(2,1)S(1)} collective-permute-done((bf16[64,1024]{1,0:T(8,128)(2,1)S(1)}, bf16[64,1024]{1,0:T(8,128)(2,1)S(1)}, u32[]{:S(2)}, u32[]{:S(2)}) %collective-permute-start.9) | collective-permute-done | bytes 131104 | tf_op jit(solution)/shard_map/ppermute | solution.py:222
  29.6 0.0 collective-permute-done.6
  29.6 0.0 collective-permute-done.7
  29.7 3.1 %collective-permute-start.13 = (bf16[4,64,1024]{2,1,0:T(8,128)(2,1)S(1)}, bf16[4,64,1024]{2,1,0:T(8,128)(2,1)S(1)}, u32[]{:S(2)}, u32[]{:S(2)}) collective-permute-start(bf16[4,64,1024]{2,1,0:T(8,128)(2,1)S(1)} %constant_dynamic-update-slice_fusion.refs_1_), channel_id=1, source_target_pairs={{0,4},{4,0},{8,12},{12,8},{16,20},{20,16},{24,28},{28,24},{1,5},{5... | collective-permute-start | bytes 1572872 | tf_op jit(solution)/shard_map/ppermute | solution.py:228
  32.8 0.5 collective-permute-start.11
  33.3 1.2 %collective-permute-start.12 = (bf16[2,64,1024]{2,1,0:T(8,128)(2,1)S(1)}, bf16[2,64,1024]{2,1,0:T(8,128)(2,1)S(1)}, u32[]{:S(2)}, u32[]{:S(2)}) collective-permute-start(bf16[2,64,1024]{2,1,0:T(8,128)(2,1)S(1)} %collect.1), channel_id=1, source_target_pairs={{0,16},{4,20},{8,24},{12,28},{16,0},{20,4},{24,8},{28,12},{1,17},{... | collective-permute-start | bytes 786440 | tf_op jit(solution)/shard_map/ppermute | solution.py:225
  34.5 3.1 %collective-permute-start.10 = (bf16[1,2,1,64,1024]{4,3,2,1,0:T(8,128)(2,1)S(1)}, bf16[1,2,1,64,1024]{4,3,2,1,0:T(8,128)(2,1)S(1)}, u32[]{:S(2)}, u32[]{:S(2)}) collective-permute-start(bf16[1,2,1,64,1024]{4,3,2,1,0:T(8,128)(2,1)S(1)} %get-tuple-element.102.refs_0_), channel_id=1, source_target_pairs={{0,2},{1,3},{2,0},{3,1},{4,6},{5,7},{6,4},{7,5},{8,10},{9,11},{10,... | collective-permute-start | bytes 786440 | tf_op jit(solution)/shard_map/ppermute | solution.py:222
  37.6 2.6 %collective-permute-done.5.refs_2_ = bf16[2,2,1,64,1024]{4,3,2,1,0:T(8,128)(2,1)S(1)} collective-permute-done((bf16[2,2,1,64,1024]{4,3,2,1,0:T(8,128)(2,1)S(1)}, bf16[2,2,1,64,1024]{4,3,2,1,0:T(8,128)(2,1)S(1)}, u32[]{:S(2)}, u32[]{:S(2)}) %collective-permute-start.5) | collective-permute-done | bytes 524320 | tf_op jit(solution)/shard_map/ppermute | solution.py:222
  40.2 0.2 turn.4.refs_0_.refs_2_
  40.4 0.0 collective-permute-done.13.refs_3_
  40.4 6.2 %product.6.refs_2_ = f32[2,4,1024,2048]{3,2,1,0:T(8,128)} custom-call(bf16[1024,256]{1,0:T(8,128)(2,1)S(1)} %turn.4.refs_0_.refs_2_, bf16[4,64,1024]{2,1,0:T(8,128)(2,1)S(1)} %constant_dynamic-update-slice_fusion.refs_1_, bf16[1024,256]{1,0:T(8,128)(2,1)S(1)} %turn.4.refs_0_.refs_2_, bf16[4,64,1024]{2,1,0:T(8,128)(2,1)S(1)} %collective-permute-done.13.refs_3_), custom_call_target="tpu_custom_call" | custom-call | flops 536870912 | bytes 4194304 | tf_op jit(solution)/shard_map/product/pallas_call | solution.py:192
  46.7 0.0 collective-permute-done.11
  46.7 0.0 collective-permute-done.12
  46.8 2.6 %collective-permute-done.10.refs_1_ = bf16[1,2,1,64,1024]{4,3,2,1,0:T(8,128)(2,1)S(1)} collective-permute-done((bf16[1,2,1,64,1024]{4,3,2,1,0:T(8,128)(2,1)S(1)}, bf16[1,2,1,64,1024]{4,3,2,1,0:T(8,128)(2,1)S(1)}, u32[]{:S(2)}, u32[]{:S(2)}) %collective-permute-start.10) | collective-permute-done | bytes 262176 | tf_op jit(solution)/shard_map/ppermute | solution.py:222
  49.4 1.2 %collective-permute-start.15 = (bf16[4,64,1024]{2,1,0:T(8,128)(2,1)S(1)}, bf16[4,64,1024]{2,1,0:T(8,128)(2,1)S(1)}, u32[]{:S(2)}, u32[]{:S(2)}) collective-permute-start(bf16[4,64,1024]{2,1,0:T(8,128)(2,1)S(1)} %pad_maximum_fusion.1.refs_1_), channel_id=1, source_target_pairs={{0,4},{4,0},{8,12},{12,8},{16,20},{20,16},{24,28},{28,24},{1,5},{5... | collective-permute-start | bytes 1572872 | tf_op jit(solution)/shard_map/ppermute | solution.py:228
  50.5 0.0 collective-permute-start.16
  50.6 0.1 collective-permute-start.14
  50.7 1.3 %collective-permute-start.18 = (bf16[4,64,1024]{2,1,0:T(8,128)(2,1)S(1)}, bf16[4,64,1024]{2,1,0:T(8,128)(2,1)S(1)}, u32[]{:S(2)}, u32[]{:S(2)}) collective-permute-start(bf16[4,64,1024]{2,1,0:T(8,128)(2,1)S(1)} %constant_dynamic-update-slice_fusion.2.refs_1_), channel_id=1, source_target_pairs={{0,8},{4,12},{8,0},{12,4},{16,24},{20,28},{24,16},{28,20},{1,9},{5... | collective-permute-start | bytes 1572872 | tf_op jit(solution)/shard_map/ppermute | solution.py:225
  52.0 0.2 turn.5.refs_0_
  52.2 3.7 %product.7.refs_2_ = f32[2,4,1024,2048]{3,2,1,0:T(8,128)} custom-call(bf16[1024,256]{1,0:T(8,128)(2,1)S(1)} %turn.5.refs_0_, bf16[4,64,1024]{2,1,0:T(8,128)(2,1)S(1)} %pad_maximum_fusion.1.refs_1_, f32[2,4,1024,2048]{3,2,1,0:T(8,128)} %product.6.refs_2_), custom_call_target="tpu_custom_call", output_to_operand_aliasing={{}: (2, {})} | custom-call | flops 268435456 | bytes 2097152 | tf_op jit(solution)/shard_map/product/pallas_call | solution.py:192
  55.9 0.0 collective-permute-done.15.refs_1_
  55.9 0.0 collective-permute-done.16.refs_3_
  55.9 3.7 %product.8.refs_4_ = f32[2,4,1024,2048]{3,2,1,0:T(8,128)} custom-call(bf16[1024,256]{1,0:T(8,128)(2,1)S(1)} %turn.5.refs_0_, bf16[4,64,1024]{2,1,0:T(8,128)(2,1)S(1)} %collective-permute-done.15.refs_1_, f32[2,4,1024,2048]{3,2,1,0:T(8,128)} %product.7.refs_2_), custom_call_target="tpu_custom_call", output_to_operand_aliasing={{}: (2, {})} | custom-call | flops 268435456 | bytes 2097152 | tf_op jit(solution)/shard_map/product/pallas_call | solution.py:192
  59.6 0.0 collective-permute-done.14.refs_2_
  59.7 1.5 %collective-permute-start.17 = (bf16[2,1,64,1024]{3,2,1,0:T(8,128)(2,1)S(1)}, bf16[2,1,64,1024]{3,2,1,0:T(8,128)(2,1)S(1)}, u32[]{:S(2)}, u32[]{:S(2)}) collective-permute-start(bf16[2,1,64,1024]{3,2,1,0:T(8,128)(2,1)S(1)} %pad_maximum_fusion.4), channel_id=1, source_target_pairs={{0,1},{1,0},{2,3},{3,2},{4,5},{5,4},{6,7},{7,6},{8,9},{9,8},{10,11... | collective-permute-start | bytes 786440 | tf_op jit(solution)/shard_map/ppermute | solution.py:222
  61.1 0.2 turn.6.refs_0_.refs_2_
  61.3 6.2 %product.9.refs_2_ = f32[2,4,1024,2048]{3,2,1,0:T(8,128)} custom-call(bf16[1024,256]{1,0:T(8,128)(2,1)S(1)} %turn.6.refs_0_.refs_2_, bf16[4,64,1024]{2,1,0:T(8,128)(2,1)S(1)} %constant_dynamic-update-slice_fusion.2.refs_1_, bf16[1024,256]{1,0:T(8,128)(2,1)S(1)} %turn.6.refs_0_.refs_2_, ...), custom_call_target="tpu_custom_call", output_to_operand_aliasing={{}: (4, {})} | custom-call | flops 536870912 | bytes 4194304 | tf_op jit(solution)/shard_map/product/pallas_call | solution.py:192
  67.6 0.0 collective-permute-done.18.refs_1_
  67.6 0.0 collective-permute-done.17.refs_2_
  67.6 1.3 %collective-permute-start.19 = (bf16[4,64,1024]{2,1,0:T(8,128)(2,1)S(1)}, bf16[4,64,1024]{2,1,0:T(8,128)(2,1)S(1)}, u32[]{:S(2)}, u32[]{:S(2)}) collective-permute-start(bf16[4,64,1024]{2,1,0:T(8,128)(2,1)S(1)} %collective-permute-done.18.refs_1_), channel_id=1, source_target_pairs={{0,4},{4,0},{8,12},{12,8},{16,20},{20,16},{24,28},{28,24},{1,5},{5... | collective-permute-start | bytes 1572872 | tf_op jit(solution)/shard_map/ppermute | solution.py:228
  68.9 0.2 turn.7.refs_0_
  69.1 3.7 %product.10.refs_2_ = f32[2,4,1024,2048]{3,2,1,0:T(8,128)} custom-call(bf16[1024,256]{1,0:T(8,128)(2,1)S(1)} %turn.7.refs_0_, bf16[4,64,1024]{2,1,0:T(8,128)(2,1)S(1)} %collective-permute-done.18.refs_1_, f32[2,4,1024,2048]{3,2,1,0:T(8,128)} %product.9.refs_2_), custom_call_target="tpu_custom_call", output_to_operand_aliasing={{}: (2, {})} | custom-call | flops 268435456 | bytes 2097152 | tf_op jit(solution)/shard_map/product/pallas_call | solution.py:192
  72.8 0.0 collective-permute-done.19.refs_1_
  72.8 3.7 %product.11 = f32[2,4,1024,2048]{3,2,1,0:T(8,128)} custom-call(bf16[1024,256]{1,0:T(8,128)(2,1)S(1)} %turn.7.refs_0_, bf16[4,64,1024]{2,1,0:T(8,128)(2,1)S(1)} %collective-permute-done.19.refs_1_, f32[2,4,1024,2048]{3,2,1,0:T(8,128)} %product.10.refs_2_), custom_call_target="tpu_custom_call", output_to_operand_aliasing={{}: (2, {})} | custom-call | flops 268435456 | bytes 2097152 | tf_op jit(solution)/shard_map/product/pallas_call | solution.py:192
  (12 shorter events, 0.3 us)
Async XLA Ops:
  0.0 1.0 %copy-start = (bf16[2,4,32,1024]{3,2,1,0:T(8,128)(2,1)S(1)}, bf16[2,4,32,1024]{3,2,1,0:T(8,128)(2,1)}, u32[]{:S(2)}) copy-start(bf16[2,4,32,1024]{3,2,1,0:T(8,128)(2,1)} %raw.1) | copy-start | bytes 1572868
  1.5 14.9 %collective-permute-start = (bf16[1,2,1,64,1024]{4,3,2,1,0:T(8,128)(2,1)S(1)}, bf16[1,2,1,64,1024]{4,3,2,1,0:T(8,128)(2,1)S(1)}, u32[]{:S(2)}, u32[]{:S(2)}) collective-permute-start(bf16[1,2,1,64,1024]{4,3,2,1,0:T(8,128)(2,1)S(1)} %get-tuple-element.84.refs_0_), channel_id=1, source_target_pairs={{0,2},{1,3},{2,0},{3,1},{4,6},{5,7},{6,4},{7,5},{8,10},{9,11},{10,... | collective-permute-start | bytes 786440 | tf_op jit(solution)/shard_map/ppermute | solution.py:222
  4.7 4.1 %collective-permute-start.1 = (bf16[64,1024]{1,0:T(8,128)(2,1)S(1)}, bf16[64,1024]{1,0:T(8,128)(2,1)S(1)}, u32[]{:S(2)}, u32[]{:S(2)}) collective-permute-start(bf16[64,1024]{1,0:T(8,128)(2,1)S(1)} %get-tuple-element.59), channel_id=1, source_target_pairs={{0,8},{4,12},{8,0},{12,4},{16,24},{20,28},{24,16},{28,20},{1,9},{5... | collective-permute-start | bytes 393224 | tf_op jit(solution)/shard_map/ppermute | solution.py:225
  5.9 4.1 %collective-permute-start.2 = (bf16[64,1024]{1,0:T(8,128)(2,1)S(1)}, bf16[64,1024]{1,0:T(8,128)(2,1)S(1)}, u32[]{:S(2)}, u32[]{:S(2)}) collective-permute-start(bf16[64,1024]{1,0:T(8,128)(2,1)S(1)} %get-tuple-element.60), channel_id=1, source_target_pairs={{0,16},{4,20},{8,24},{12,28},{16,0},{20,4},{24,8},{28,12},{1,17},{... | collective-permute-start | bytes 393224 | tf_op jit(solution)/shard_map/ppermute | solution.py:225
  7.1 5.4 %collective-permute-start.3 = (bf16[64,1024]{1,0:T(8,128)(2,1)S(1)}, bf16[64,1024]{1,0:T(8,128)(2,1)S(1)}, u32[]{:S(2)}, u32[]{:S(2)}) collective-permute-start(bf16[64,1024]{1,0:T(8,128)(2,1)S(1)} %get-tuple-element.61), channel_id=1, source_target_pairs={{0,24},{4,28},{8,16},{12,20},{16,8},{20,12},{24,0},{28,4},{1,25},{... | collective-permute-start | bytes 393224 | tf_op jit(solution)/shard_map/ppermute | solution.py:225
  16.4 4.3 %collective-permute-start.4 = (bf16[64,1024]{1,0:T(8,128)(2,1)S(1)}, bf16[64,1024]{1,0:T(8,128)(2,1)S(1)}, u32[]{:S(2)}, u32[]{:S(2)}) collective-permute-start(bf16[64,1024]{1,0:T(8,128)(2,1)S(1)} %get-tuple-element.67), channel_id=1, source_target_pairs={{0,1},{1,0},{2,3},{3,2},{4,5},{5,4},{6,7},{7,6},{8,9},{9,8},{10,11... | collective-permute-start | bytes 393224 | tf_op jit(solution)/shard_map/ppermute | solution.py:222
  17.7 7.2 %collective-permute-start.8 = (bf16[64,1024]{1,0:T(8,128)(2,1)S(1)}, bf16[64,1024]{1,0:T(8,128)(2,1)S(1)}, u32[]{:S(2)}, u32[]{:S(2)}) collective-permute-start(bf16[64,1024]{1,0:T(8,128)(2,1)S(1)} %get-tuple-element.72), channel_id=1, source_target_pairs={{0,2},{1,3},{2,0},{3,1},{4,6},{5,7},{6,4},{7,5},{8,10},{9,11},{10,... | collective-permute-start | bytes 393224 | tf_op jit(solution)/shard_map/ppermute | solution.py:222
  20.8 8.8 %collective-permute-start.9 = (bf16[64,1024]{1,0:T(8,128)(2,1)S(1)}, bf16[64,1024]{1,0:T(8,128)(2,1)S(1)}, u32[]{:S(2)}, u32[]{:S(2)}) collective-permute-start(bf16[64,1024]{1,0:T(8,128)(2,1)S(1)} %get-tuple-element.73), channel_id=1, source_target_pairs={{0,3},{1,2},{2,1},{3,0},{4,7},{5,6},{6,5},{7,4},{8,11},{9,10},{10,... | collective-permute-start | bytes 393224 | tf_op jit(solution)/shard_map/ppermute | solution.py:222
  20.8 8.8 %collective-permute-start.6 = (bf16[2,64,1024]{2,1,0:T(8,128)(2,1)S(1)}, bf16[2,64,1024]{2,1,0:T(8,128)(2,1)S(1)}, u32[]{:S(2)}, u32[]{:S(2)}) collective-permute-start(bf16[2,64,1024]{2,1,0:T(8,128)(2,1)S(1)} %pad_maximum_fusion.2), channel_id=1, source_target_pairs={{0,8},{4,12},{8,0},{12,4},{16,24},{20,28},{24,16},{28,20},{1,9},{5... | collective-permute-start | bytes 786440 | tf_op jit(solution)/shard_map/ppermute | solution.py:225
  22.1 7.5 %collective-permute-start.7 = (bf16[2,64,1024]{2,1,0:T(8,128)(2,1)S(1)}, bf16[2,64,1024]{2,1,0:T(8,128)(2,1)S(1)}, u32[]{:S(2)}, u32[]{:S(2)}) collective-permute-start(bf16[2,64,1024]{2,1,0:T(8,128)(2,1)S(1)} %pad_maximum_fusion.2), channel_id=1, source_target_pairs={{0,16},{4,20},{8,24},{12,28},{16,0},{20,4},{24,8},{28,12},{1,17},{... | collective-permute-start | bytes 786440 | tf_op jit(solution)/shard_map/ppermute | solution.py:225
  23.4 16.8 %collective-permute-start.5 = (bf16[2,2,1,64,1024]{4,3,2,1,0:T(8,128)(2,1)S(1)}, bf16[2,2,1,64,1024]{4,3,2,1,0:T(8,128)(2,1)S(1)}, u32[]{:S(2)}, u32[]{:S(2)}) collective-permute-start(bf16[2,2,1,64,1024]{4,3,2,1,0:T(8,128)(2,1)S(1)} %pad_maximum_fusion), channel_id=1, source_target_pairs={{0,1},{1,0},{2,3},{3,2},{4,5},{5,4},{6,7},{7,6},{8,9},{9,8},{10,11... | collective-permute-start | bytes 1572872 | tf_op jit(solution)/shard_map/ppermute | solution.py:222
  29.7 10.7 %collective-permute-start.13 = (bf16[4,64,1024]{2,1,0:T(8,128)(2,1)S(1)}, bf16[4,64,1024]{2,1,0:T(8,128)(2,1)S(1)}, u32[]{:S(2)}, u32[]{:S(2)}) collective-permute-start(bf16[4,64,1024]{2,1,0:T(8,128)(2,1)S(1)} %constant_dynamic-update-slice_fusion.refs_1_), channel_id=1, source_target_pairs={{0,4},{4,0},{8,12},{12,8},{16,20},{20,16},{24,28},{28,24},{1,5},{5... | collective-permute-start | bytes 1572872 | tf_op jit(solution)/shard_map/ppermute | solution.py:228
  32.8 13.9 %collective-permute-start.11 = (bf16[2,64,1024]{2,1,0:T(8,128)(2,1)S(1)}, bf16[2,64,1024]{2,1,0:T(8,128)(2,1)S(1)}, u32[]{:S(2)}, u32[]{:S(2)}) collective-permute-start(bf16[2,64,1024]{2,1,0:T(8,128)(2,1)S(1)} %collect.1), channel_id=1, source_target_pairs={{0,8},{4,12},{8,0},{12,4},{16,24},{20,28},{24,16},{28,20},{1,9},{5... | collective-permute-start | bytes 786440 | tf_op jit(solution)/shard_map/ppermute | solution.py:225
  33.3 13.4 %collective-permute-start.12 = (bf16[2,64,1024]{2,1,0:T(8,128)(2,1)S(1)}, bf16[2,64,1024]{2,1,0:T(8,128)(2,1)S(1)}, u32[]{:S(2)}, u32[]{:S(2)}) collective-permute-start(bf16[2,64,1024]{2,1,0:T(8,128)(2,1)S(1)} %collect.1), channel_id=1, source_target_pairs={{0,16},{4,20},{8,24},{12,28},{16,0},{20,4},{24,8},{28,12},{1,17},{... | collective-permute-start | bytes 786440 | tf_op jit(solution)/shard_map/ppermute | solution.py:225
  34.5 14.9 %collective-permute-start.10 = (bf16[1,2,1,64,1024]{4,3,2,1,0:T(8,128)(2,1)S(1)}, bf16[1,2,1,64,1024]{4,3,2,1,0:T(8,128)(2,1)S(1)}, u32[]{:S(2)}, u32[]{:S(2)}) collective-permute-start(bf16[1,2,1,64,1024]{4,3,2,1,0:T(8,128)(2,1)S(1)} %get-tuple-element.102.refs_0_), channel_id=1, source_target_pairs={{0,2},{1,3},{2,0},{3,1},{4,6},{5,7},{6,4},{7,5},{8,10},{9,11},{10,... | collective-permute-start | bytes 786440 | tf_op jit(solution)/shard_map/ppermute | solution.py:222
  49.4 6.5 %collective-permute-start.15 = (bf16[4,64,1024]{2,1,0:T(8,128)(2,1)S(1)}, bf16[4,64,1024]{2,1,0:T(8,128)(2,1)S(1)}, u32[]{:S(2)}, u32[]{:S(2)}) collective-permute-start(bf16[4,64,1024]{2,1,0:T(8,128)(2,1)S(1)} %pad_maximum_fusion.1.refs_1_), channel_id=1, source_target_pairs={{0,4},{4,0},{8,12},{12,8},{16,20},{20,16},{24,28},{28,24},{1,5},{5... | collective-permute-start | bytes 1572872 | tf_op jit(solution)/shard_map/ppermute | solution.py:228
  50.5 5.3 %collective-permute-start.16 = (bf16[4,64,1024]{2,1,0:T(8,128)(2,1)S(1)}, bf16[4,64,1024]{2,1,0:T(8,128)(2,1)S(1)}, u32[]{:S(2)}, u32[]{:S(2)}) collective-permute-start(bf16[4,64,1024]{2,1,0:T(8,128)(2,1)S(1)} %constant_dynamic-update-slice_fusion.2.refs_1_), channel_id=1, source_target_pairs={{0,4},{4,0},{8,12},{12,8},{16,20},{20,16},{24,28},{28,24},{1,5},{5... | collective-permute-start | bytes 1572872 | tf_op jit(solution)/shard_map/ppermute | solution.py:228
  50.6 9.0 %collective-permute-start.14 = (bf16[2,1,64,1024]{3,2,1,0:T(8,128)(2,1)S(1)}, bf16[2,1,64,1024]{3,2,1,0:T(8,128)(2,1)S(1)}, u32[]{:S(2)}, u32[]{:S(2)}) collective-permute-start(bf16[2,1,64,1024]{3,2,1,0:T(8,128)(2,1)S(1)} %pad_maximum_fusion.3), channel_id=1, source_target_pairs={{0,1},{1,0},{2,3},{3,2},{4,5},{5,4},{6,7},{7,6},{8,9},{9,8},{10,11... | collective-permute-start | bytes 786440 | tf_op jit(solution)/shard_map/ppermute | solution.py:222
  50.7 16.9 %collective-permute-start.18 = (bf16[4,64,1024]{2,1,0:T(8,128)(2,1)S(1)}, bf16[4,64,1024]{2,1,0:T(8,128)(2,1)S(1)}, u32[]{:S(2)}, u32[]{:S(2)}) collective-permute-start(bf16[4,64,1024]{2,1,0:T(8,128)(2,1)S(1)} %constant_dynamic-update-slice_fusion.2.refs_1_), channel_id=1, source_target_pairs={{0,8},{4,12},{8,0},{12,4},{16,24},{20,28},{24,16},{28,20},{1,9},{5... | collective-permute-start | bytes 1572872 | tf_op jit(solution)/shard_map/ppermute | solution.py:225
  59.7 7.9 %collective-permute-start.17 = (bf16[2,1,64,1024]{3,2,1,0:T(8,128)(2,1)S(1)}, bf16[2,1,64,1024]{3,2,1,0:T(8,128)(2,1)S(1)}, u32[]{:S(2)}, u32[]{:S(2)}) collective-permute-start(bf16[2,1,64,1024]{3,2,1,0:T(8,128)(2,1)S(1)} %pad_maximum_fusion.4), channel_id=1, source_target_pairs={{0,1},{1,0},{2,3},{3,2},{4,5},{5,4},{6,7},{7,6},{8,9},{9,8},{10,11... | collective-permute-start | bytes 786440 | tf_op jit(solution)/shard_map/ppermute | solution.py:222
  67.6 5.2 %collective-permute-start.19 = (bf16[4,64,1024]{2,1,0:T(8,128)(2,1)S(1)}, bf16[4,64,1024]{2,1,0:T(8,128)(2,1)S(1)}, u32[]{:S(2)}, u32[]{:S(2)}) collective-permute-start(bf16[4,64,1024]{2,1,0:T(8,128)(2,1)S(1)} %collective-permute-done.18.refs_1_), channel_id=1, source_target_pairs={{0,4},{4,0},{8,12},{12,8},{16,20},{20,16},{24,28},{28,24},{1,5},{5... | collective-permute-start | bytes 1572872 | tf_op jit(solution)/shard_map/ppermute | solution.py:228

commit v7 on v6

--- a/solution.py
+++ b/solution.py
@@ -247,15 +247,13 @@
     arrived = [along_line(x, e) if e else x for e, x in enumerate(route(blocks))]
     firsts, arrived[1] = wait(firsts, arrived[1])
     parts = [gather_rows([rows[0], firsts[0]])]
-    halves = [jnp.stack(arrived[: n // 2]), collect(arrived[n // 2 :])]
+    held = collect(arrived)
+    (rows, firsts), held = wait((rows, firsts), held)
+    near = [held] + [None] * (n - 1)
     direct = [d for d in range(1, n) if d & (d - 1) == 0]
-    early = [from_chip(halves[0], d) for d in direct]
-    (rows, firsts, early), halves = wait((rows, firsts, early), halves)
-    near = [jnp.concatenate(halves)] + [None] * (n - 1)
-    late = [from_chip(halves[1], d) for d in direct]
-    for d in range(1, n_split):
-        low = d & -d
-        near[d] = jnp.concatenate([early[direct.index(d)], late[direct.index(d)]]) if d == low else from_chip(near[d ^ low], low)
+    for d in range(1, n):
+        if d in direct or d < n_split:
+            near[d] = from_chip(near[d ^ (d & -d)], d & -d)
     far = [from_core(x) for x in near[:n_split]]
     parts.append(parts[0])
     firsts += [along_line(x, n // 2) for x in rows[1:2]]
@@ -264,10 +262,10 @@
     of_bin = lambda x, f: x[f * n_split : (f + 1) * n_split]
     turned = turn(0, parts[0], n)
     out = call([(0, False), (0, True)], [turned] * 2, [of_bin(near, 0), far], None)
-    late, out = wait(late, out)
+    near[n_split:], out = wait(near[n_split:], out)
     for d in range(n_split, n):
-        low = d & -d
-        near[d] = jnp.concatenate([early[direct.index(d)], late[direct.index(d)]]) if d == low else from_chip(near[d ^ low], low)
+        if near[d] is None:
+            near[d] = from_chip(near[d ^ (d & -d)], d & -d)
     for f in range(1, n_bins):
         needed = (parts[f], firsts, rows, of_bin(near, f), of_bin(near, f + 1) if f + 2 < n_bins else [])
         (parts[f], firsts, rows, mine, later), out = wait(needed, out)

time: 76.7 us -> 77.5 us (1.010)
  the two profiles are of different devices: /device:TPU:1 before, /device:TPU:21 now
where the time goes in v7:
time: 77.5 us; the launch traced here: 77.3 us
  Pallas kernels  28.6 us (37%)
  waiting for transfers between devices  25.5 us (33%)
  starting transfers between devices  21.9 us (28%)
  local copies, waits for them, and re-layouts  1.08 us (1%)
    pallas_call x6, Pallas kernels, product(): pl.pallas_call(functools.partial(product_kernel, items, n, n_split, width...  27.3 us
    ppermute x8, waiting for transfers between devices, along_line(): return lax.ppermute(values, 'col', [(z, z ^ bit) for z in range(n)])  21.2 us
    ppermute x8, starting transfers between devices, along_line(): return lax.ppermute(values, 'col', [(z, z ^ bit) for z in range(n)])  11.5 us
    ppermute x6, starting transfers between devices, from_chip(): lax.ppermute(values, 'row', [(2 * q + k, 2 * (q ^ d) + k) for q in range(...  6.3 us
    ppermute x6, waiting for transfers between devices, from_chip(): lax.ppermute(values, 'row', [(2 * q + k, 2 * (q ^ d) + k) for q in range(...  4.27 us
    ppermute x4, starting transfers between devices, from_core(): return lax.ppermute(values, 'row', [(r, r ^ 1) for r in range(2 * n)])  4.13 us
  transfers between devices with their start and end apart: 18, of which 8 were waited for; matrix products, arithmetic and copies ran while one was open for 0% of the time, Pallas kernels for 31%

profile of v7, /device:TPU:21, one launch (start us, length us, event | category | flops | bytes accessed | tf_op | source)
XLA Modules:
  0.0 77.3 jit_solution(9690440460856322592)
XLA Ops:
  0.0 0.0 copy-start
  0.0 1.0 %copy-done = bf16[2,4,32,1024]{3,2,1,0:T(8,128)(2,1)S(1)} copy-done((bf16[2,4,32,1024]{3,2,1,0:T(8,128)(2,1)S(1)}, bf16[2,4,32,1024]{3,2,1,0:T(8,128)(2,1)}, u32[]{:S(2)}) %copy-start) | copy-done | bytes 524312
  1.0 0.4 whiten.1
  1.5 0.1 collective-permute-start
  1.6 1.2 %collective-permute-start.1 = (bf16[64,1024]{1,0:T(8,128)(2,1)S(1)}, bf16[64,1024]{1,0:T(8,128)(2,1)S(1)}, u32[]{:S(2)}, u32[]{:S(2)}) collective-permute-start(bf16[64,1024]{1,0:T(8,128)(2,1)S(1)} %get-tuple-element.56), channel_id=1, source_target_pairs={{0,8},{4,12},{8,0},{12,4},{16,24},{20,28},{24,16},{28,20},{1,9},{5... | collective-permute-start | bytes 393224 | tf_op jit(solution)/shard_map/ppermute | solution.py:225
  2.8 0.2 collective-permute-start.2
  3.1 1.2 %collective-permute-start.3 = (bf16[64,1024]{1,0:T(8,128)(2,1)S(1)}, bf16[64,1024]{1,0:T(8,128)(2,1)S(1)}, u32[]{:S(2)}, u32[]{:S(2)}) collective-permute-start(bf16[64,1024]{1,0:T(8,128)(2,1)S(1)} %get-tuple-element.58), channel_id=1, source_target_pairs={{0,24},{4,28},{8,16},{12,20},{16,8},{20,12},{24,0},{28,4},{1,25},{... | collective-permute-start | bytes 393224 | tf_op jit(solution)/shard_map/ppermute | solution.py:225
  4.3 1.2 %collective-permute-done.1.refs_1_ = bf16[64,1024]{1,0:T(8,128)(2,1)S(1)} collective-permute-done((bf16[64,1024]{1,0:T(8,128)(2,1)S(1)}, bf16[64,1024]{1,0:T(8,128)(2,1)S(1)}, u32[]{:S(2)}, u32[]{:S(2)}) %collective-permute-start.1) | collective-permute-done | bytes 131104 | tf_op jit(solution)/shard_map/ppermute | solution.py:225
  5.4 1.7 %collective-permute-done.2.refs_2_ = bf16[64,1024]{1,0:T(8,128)(2,1)S(1)} collective-permute-done((bf16[64,1024]{1,0:T(8,128)(2,1)S(1)}, bf16[64,1024]{1,0:T(8,128)(2,1)S(1)}, u32[]{:S(2)}, u32[]{:S(2)}) %collective-permute-start.2) | collective-permute-done | bytes 131104 | tf_op jit(solution)/shard_map/ppermute | solution.py:225
  7.2 1.3 %collective-permute-done.3.refs_3_ = bf16[64,1024]{1,0:T(8,128)(2,1)S(1)} collective-permute-done((bf16[64,1024]{1,0:T(8,128)(2,1)S(1)}, bf16[64,1024]{1,0:T(8,128)(2,1)S(1)}, u32[]{:S(2)}, u32[]{:S(2)}) %collective-permute-start.3) | collective-permute-done | bytes 131104 | tf_op jit(solution)/shard_map/ppermute | solution.py:225
  8.5 3.7 %collective-permute-done.refs_1_ = bf16[1,2,1,64,1024]{4,3,2,1,0:T(8,128)(2,1)S(1)} collective-permute-done((bf16[1,2,1,64,1024]{4,3,2,1,0:T(8,128)(2,1)S(1)}, bf16[1,2,1,64,1024]{4,3,2,1,0:T(8,128)(2,1)S(1)}, u32[]{:S(2)}, u32[]{:S(2)}) %collective-permute-start) | collective-permute-done | bytes 262176 | tf_op jit(solution)/shard_map/ppermute | solution.py:222
  12.2 0.1 route.1
  12.3 5.3 %collective-permute-start.4 = (bf16[64,1024]{1,0:T(8,128)(2,1)S(1)}, bf16[64,1024]{1,0:T(8,128)(2,1)S(1)}, u32[]{:S(2)}, u32[]{:S(2)}) collective-permute-start(bf16[64,1024]{1,0:T(8,128)(2,1)S(1)} %get-tuple-element.64), channel_id=1, source_target_pairs={{0,1},{1,0},{2,3},{3,2},{4,5},{5,4},{6,7},{7,6},{8,9},{9,8},{10,11... | collective-permute-start | bytes 393224 | tf_op jit(solution)/shard_map/ppermute | solution.py:222
  17.6 0.0 collective-permute-start.6
  17.6 1.3 %collective-permute-start.7 = (bf16[64,1024]{1,0:T(8,128)(2,1)S(1)}, bf16[64,1024]{1,0:T(8,128)(2,1)S(1)}, u32[]{:S(2)}, u32[]{:S(2)}) collective-permute-start(bf16[64,1024]{1,0:T(8,128)(2,1)S(1)} %get-tuple-element.70), channel_id=1, source_target_pairs={{0,3},{1,2},{2,1},{3,0},{4,7},{5,6},{6,5},{7,4},{8,11},{9,10},{10,... | collective-permute-start | bytes 393224 | tf_op jit(solution)/shard_map/ppermute | solution.py:222
  18.9 2.2 %collective-permute-done.4.refs_1_ = bf16[64,1024]{1,0:T(8,128)(2,1)S(1)} collective-permute-done((bf16[64,1024]{1,0:T(8,128)(2,1)S(1)}, bf16[64,1024]{1,0:T(8,128)(2,1)S(1)}, u32[]{:S(2)}, u32[]{:S(2)}) %collective-permute-start.4) | collective-permute-done | bytes 131104 | tf_op jit(solution)/shard_map/ppermute | solution.py:222
  21.1 0.1 pad_maximum_fusion
  21.1 2.4 %collective-permute-start.5 = (bf16[2,2,1,64,1024]{4,3,2,1,0:T(8,128)(2,1)S(1)}, bf16[2,2,1,64,1024]{4,3,2,1,0:T(8,128)(2,1)S(1)}, u32[]{:S(2)}, u32[]{:S(2)}) collective-permute-start(bf16[2,2,1,64,1024]{4,3,2,1,0:T(8,128)(2,1)S(1)} %pad_maximum_fusion), channel_id=1, source_target_pairs={{0,1},{1,0},{2,3},{3,2},{4,5},{5,4},{6,7},{7,6},{8,9},{9,8},{10,11... | collective-permute-start | bytes 1572872 | tf_op jit(solution)/shard_map/ppermute | solution.py:222
  23.5 0.0 collective-permute-done.6.refs_2_
  23.5 7.0 %collective-permute-done.7.refs_3_ = bf16[64,1024]{1,0:T(8,128)(2,1)S(1)} collective-permute-done((bf16[64,1024]{1,0:T(8,128)(2,1)S(1)}, bf16[64,1024]{1,0:T(8,128)(2,1)S(1)}, u32[]{:S(2)}, u32[]{:S(2)}) %collective-permute-start.7) | collective-permute-done | bytes 131104 | tf_op jit(solution)/shard_map/ppermute | solution.py:222
  30.6 1.4 %collective-permute-start.11 = (bf16[4,64,1024]{2,1,0:T(8,128)(2,1)S(1)}, bf16[4,64,1024]{2,1,0:T(8,128)(2,1)S(1)}, u32[]{:S(2)}, u32[]{:S(2)}) collective-permute-start(bf16[4,64,1024]{2,1,0:T(8,128)(2,1)S(1)} %collect.1.refs_1_), channel_id=1, source_target_pairs={{0,4},{4,0},{8,12},{12,8},{16,20},{20,16},{24,28},{28,24},{1,5},{5... | collective-permute-start | bytes 1572872 | tf_op jit(solution)/shard_map/ppermute | solution.py:228
  32.0 0.2 collective-permute-start.10
  32.2 1.2 %collective-permute-start.9 = (bf16[4,64,1024]{2,1,0:T(8,128)(2,1)S(1)}, bf16[4,64,1024]{2,1,0:T(8,128)(2,1)S(1)}, u32[]{:S(2)}, u32[]{:S(2)}) collective-permute-start(bf16[4,64,1024]{2,1,0:T(8,128)(2,1)S(1)} %collect.1.refs_1_), channel_id=1, source_target_pairs={{0,8},{4,12},{8,0},{12,4},{16,24},{20,28},{24,16},{28,20},{1,9},{5... | collective-permute-start | bytes 1572872 | tf_op jit(solution)/shard_map/ppermute | solution.py:225
  33.4 0.0 collective-permute-start.8
  33.4 8.0 %collective-permute-done.5.refs_2_ = bf16[2,2,1,64,1024]{4,3,2,1,0:T(8,128)(2,1)S(1)} collective-permute-done((bf16[2,2,1,64,1024]{4,3,2,1,0:T(8,128)(2,1)S(1)}, bf16[2,2,1,64,1024]{4,3,2,1,0:T(8,128)(2,1)S(1)}, u32[]{:S(2)}, u32[]{:S(2)}) %collective-permute-start.5) | collective-permute-done | bytes 524320 | tf_op jit(solution)/shard_map/ppermute | solution.py:222
  41.4 0.2 turn.4.refs_0_.refs_2_
  41.6 0.0 collective-permute-done.11.refs_3_
  41.6 6.2 %product.6.refs_2_ = f32[2,4,1024,2048]{3,2,1,0:T(8,128)} custom-call(bf16[1024,256]{1,0:T(8,128)(2,1)S(1)} %turn.4.refs_0_.refs_2_, bf16[4,64,1024]{2,1,0:T(8,128)(2,1)S(1)} %collect.1.refs_1_, bf16[1024,256]{1,0:T(8,128)(2,1)S(1)} %turn.4.refs_0_.refs_2_, bf16[4,64,1024]{2,1,0:T(8,128)(2,1)S(1)} %collective-permute-done.11.refs_3_), custom_call_target="tpu_custom_call" | custom-call | flops 536870912 | bytes 4194304 | tf_op jit(solution)/shard_map/product/pallas_call | solution.py:192
  47.8 0.0 collective-permute-done.10.refs_1_
  47.9 0.0 collective-permute-done.9.refs_1_
  47.9 0.0 collective-permute-done.8.refs_1_
  47.9 0.7 collective-permute-start.13
  48.6 0.1 collective-permute-start.14
  48.8 2.3 %collective-permute-start.12 = (bf16[2,1,64,1024]{3,2,1,0:T(8,128)(2,1)S(1)}, bf16[2,1,64,1024]{3,2,1,0:T(8,128)(2,1)S(1)}, u32[]{:S(2)}, u32[]{:S(2)}) collective-permute-start(bf16[2,1,64,1024]{3,2,1,0:T(8,128)(2,1)S(1)} %pad_maximum_fusion.1), channel_id=1, source_target_pairs={{0,1},{1,0},{2,3},{3,2},{4,5},{5,4},{6,7},{7,6},{8,9},{9,8},{10,11... | collective-permute-start | bytes 786440 | tf_op jit(solution)/shard_map/ppermute | solution.py:222
  51.0 2.2 %collective-permute-start.16 = (bf16[4,64,1024]{2,1,0:T(8,128)(2,1)S(1)}, bf16[4,64,1024]{2,1,0:T(8,128)(2,1)S(1)}, u32[]{:S(2)}, u32[]{:S(2)}) collective-permute-start(bf16[4,64,1024]{2,1,0:T(8,128)(2,1)S(1)} %collective-permute-done.10.refs_1_), channel_id=1, source_target_pairs={{0,8},{4,12},{8,0},{12,4},{16,24},{20,28},{24,16},{28,20},{1,9},{5... | collective-permute-start | bytes 1572872 | tf_op jit(solution)/shard_map/ppermute | solution.py:225
  53.2 0.2 turn.5.refs_0_
  53.4 3.7 %product.7.refs_2_ = f32[2,4,1024,2048]{3,2,1,0:T(8,128)} custom-call(bf16[1024,256]{1,0:T(8,128)(2,1)S(1)} %turn.5.refs_0_, bf16[4,64,1024]{2,1,0:T(8,128)(2,1)S(1)} %collective-permute-done.9.refs_1_, f32[2,4,1024,2048]{3,2,1,0:T(8,128)} %product.6.refs_2_), custom_call_target="tpu_custom_call", output_to_operand_aliasing={{}: (2, {})} | custom-call | flops 268435456 | bytes 2097152 | tf_op jit(solution)/shard_map/product/pallas_call | solution.py:192
  57.1 0.0 collective-permute-done.13.refs_1_
  57.1 0.0 collective-permute-done.14.refs_3_
  57.1 3.7 %product.8.refs_4_ = f32[2,4,1024,2048]{3,2,1,0:T(8,128)} custom-call(bf16[1024,256]{1,0:T(8,128)(2,1)S(1)} %turn.5.refs_0_, bf16[4,64,1024]{2,1,0:T(8,128)(2,1)S(1)} %collective-permute-done.13.refs_1_, f32[2,4,1024,2048]{3,2,1,0:T(8,128)} %product.7.refs_2_), custom_call_target="tpu_custom_call", output_to_operand_aliasing={{}: (2, {})} | custom-call | flops 268435456 | bytes 2097152 | tf_op jit(solution)/shard_map/product/pallas_call | solution.py:192
  60.8 0.0 collective-permute-done.12.refs_2_
  60.9 0.1 collective-permute-start.15
  61.1 0.2 turn.6.refs_0_.refs_2_
  61.3 6.2 %product.9.refs_2_ = f32[2,4,1024,2048]{3,2,1,0:T(8,128)} custom-call(bf16[1024,256]{1,0:T(8,128)(2,1)S(1)} %turn.6.refs_0_.refs_2_, bf16[4,64,1024]{2,1,0:T(8,128)(2,1)S(1)} %collective-permute-done.10.refs_1_, bf16[1024,256]{1,0:T(8,128)(2,1)S(1)} %turn.6.refs_0_.refs_2_, ...), custom_call_target="tpu_custom_call", output_to_operand_aliasing={{}: (4, {})} | custom-call | flops 536870912 | bytes 4194304 | tf_op jit(solution)/shard_map/product/pallas_call | solution.py:192
  67.5 0.0 collective-permute-done.16.refs_1_
  67.5 0.3 collective-permute-done.15.refs_2_
  67.8 1.9 %collective-permute-start.17 = (bf16[4,64,1024]{2,1,0:T(8,128)(2,1)S(1)}, bf16[4,64,1024]{2,1,0:T(8,128)(2,1)S(1)}, u32[]{:S(2)}, u32[]{:S(2)}) collective-permute-start(bf16[4,64,1024]{2,1,0:T(8,128)(2,1)S(1)} %collective-permute-done.16.refs_1_), channel_id=1, source_target_pairs={{0,4},{4,0},{8,12},{12,8},{16,20},{20,16},{24,28},{28,24},{1,5},{5... | collective-permute-start | bytes 1572872 | tf_op jit(solution)/shard_map/ppermute | solution.py:228
  69.7 0.2 turn.7.refs_0_
  69.9 3.7 %product.10.refs_2_ = f32[2,4,1024,2048]{3,2,1,0:T(8,128)} custom-call(bf16[1024,256]{1,0:T(8,128)(2,1)S(1)} %turn.7.refs_0_, bf16[4,64,1024]{2,1,0:T(8,128)(2,1)S(1)} %collective-permute-done.16.refs_1_, f32[2,4,1024,2048]{3,2,1,0:T(8,128)} %product.9.refs_2_), custom_call_target="tpu_custom_call", output_to_operand_aliasing={{}: (2, {})} | custom-call | flops 268435456 | bytes 2097152 | tf_op jit(solution)/shard_map/product/pallas_call | solution.py:192
  73.6 0.0 collective-permute-done.17.refs_1_
  73.6 3.7 %product.11 = f32[2,4,1024,2048]{3,2,1,0:T(8,128)} custom-call(bf16[1024,256]{1,0:T(8,128)(2,1)S(1)} %turn.7.refs_0_, bf16[4,64,1024]{2,1,0:T(8,128)(2,1)S(1)} %collective-permute-done.17.refs_1_, f32[2,4,1024,2048]{3,2,1,0:T(8,128)} %product.10.refs_2_), custom_call_target="tpu_custom_call", output_to_operand_aliasing={{}: (2, {})} | custom-call | flops 268435456 | bytes 2097152 | tf_op jit(solution)/shard_map/product/pallas_call | solution.py:192
  (6 shorter events, 0.1 us)
Async XLA Ops:
  0.0 1.0 %copy-start = (bf16[2,4,32,1024]{3,2,1,0:T(8,128)(2,1)S(1)}, bf16[2,4,32,1024]{3,2,1,0:T(8,128)(2,1)}, u32[]{:S(2)}) copy-start(bf16[2,4,32,1024]{3,2,1,0:T(8,128)(2,1)} %raw.1) | copy-start | bytes 1572868
  1.5 10.7 %collective-permute-start = (bf16[1,2,1,64,1024]{4,3,2,1,0:T(8,128)(2,1)S(1)}, bf16[1,2,1,64,1024]{4,3,2,1,0:T(8,128)(2,1)S(1)}, u32[]{:S(2)}, u32[]{:S(2)}) collective-permute-start(bf16[1,2,1,64,1024]{4,3,2,1,0:T(8,128)(2,1)S(1)} %get-tuple-element.78.refs_0_), channel_id=1, source_target_pairs={{0,2},{1,3},{2,0},{3,1},{4,6},{5,7},{6,4},{7,5},{8,10},{9,11},{10,... | collective-permute-start | bytes 786440 | tf_op jit(solution)/shard_map/ppermute | solution.py:222
  1.6 3.8 %collective-permute-start.1 = (bf16[64,1024]{1,0:T(8,128)(2,1)S(1)}, bf16[64,1024]{1,0:T(8,128)(2,1)S(1)}, u32[]{:S(2)}, u32[]{:S(2)}) collective-permute-start(bf16[64,1024]{1,0:T(8,128)(2,1)S(1)} %get-tuple-element.56), channel_id=1, source_target_pairs={{0,8},{4,12},{8,0},{12,4},{16,24},{20,28},{24,16},{28,20},{1,9},{5... | collective-permute-start | bytes 393224 | tf_op jit(solution)/shard_map/ppermute | solution.py:225
  2.8 4.4 %collective-permute-start.2 = (bf16[64,1024]{1,0:T(8,128)(2,1)S(1)}, bf16[64,1024]{1,0:T(8,128)(2,1)S(1)}, u32[]{:S(2)}, u32[]{:S(2)}) collective-permute-start(bf16[64,1024]{1,0:T(8,128)(2,1)S(1)} %get-tuple-element.57), channel_id=1, source_target_pairs={{0,16},{4,20},{8,24},{12,28},{16,0},{20,4},{24,8},{28,12},{1,17},{... | collective-permute-start | bytes 393224 | tf_op jit(solution)/shard_map/ppermute | solution.py:225
  3.1 5.5 %collective-permute-start.3 = (bf16[64,1024]{1,0:T(8,128)(2,1)S(1)}, bf16[64,1024]{1,0:T(8,128)(2,1)S(1)}, u32[]{:S(2)}, u32[]{:S(2)}) collective-permute-start(bf16[64,1024]{1,0:T(8,128)(2,1)S(1)} %get-tuple-element.58), channel_id=1, source_target_pairs={{0,24},{4,28},{8,16},{12,20},{16,8},{20,12},{24,0},{28,4},{1,25},{... | collective-permute-start | bytes 393224 | tf_op jit(solution)/shard_map/ppermute | solution.py:225
  12.3 8.8 %collective-permute-start.4 = (bf16[64,1024]{1,0:T(8,128)(2,1)S(1)}, bf16[64,1024]{1,0:T(8,128)(2,1)S(1)}, u32[]{:S(2)}, u32[]{:S(2)}) collective-permute-start(bf16[64,1024]{1,0:T(8,128)(2,1)S(1)} %get-tuple-element.64), channel_id=1, source_target_pairs={{0,1},{1,0},{2,3},{3,2},{4,5},{5,4},{6,7},{7,6},{8,9},{9,8},{10,11... | collective-permute-start | bytes 393224 | tf_op jit(solution)/shard_map/ppermute | solution.py:222
  17.6 5.9 %collective-permute-start.6 = (bf16[64,1024]{1,0:T(8,128)(2,1)S(1)}, bf16[64,1024]{1,0:T(8,128)(2,1)S(1)}, u32[]{:S(2)}, u32[]{:S(2)}) collective-permute-start(bf16[64,1024]{1,0:T(8,128)(2,1)S(1)} %get-tuple-element.69), channel_id=1, source_target_pairs={{0,2},{1,3},{2,0},{3,1},{4,6},{5,7},{6,4},{7,5},{8,10},{9,11},{10,... | collective-permute-start | bytes 393224 | tf_op jit(solution)/shard_map/ppermute | solution.py:222
  17.6 12.9 %collective-permute-start.7 = (bf16[64,1024]{1,0:T(8,128)(2,1)S(1)}, bf16[64,1024]{1,0:T(8,128)(2,1)S(1)}, u32[]{:S(2)}, u32[]{:S(2)}) collective-permute-start(bf16[64,1024]{1,0:T(8,128)(2,1)S(1)} %get-tuple-element.70), channel_id=1, source_target_pairs={{0,3},{1,2},{2,1},{3,0},{4,7},{5,6},{6,5},{7,4},{8,11},{9,10},{10,... | collective-permute-start | bytes 393224 | tf_op jit(solution)/shard_map/ppermute | solution.py:222
  21.1 20.3 %collective-permute-start.5 = (bf16[2,2,1,64,1024]{4,3,2,1,0:T(8,128)(2,1)S(1)}, bf16[2,2,1,64,1024]{4,3,2,1,0:T(8,128)(2,1)S(1)}, u32[]{:S(2)}, u32[]{:S(2)}) collective-permute-start(bf16[2,2,1,64,1024]{4,3,2,1,0:T(8,128)(2,1)S(1)} %pad_maximum_fusion), channel_id=1, source_target_pairs={{0,1},{1,0},{2,3},{3,2},{4,5},{5,4},{6,7},{7,6},{8,9},{9,8},{10,11... | collective-permute-start | bytes 1572872 | tf_op jit(solution)/shard_map/ppermute | solution.py:222
  30.6 11.0 %collective-permute-start.11 = (bf16[4,64,1024]{2,1,0:T(8,128)(2,1)S(1)}, bf16[4,64,1024]{2,1,0:T(8,128)(2,1)S(1)}, u32[]{:S(2)}, u32[]{:S(2)}) collective-permute-start(bf16[4,64,1024]{2,1,0:T(8,128)(2,1)S(1)} %collect.1.refs_1_), channel_id=1, source_target_pairs={{0,4},{4,0},{8,12},{12,8},{16,20},{20,16},{24,28},{28,24},{1,5},{5... | collective-permute-start | bytes 1572872 | tf_op jit(solution)/shard_map/ppermute | solution.py:228
  32.0 15.9 %collective-permute-start.10 = (bf16[4,64,1024]{2,1,0:T(8,128)(2,1)S(1)}, bf16[4,64,1024]{2,1,0:T(8,128)(2,1)S(1)}, u32[]{:S(2)}, u32[]{:S(2)}) collective-permute-start(bf16[4,64,1024]{2,1,0:T(8,128)(2,1)S(1)} %collect.1.refs_1_), channel_id=1, source_target_pairs={{0,16},{4,20},{8,24},{12,28},{16,0},{20,4},{24,8},{28,12},{1,17},{... | collective-permute-start | bytes 1572872 | tf_op jit(solution)/shard_map/ppermute | solution.py:225
  32.2 15.7 %collective-permute-start.9 = (bf16[4,64,1024]{2,1,0:T(8,128)(2,1)S(1)}, bf16[4,64,1024]{2,1,0:T(8,128)(2,1)S(1)}, u32[]{:S(2)}, u32[]{:S(2)}) collective-permute-start(bf16[4,64,1024]{2,1,0:T(8,128)(2,1)S(1)} %collect.1.refs_1_), channel_id=1, source_target_pairs={{0,8},{4,12},{8,0},{12,4},{16,24},{20,28},{24,16},{28,20},{1,9},{5... | collective-permute-start | bytes 1572872 | tf_op jit(solution)/shard_map/ppermute | solution.py:225
  33.4 14.5 %collective-permute-start.8 = (bf16[1,2,1,64,1024]{4,3,2,1,0:T(8,128)(2,1)S(1)}, bf16[1,2,1,64,1024]{4,3,2,1,0:T(8,128)(2,1)S(1)}, u32[]{:S(2)}, u32[]{:S(2)}) collective-permute-start(bf16[1,2,1,64,1024]{4,3,2,1,0:T(8,128)(2,1)S(1)} %get-tuple-element.96.refs_0_), channel_id=1, source_target_pairs={{0,2},{1,3},{2,0},{3,1},{4,6},{5,7},{6,4},{7,5},{8,10},{9,11},{10,... | collective-permute-start | bytes 786440 | tf_op jit(solution)/shard_map/ppermute | solution.py:222
  47.9 9.2 %collective-permute-start.13 = (bf16[4,64,1024]{2,1,0:T(8,128)(2,1)S(1)}, bf16[4,64,1024]{2,1,0:T(8,128)(2,1)S(1)}, u32[]{:S(2)}, u32[]{:S(2)}) collective-permute-start(bf16[4,64,1024]{2,1,0:T(8,128)(2,1)S(1)} %collective-permute-done.9.refs_1_), channel_id=1, source_target_pairs={{0,4},{4,0},{8,12},{12,8},{16,20},{20,16},{24,28},{28,24},{1,5},{5... | collective-permute-start | bytes 1572872 | tf_op jit(solution)/shard_map/ppermute | solution.py:228
  48.6 8.5 %collective-permute-start.14 = (bf16[4,64,1024]{2,1,0:T(8,128)(2,1)S(1)}, bf16[4,64,1024]{2,1,0:T(8,128)(2,1)S(1)}, u32[]{:S(2)}, u32[]{:S(2)}) collective-permute-start(bf16[4,64,1024]{2,1,0:T(8,128)(2,1)S(1)} %collective-permute-done.10.refs_1_), channel_id=1, source_target_pairs={{0,4},{4,0},{8,12},{12,8},{16,20},{20,16},{24,28},{28,24},{1,5},{5... | collective-permute-start | bytes 1572872 | tf_op jit(solution)/shard_map/ppermute | solution.py:228
  48.8 12.1 %collective-permute-start.12 = (bf16[2,1,64,1024]{3,2,1,0:T(8,128)(2,1)S(1)}, bf16[2,1,64,1024]{3,2,1,0:T(8,128)(2,1)S(1)}, u32[]{:S(2)}, u32[]{:S(2)}) collective-permute-start(bf16[2,1,64,1024]{3,2,1,0:T(8,128)(2,1)S(1)} %pad_maximum_fusion.1), channel_id=1, source_target_pairs={{0,1},{1,0},{2,3},{3,2},{4,5},{5,4},{6,7},{7,6},{8,9},{9,8},{10,11... | collective-permute-start | bytes 786440 | tf_op jit(solution)/shard_map/ppermute | solution.py:222
  51.0 16.5 %collective-permute-start.16 = (bf16[4,64,1024]{2,1,0:T(8,128)(2,1)S(1)}, bf16[4,64,1024]{2,1,0:T(8,128)(2,1)S(1)}, u32[]{:S(2)}, u32[]{:S(2)}) collective-permute-start(bf16[4,64,1024]{2,1,0:T(8,128)(2,1)S(1)} %collective-permute-done.10.refs_1_), channel_id=1, source_target_pairs={{0,8},{4,12},{8,0},{12,4},{16,24},{20,28},{24,16},{28,20},{1,9},{5... | collective-permute-start | bytes 1572872 | tf_op jit(solution)/shard_map/ppermute | solution.py:225
  60.9 6.9 %collective-permute-start.15 = (bf16[2,1,64,1024]{3,2,1,0:T(8,128)(2,1)S(1)}, bf16[2,1,64,1024]{3,2,1,0:T(8,128)(2,1)S(1)}, u32[]{:S(2)}, u32[]{:S(2)}) collective-permute-start(bf16[2,1,64,1024]{3,2,1,0:T(8,128)(2,1)S(1)} %pad_maximum_fusion.2), channel_id=1, source_target_pairs={{0,1},{1,0},{2,3},{3,2},{4,5},{5,4},{6,7},{7,6},{8,9},{9,8},{10,11... | collective-permute-start | bytes 786440 | tf_op jit(solution)/shard_map/ppermute | solution.py:222
  67.8 5.8 %collective-permute-start.17 = (bf16[4,64,1024]{2,1,0:T(8,128)(2,1)S(1)}, bf16[4,64,1024]{2,1,0:T(8,128)(2,1)S(1)}, u32[]{:S(2)}, u32[]{:S(2)}) collective-permute-start(bf16[4,64,1024]{2,1,0:T(8,128)(2,1)S(1)} %collective-permute-done.16.refs_1_), channel_id=1, source_target_pairs={{0,4},{4,0},{8,12},{12,8},{16,20},{20,16},{24,28},{28,24},{1,5},{5... | collective-permute-start | bytes 1572872 | tf_op jit(solution)/shard_map/ppermute | solution.py:228
